TPU v7x, 256 devices: a whole 4x4x8 slice. The times are simulated.
256 devices in a mesh: row: 8 (over z), col: 32 (over y, x, core).
Axes of the slice: x: 4, y: 4, z: 8, core: 2. Of those that a mesh axis runs over, the one named last changes fastest.
Arguments:
- source_latent: bfloat16 [64, 65536], P(None, ('row', 'col')), may hold values from -27 to 27
- target_latent: bfloat16 [64, 65536], P(None, 'col'), may hold values from -6 to 6
- log_source_mass: float32 [65536], P('row'), may hold values from -2 to 2
- log_target_mass: bfloat16 [65536], P('col'), may hold values from -2 to 2
- target_coords: bfloat16 [2, 65536], P(None, 'col'), may hold values from -2 to 2
- support: int32 [512, 32], P('row'), may hold values from 0 to 511, as said below
Outputs:
- source_potential: float32 [65536], P(('row', 'col'))
- target_potential: float32 [65536], P('col')
- projection: float32 [2, 65536], P(None, ('row', 'col'))
Inputs may be any that keep to these rules, and one draw needn't show every extreme that they name: `support`: each source block lists 32 distinct target blocks. Of the 64 source blocks of one row shard, at most 192 listed entries fall into the 16 target blocks of one col shard, and exactly 192 for some col shard. Every target block is listed by some source block.
All inputs are finite; a program needn't handle non-finite values.
Results may differ from a plain program's by a relative error of at most 0.0003.
Values may be sent and summed in bfloat16 or wider, within the bound.
No kernel may reach another device: no remote copies, remote signals or barrier semaphores. Data moves between devices by JAX's collectives and lax.ppermute only.
A program may use at most 320 MiB of HBM per device.

v0:
```python
import jax
import jax.numpy as jnp
from jax import lax
from jax.experimental import pallas as pl
from jax.experimental.pallas import tpu as pltpu
from jax.sharding import PartitionSpec as P

LAT = 64
BLK = 128
ITERS = 2
NEG = -1e30
LN2 = 0.6931471805599453
KAPPA = 0.3125 / LN2
UNROLL = 32
PACK = 80


def chip_groups(cols):
    return [[c for c in range(cols) if c % 2 == core] for core in range(2)]


def stack_groups(rows, cols):
    return [
        [r * cols + 2 * chip + core for r in range(rows) for core in range(2)]
        for chip in range(cols // 2)
    ]


def exchange(x, axis, groups):
    return lax.all_to_all(x, axis, 0, 0, axis_index_groups=groups)


def join(parts):
    top = jnp.max(parts, axis=0)
    return top + jnp.log2(jnp.sum(jnp.exp2(parts - top[None]), axis=0))


def bias_of(mass, level):
    return 3.2 * (mass - LN2 * level)


def pieces(a):
    hi = a.astype(jnp.bfloat16)
    rest = a - hi.astype(jnp.float32)
    mid = rest.astype(jnp.bfloat16)
    low = (rest - mid.astype(jnp.float32)).astype(jnp.bfloat16)
    return hi, mid, low


def one_rows():
    row = lax.broadcasted_iota(jnp.int32, (BLK - LAT, BLK), 0)
    return jnp.where(row < 3, 1.0, 0.0).astype(jnp.bfloat16)


def side_rows(bias):
    hi, mid, low = (p.astype(jnp.float32) for p in pieces(bias))
    row = lax.broadcasted_iota(jnp.int32, (BLK - LAT, BLK), 0)
    full = jnp.where(row == 0, hi, jnp.where(row == 1, mid, jnp.where(row == 2, low, 0.0)))
    return full.astype(jnp.bfloat16)


def columns(jb):
    return pl.ds(pl.multiple_of(jb * BLK, BLK), BLK)


def dot(lhs, rhs):
    return jnp.dot(lhs, rhs, preferred_element_type=jnp.float32)


def sweep(count_ref, list_ref, body):
    def turn(g, c):
        body([list_ref[g * UNROLL + u] for u in range(UNROLL)])
        return c

    lax.fori_loop(0, (count_ref[0] + (UNROLL - 1)) // UNROLL, turn, 0)


def source_of(e):
    return e >> 6


def target_of(e):
    return e & 63


def fold_into(index, m, s, m_ref, s_ref):
    old = m_ref[index]
    new = jnp.maximum(old, m)
    s_ref[index] = s_ref[index] * jnp.exp2((old - new) * KAPPA) + s * jnp.exp2((m - new) * KAPPA)
    m_ref[index] = new


def finish(m, s):
    top = jnp.max(m, axis=1)
    total = jnp.sum(s * jnp.exp2((m - top[:, None, :]) * KAPPA), axis=1)
    return jnp.where(total > 0.0, top * KAPPA + jnp.log2(total), NEG)


def partial_stats(acc):
    split = acc.reshape(BLK // 8, 8, BLK)
    m = jnp.max(split, axis=0)
    return m, jnp.sum(jnp.exp2((split - m[None]) * KAPPA), axis=0)


def clear(m_ref, s_ref):
    m_ref[...] = jnp.full_like(m_ref, NEG)
    s_ref[...] = jnp.zeros_like(s_ref)


def fill_targets(pack_ref, b, yt_ref):
    for jb in range(yt_ref.shape[0]):
        block = pack_ref[:LAT, jb * BLK : (jb + 1) * BLK]
        yt_ref[jb] = jnp.concatenate([block, side_rows(b[jb : jb + 1, :])], axis=0).T


def target_by_source(entries, x_ref, yt_ref):
    ones = one_rows()
    last = x_ref.shape[0] - 1
    return [
        dot(
            yt_ref[target_of(e) & 31],
            jnp.concatenate([x_ref[jnp.minimum(source_of(e), last)], ones], axis=0),
        )
        for e in entries
    ]


def row_sweep(count_ref, list_ref, x_ref, pack_ref, b, out_ref, yt_ref, m_ref, s_ref):
    fill_targets(pack_ref, b, yt_ref)
    clear(m_ref, s_ref)

    def body(entries):
        stats = [partial_stats(acc) for acc in target_by_source(entries, x_ref, yt_ref)]
        for e, (m, s) in zip(entries, stats):
            fold_into(source_of(e), m, s, m_ref, s_ref)

    sweep(count_ref, list_ref, body)
    n = x_ref.shape[0]
    out_ref[...] = jnp.broadcast_to(finish(m_ref[:n], s_ref[:n])[None], out_ref.shape)


def first_row_kernel(count_ref, list_ref, x_ref, pack_ref, b_ref, out_ref, yt_ref, m_ref, s_ref):
    row_sweep(count_ref, list_ref, x_ref, pack_ref, b_ref[...], out_ref, yt_ref, m_ref, s_ref)


def row_kernel(
    count_ref, list_ref, x_ref, pack_ref, c_ref, mass_ref, out_ref, yt_ref, m_ref, s_ref
):
    b = bias_of(mass_ref[...], join(c_ref[...]))
    row_sweep(count_ref, list_ref, x_ref, pack_ref, b, out_ref, yt_ref, m_ref, s_ref)


def col_kernel(
    count_ref, list_ref, x_ref, pack_ref, r_ref, mass_ref, out_ref, xt_ref, m_ref, s_ref
):
    n = x_ref.shape[0]
    a = bias_of(mass_ref[...], join(r_ref[...]))
    for ib in range(n):
        xt_ref[ib] = jnp.concatenate([x_ref[ib], side_rows(a[ib : ib + 1, :])], axis=0).T
    clear(m_ref, s_ref)

    def body(entries):
        ones = one_rows()
        accs = [
            dot(
                xt_ref[jnp.minimum(source_of(e), n - 1)],
                jnp.concatenate([pack_ref[:LAT, columns(target_of(e) & 31)], ones], axis=0),
            )
            for e in entries
        ]
        stats = [partial_stats(acc) for acc in accs]
        for e, (m, s) in zip(entries, stats):
            fold_into(target_of(e), m, s, m_ref, s_ref)

    sweep(count_ref, list_ref, body)
    k = m_ref.shape[0] - 1
    out_ref[...] = jnp.broadcast_to(finish(m_ref[:k], s_ref[:k])[None], out_ref.shape)


def project_kernel(
    count_ref, list_ref, x_ref, pack_ref, c_ref, mass_ref, out_ref, yt_ref, m_ref, w_ref
):
    b = bias_of(mass_ref[...], join(c_ref[...]))
    fill_targets(pack_ref, b, yt_ref)
    clear(m_ref, w_ref)

    def body(entries):
        stats = []
        for e, acc in zip(entries, target_by_source(entries, x_ref, yt_ref)):
            m = jnp.max(acc, axis=0, keepdims=True)
            p = jnp.exp2((acc - m) * KAPPA)
            hi = p.astype(jnp.bfloat16)
            low = (p - hi.astype(jnp.float32)).astype(jnp.bfloat16)
            side = pack_ref[LAT:, columns(target_of(e) & 31)]
            stats.append((m, (dot(side, hi) + dot(side, low))[:8]))
        for e, (m, w) in zip(entries, stats):
            fold_into(source_of(e), m, w, m_ref, w_ref)

    sweep(count_ref, list_ref, body)
    out_ref[...] = jnp.zeros_like(out_ref)
    for ib in range(x_ref.shape[0]):
        w = w_ref[ib]
        total = w[2:3]
        live = total > 0.0
        safe = jnp.where(live, total, 1.0)
        half = ib % 2
        out_ref[ib // 2, half : half + 1, :] = jnp.where(
            live, m_ref[ib] * KAPPA + jnp.log2(safe), NEG
        )
        out_ref[ib // 2, 2 + half : 3 + half, :] = w[0:1] / safe
        out_ref[ib // 2, 4 + half : 5 + half, :] = w[1:2] / safe


SMEM = pl.BlockSpec(memory_space=pltpu.SMEM)
VMEM = pl.BlockSpec(memory_space=pltpu.VMEM)


def call(kernel, shape, scratch, count, tiles, *args):
    return pl.pallas_call(
        kernel,
        out_shape=jax.ShapeDtypeStruct(shape, jnp.float32),
        in_specs=[SMEM] * 2 + [VMEM] * len(args),
        out_specs=VMEM,
        scratch_shapes=scratch,
        compiler_params=pltpu.CompilerParams(vmem_limit_bytes=32 << 20),
    )(count, tiles, *args)


def tile_list(support, chip, per_chip, slots):
    rows, per_list = support.shape
    owned = support // per_chip == chip
    flags = owned.astype(jnp.float32)
    upto = (jnp.arange(per_list)[:, None] <= jnp.arange(per_list)[None, :]).astype(jnp.float32)
    before = (jnp.arange(rows)[None, :] < jnp.arange(rows)[:, None]).astype(jnp.float32)
    within = flags @ upto
    start = before @ within[:, -1:]
    place = jnp.where(owned, (within + start).astype(jnp.int32) - 1, -1)
    count = jnp.sum(owned.astype(jnp.int32)).reshape(1)
    code = jnp.arange(rows, dtype=jnp.int32)[:, None] * 64 + support % per_chip
    slot = jnp.arange(slots, dtype=jnp.int32)
    listed = jnp.sum(
        jnp.where(place[:, :, None] == slot, code[:, :, None], 0), axis=(0, 1), dtype=jnp.int32
    )
    return count, jnp.where(slot < count, listed, rows * 64 + per_chip)


def on_device(
    source_latent, target_latent, log_source_mass, log_target_mass, target_coords, support
):
    rows, cols = lax.axis_size("row"), lax.axis_size("col")
    here = lax.axis_index("col")
    chip, core = here // 2, here % 2
    chips = cols // 2
    mine = support.shape[0] // cols
    own_k = target_latent.shape[1] // BLK
    n, k = chips * mine, 2 * own_k
    bf16, f32 = jnp.bfloat16, jnp.float32
    by_chip, by_stack = chip_groups(cols), stack_groups(rows, cols)

    def of_core(a):
        split = a.reshape((chips, 2, mine) + a.shape[1:])
        split = jnp.where(core == 0, split[:, 0], split[:, 1])
        return split.reshape((n,) + a.shape[1:])

    own = source_latent.reshape(LAT, mine, BLK).transpose(1, 0, 2)
    spread = jnp.broadcast_to(own[None], (chips,) + own.shape)
    x = exchange(spread, "col", by_chip).reshape(n, LAT, BLK)

    width = target_latent.shape[1]
    pack = jnp.concatenate(
        [
            target_latent,
            target_coords,
            jnp.ones((1, width), bf16),
            log_target_mass[None],
            jnp.zeros((PACK - LAT - 4, width), bf16),
        ],
        axis=0,
    )
    other = lax.ppermute(pack, "col", [(i, i ^ 1) for i in range(cols)])
    pack = jnp.concatenate(
        [jnp.where(core == 0, pack, other), jnp.where(core == 0, other, pack)], axis=1
    )
    y_half = 0.5 * jnp.sum(jnp.square(pack[:LAT].astype(f32)), axis=0).reshape(k, BLK)
    target_log = pack[LAT + 3].astype(f32).reshape(k, BLK)
    source_log = of_core(log_source_mass.reshape(-1, BLK))
    count, tiles = tile_list(of_core(support), chip, k, 12 * mine * chips)

    stats = [pltpu.VMEM((n + 1, 8, BLK), f32)] * 2
    row_scratch = [pltpu.VMEM((k, BLK, BLK), bf16)] + stats
    col_scratch = [pltpu.VMEM((n, BLK, BLK), bf16)] + [pltpu.VMEM((k + 1, 8, BLK), f32)] * 2
    project_scratch = [
        pltpu.VMEM((k, BLK, BLK), bf16),
        pltpu.VMEM((n + 1, 1, BLK), f32),
        pltpu.VMEM((n + 1, 8, BLK), f32),
    ]
    for sweep_index in range(ITERS):
        to_chips = (chips, n, BLK)
        if sweep_index == 0:
            r = call(first_row_kernel, to_chips, row_scratch, count, tiles, x, pack, -y_half)
        else:
            r = call(row_kernel, to_chips, row_scratch, count, tiles, x, pack, c, target_log)
        r = exchange(r, "col", by_chip)
        c = call(
            col_kernel, (2 * rows, k, BLK), col_scratch, count, tiles, x, pack, r, source_log
        )
        c = exchange(c, ("row", "col"), by_stack)
    part = call(
        project_kernel, (chips, 8, BLK), project_scratch, count, tiles, x, pack, c, target_log
    )
    part = exchange(part, "col", by_chip)
    level = part[:, :mine]
    weight = jnp.exp2(level - jnp.max(level, axis=0))
    bottom = jnp.sum(weight, axis=0)
    mapped = jnp.stack(
        [
            jnp.sum(weight * part[:, (q + 1) * mine : (q + 2) * mine], axis=0) / bottom
            for q in range(2)
        ]
    ).reshape(2, mine * BLK)

    own_r = join(lax.dynamic_slice_in_dim(r, chip * mine, mine, 1))
    own_log = lax.dynamic_slice_in_dim(source_log, chip * mine, mine)
    x_half = 0.5 * jnp.sum(jnp.square(source_latent.astype(f32)), axis=0)
    out_source = (bias_of(own_log, own_r).reshape(-1) + x_half) / 32.0
    b = bias_of(target_log, join(c))
    out_target = lax.dynamic_slice_in_dim((b + y_half) / 32.0, core * own_k, own_k).reshape(-1)
    return out_source, out_target, mapped


def solution(mesh):
    in_specs = (
        P(None, ("row", "col")),
        P(None, "col"),
        P("row"),
        P("col"),
        P(None, "col"),
        P("row", None),
    )
    out_specs = (P(("row", "col")), P("col"), P(None, ("row", "col")))
    return jax.shard_map(
        on_device, mesh=mesh, in_specs=in_specs, out_specs=out_specs, check_vma=False
    )
```

profile of v0, /device:TPU:1, one launch (start us, length us, event | category | flops | bytes accessed | tf_op | source)
XLA Modules:
  0.0 118.7 jit_solution(13021884319292933846)
XLA Ops:
  0.6 0.0 copy-start
  0.6 0.7 broadcast_in_dim.49
  1.4 1.9 %concatenate.7 = bf16[80,2048]{1,0:T(8,128)(2,1)S(1)} concatenate(bf16[64,2048]{1,0:T(8,128)(2,1)} %param.7, bf16[2,2048]{1,0:T(2,128)(2,1)} %param.10, bf16[1,2048]{1,0:T(2,128)(2,1)S(1)} %broadcast_in_dim.48, bf16[1,2048]{1,0:T(2,128)(2,1)S(1)} %broadcast_in_dim.49, bf16[12,2048]{1,0:T(8,128)(2,1)S(1)} %broadcast_in_dim.50), dimensions={0} | concatenate | bytes 655360 | tf_op jit(solution)/shard_map/concatenate | solution.py:270
  3.3 3.3 %collective-permute-start = (bf16[80,2048]{1,0:T(8,128)(2,1)S(1)}, bf16[80,2048]{1,0:T(8,128)(2,1)S(1)}, u32[]{:S(2)}, u32[]{:S(2)}) collective-permute-start(bf16[80,2048]{1,0:T(8,128)(2,1)S(1)} %concatenate.7), channel_id=1, source_target_pairs={{0,1},{1,0},{2,3},{3,2},{4,5},{5,4},{6,7},{7,6},{8,9},{9,8},{10,11... | collective-permute-start | bytes 983048 | tf_op jit(solution)/shard_map/ppermute | solution.py:280
  6.6 0.0 copy-done
  6.7 0.9 broadcast_in_dim.29
  7.6 0.0 copy-start.2
  7.6 5.2 %all-to-all-start = ((bf16[16,2,64,128]{3,2,1,0:T(8,128)(2,1)}), bf16[16,2,64,128]{3,2,1,0:T(8,128)(2,1)S(1)}, u32[]{:S(2)}, u32[]{:S(2)}) async-start(bf16[16,2,64,128]{3,2,1,0:T(8,128)(2,1)} %broadcast_in_dim.29), calls=%async_computation | async-start | bytes 1048576 | tf_op jit(solution)/shard_map/all_to_all | solution.py:30
  12.8 0.0 copy-done.2
  12.8 0.1 copy.22
  12.9 0.7 fusion.4
  13.5 0.1 copy.23
  13.6 0.2 fusion.9
  13.8 0.1 copy.28
  13.9 0.1 convolution_bitcast_fusion
  14.1 0.1 copy.27
  14.1 0.4 select_reduce_fusion
  14.5 0.7 fusion.15.list_ref
  15.2 0.0 collective-permute-done
  15.2 0.1 multiply_reduce_fusion
  15.4 8.4 %all-to-all-done = bf16[16,2,64,128]{3,2,1,0:T(8,128)(2,1)S(1)} async-done(((bf16[16,2,64,128]{3,2,1,0:T(8,128)(2,1)}), bf16[16,2,64,128]{3,2,1,0:T(8,128)(2,1)S(1)}, u32[]{:S(2)}, u32[]{:S(2)}) %all-to-all-start) | async-done | bytes 524320 | tf_op jit(solution)/shard_map/all_to_all | solution.py:30
  23.8 0.0 copy-start.1
  23.8 3.6 %shard_map.85 = f32[16,32,128]{2,1,0:T(8,128)} custom-call(s32[1]{0:T(128)} %bitcast.3.count_ref, s32[384]{0:T(512)S(1)} %fusion.15.list_ref, bf16[32,64,128]{2,1,0:T(8,128)(2,1)S(1)} %bitcast.26, bf16[80,4096]{1,0:T(8,128)(2,1)S(1)} %pad_maximum_fusion.pack_ref, f32[32,128]{1,0:T(8,128)S(1)} %fusion.22.b_ref), custom_call_target="tpu_custom_call" | custom-call | tf_op jit(solution)/shard_map/pallas_call | solution.py:219
  27.4 3.5 %all-to-all-start.1 = ((f32[16,32,128]{2,1,0:T(8,128)}), f32[16,32,128]{2,1,0:T(8,128)S(1)}, u32[]{:S(2)}, u32[]{:S(2)}) async-start(f32[16,32,128]{2,1,0:T(8,128)} %shard_map.85), calls=%async_computation.1 | async-start | bytes 524288 | tf_op jit(solution)/shard_map/all_to_all | solution.py:30
  30.9 0.0 copy-done.1
  30.9 7.5 %all-to-all-done.1.r_ref = f32[16,32,128]{2,1,0:T(8,128)S(1)} async-done(((f32[16,32,128]{2,1,0:T(8,128)}), f32[16,32,128]{2,1,0:T(8,128)S(1)}, u32[]{:S(2)}, u32[]{:S(2)}) %all-to-all-start.1) | async-done | bytes 262176 | tf_op jit(solution)/shard_map/all_to_all | solution.py:30
  38.5 3.7 %shard_map.86 = f32[16,32,128]{2,1,0:T(8,128)} custom-call(s32[1]{0:T(128)} %bitcast.3.count_ref, s32[384]{0:T(512)S(1)} %fusion.15.list_ref, bf16[32,64,128]{2,1,0:T(8,128)(2,1)S(1)} %bitcast.27, bf16[80,4096]{1,0:T(8,128)(2,1)S(1)} %pad_maximum_fusion.pack_ref, f32[16,32,128]{2,1,0:T(8,128)S(1)} %all-to-all-done.1.r_ref, f32[32,128]{1,0:T(8,128)S(1)} %bitcast.34), custom_call_target="tpu_custom_call" | custom-call | tf_op jit(solution)/shard_map/pallas_call | solution.py:219
  42.2 12.2 %all-to-all-start.2 = ((f32[16,32,128]{2,1,0:T(8,128)}), f32[16,32,128]{2,1,0:T(8,128)S(1)}, u32[]{:S(2)}, u32[]{:S(2)}) async-start(f32[16,32,128]{2,1,0:T(8,128)} %shard_map.86), calls=%async_computation.2 | async-start | bytes 524288 | tf_op jit(solution)/shard_map/all_to_all | solution.py:30
  54.4 11.7 %all-to-all-done.2.c_ref = f32[16,32,128]{2,1,0:T(8,128)S(1)} async-done(((f32[16,32,128]{2,1,0:T(8,128)}), f32[16,32,128]{2,1,0:T(8,128)S(1)}, u32[]{:S(2)}, u32[]{:S(2)}) %all-to-all-start.2) | async-done | bytes 262176 | tf_op jit(solution)/shard_map/all_to_all | solution.py:30
  66.1 3.6 %shard_map.87 = f32[16,32,128]{2,1,0:T(8,128)} custom-call(s32[1]{0:T(128)} %bitcast.3.count_ref, s32[384]{0:T(512)S(1)} %fusion.15.list_ref, bf16[32,64,128]{2,1,0:T(8,128)(2,1)S(1)} %bitcast.28, bf16[80,4096]{1,0:T(8,128)(2,1)S(1)} %pad_maximum_fusion.pack_ref, f32[16,32,128]{2,1,0:T(8,128)S(1)} %all-to-all-done.2.c_ref, f32[32,128]{1,0:T(8,128)S(1)} %bitcast.31), custom_call_target="tpu_custom_call" | custom-call | tf_op jit(solution)/shard_map/pallas_call | solution.py:219
  69.7 3.5 %all-to-all-start.3 = ((f32[16,32,128]{2,1,0:T(8,128)}), f32[16,32,128]{2,1,0:T(8,128)S(1)}, u32[]{:S(2)}, u32[]{:S(2)}) async-start(f32[16,32,128]{2,1,0:T(8,128)} %shard_map.87), calls=%async_computation.3 | async-start | bytes 524288 | tf_op jit(solution)/shard_map/all_to_all | solution.py:30
  73.3 9.2 %all-to-all-done.3.r_ref = f32[16,32,128]{2,1,0:T(8,128)S(1)} async-done(((f32[16,32,128]{2,1,0:T(8,128)}), f32[16,32,128]{2,1,0:T(8,128)S(1)}, u32[]{:S(2)}, u32[]{:S(2)}) %all-to-all-start.3) | async-done | bytes 262176 | tf_op jit(solution)/shard_map/all_to_all | solution.py:30
  82.4 3.7 %shard_map.88 = f32[16,32,128]{2,1,0:T(8,128)} custom-call(s32[1]{0:T(128)} %bitcast.3.count_ref, s32[384]{0:T(512)S(1)} %fusion.15.list_ref, bf16[32,64,128]{2,1,0:T(8,128)(2,1)S(1)} %bitcast.29, bf16[80,4096]{1,0:T(8,128)(2,1)S(1)} %pad_maximum_fusion.pack_ref, f32[16,32,128]{2,1,0:T(8,128)S(1)} %all-to-all-done.3.r_ref, f32[32,128]{1,0:T(8,128)S(1)} %bitcast.35), custom_call_target="tpu_custom_call" | custom-call | tf_op jit(solution)/shard_map/pallas_call | solution.py:219
  86.2 3.8 %all-to-all-start.4 = ((f32[16,32,128]{2,1,0:T(8,128)}), f32[16,32,128]{2,1,0:T(8,128)S(1)}, u32[]{:S(2)}, u32[]{:S(2)}) async-start(f32[16,32,128]{2,1,0:T(8,128)} %shard_map.88), calls=%async_computation.4 | async-start | bytes 524288 | tf_op jit(solution)/shard_map/all_to_all | solution.py:30
  90.1 0.6 fusion.20
  90.6 11.1 %all-to-all-done.4.c_ref = f32[16,32,128]{2,1,0:T(8,128)S(1)} async-done(((f32[16,32,128]{2,1,0:T(8,128)}), f32[16,32,128]{2,1,0:T(8,128)S(1)}, u32[]{:S(2)}, u32[]{:S(2)}) %all-to-all-start.4) | async-done | bytes 262176 | tf_op jit(solution)/shard_map/all_to_all | solution.py:30
  101.7 4.4 %shard_map.89 = f32[16,8,128]{2,1,0:T(8,128)} custom-call(s32[1]{0:T(128)} %bitcast.3.count_ref, s32[384]{0:T(512)S(1)} %fusion.15.list_ref, bf16[32,64,128]{2,1,0:T(8,128)(2,1)S(1)} %bitcast.30, bf16[80,4096]{1,0:T(8,128)(2,1)S(1)} %pad_maximum_fusion.pack_ref, f32[16,32,128]{2,1,0:T(8,128)S(1)} %all-to-all-done.4.c_ref, f32[32,128]{1,0:T(8,128)S(1)} %bitcast.32), custom_call_target="tpu_custom_call" | custom-call | tf_op jit(solution)/shard_map/pallas_call | solution.py:219
  106.1 5.0 %all-to-all-start.5 = ((f32[16,8,128]{2,1,0:T(8,128)}), f32[16,8,128]{2,1,0:T(8,128)S(1)}, u32[]{:S(2)}, u32[]{:S(2)}) async-start(f32[16,8,128]{2,1,0:T(8,128)} %shard_map.89), calls=%async_computation.5 | async-start | bytes 131072 | tf_op jit(solution)/shard_map/all_to_all | solution.py:30
  111.1 0.1 exponential_reduce_fusion
  111.2 0.6 fusion.12
  111.8 6.2 %all-to-all-done.5 = f32[16,8,128]{2,1,0:T(8,128)S(1)} async-done(((f32[16,8,128]{2,1,0:T(8,128)}), f32[16,8,128]{2,1,0:T(8,128)S(1)}, u32[]{:S(2)}, u32[]{:S(2)}) %all-to-all-start.5) | async-done | bytes 65568 | tf_op jit(solution)/shard_map/all_to_all | solution.py:30
  118.1 0.6 pad_maximum_fusion.1
  (21 shorter events, 0.4 us)
Async XLA Ops:
  0.6 6.0 %copy-start = (bf16[64,256]{1,0:T(8,128)(2,1)S(1)}, bf16[64,256]{1,0:T(8,128)(2,1)}, u32[]{:S(2)}) copy-start(bf16[64,256]{1,0:T(8,128)(2,1)} %param.6) | copy-start | bytes 98308
  3.3 11.9 %collective-permute-start = (bf16[80,2048]{1,0:T(8,128)(2,1)S(1)}, bf16[80,2048]{1,0:T(8,128)(2,1)S(1)}, u32[]{:S(2)}, u32[]{:S(2)}) collective-permute-start(bf16[80,2048]{1,0:T(8,128)(2,1)S(1)} %concatenate.7), channel_id=1, source_target_pairs={{0,1},{1,0},{2,3},{3,2},{4,5},{5,4},{6,7},{7,6},{8,9},{9,8},{10,11... | collective-permute-start | bytes 983048 | tf_op jit(solution)/shard_map/ppermute | solution.py:280
  7.6 5.2 %copy-start.2 = (s32[64,32]{0,1:T(8,128)S(1)}, s32[64,32]{0,1:T(8,128)}, u32[]{:S(2)}) copy-start(s32[64,32]{0,1:T(8,128)} %param.11) | copy-start | bytes 24580
  7.6 16.2 %all-to-all-start = ((bf16[16,2,64,128]{3,2,1,0:T(8,128)(2,1)}), bf16[16,2,64,128]{3,2,1,0:T(8,128)(2,1)S(1)}, u32[]{:S(2)}, u32[]{:S(2)}) async-start(bf16[16,2,64,128]{3,2,1,0:T(8,128)(2,1)} %broadcast_in_dim.29), calls=%async_computation | async-start | bytes 1048576 | tf_op jit(solution)/shard_map/all_to_all | solution.py:30
  23.8 7.1 %copy-start.1 = (f32[8192]{0:T(1024)S(1)}, f32[8192]{0:T(1024)}, u32[]{:S(2)}) copy-start(f32[8192]{0:T(1024)} %param.8) | copy-start | bytes 98308
  27.4 11.1 %all-to-all-start.1 = ((f32[16,32,128]{2,1,0:T(8,128)}), f32[16,32,128]{2,1,0:T(8,128)S(1)}, u32[]{:S(2)}, u32[]{:S(2)}) async-start(f32[16,32,128]{2,1,0:T(8,128)} %shard_map.85), calls=%async_computation.1 | async-start | bytes 524288 | tf_op jit(solution)/shard_map/all_to_all | solution.py:30
  42.2 23.9 %all-to-all-start.2 = ((f32[16,32,128]{2,1,0:T(8,128)}), f32[16,32,128]{2,1,0:T(8,128)S(1)}, u32[]{:S(2)}, u32[]{:S(2)}) async-start(f32[16,32,128]{2,1,0:T(8,128)} %shard_map.86), calls=%async_computation.2 | async-start | bytes 524288 | tf_op jit(solution)/shard_map/all_to_all | solution.py:30
  69.7 12.8 %all-to-all-start.3 = ((f32[16,32,128]{2,1,0:T(8,128)}), f32[16,32,128]{2,1,0:T(8,128)S(1)}, u32[]{:S(2)}, u32[]{:S(2)}) async-start(f32[16,32,128]{2,1,0:T(8,128)} %shard_map.87), calls=%async_computation.3 | async-start | bytes 524288 | tf_op jit(solution)/shard_map/all_to_all | solution.py:30
  86.2 15.6 %all-to-all-start.4 = ((f32[16,32,128]{2,1,0:T(8,128)}), f32[16,32,128]{2,1,0:T(8,128)S(1)}, u32[]{:S(2)}, u32[]{:S(2)}) async-start(f32[16,32,128]{2,1,0:T(8,128)} %shard_map.88), calls=%async_computation.4 | async-start | bytes 524288 | tf_op jit(solution)/shard_map/all_to_all | solution.py:30
  106.1 11.9 %all-to-all-start.5 = ((f32[16,8,128]{2,1,0:T(8,128)}), f32[16,8,128]{2,1,0:T(8,128)S(1)}, u32[]{:S(2)}, u32[]{:S(2)}) async-start(f32[16,8,128]{2,1,0:T(8,128)} %shard_map.89), calls=%async_computation.5 | async-start | bytes 131072 | tf_op jit(solution)/shard_map/all_to_all | solution.py:30
where the time goes:
time: 120 us; the launch traced here: 119 us
  waiting for transfers between devices  54 us (45%)
  starting transfers between devices  36.6 us (30%)
  Pallas kernels  19 us (16%)
  other arithmetic  4.07 us (3%)
  local copies, waits for them, and re-layouts  3.88 us (3%)
    all_to_all x6, waiting for transfers between devices, exchange(): return lax.all_to_all(x, axis, 0, 0, axis_index_groups=groups)  54 us
    all_to_all x6, starting transfers between devices, exchange(): return lax.all_to_all(x, axis, 0, 0, axis_index_groups=groups)  33.2 us
    pallas_call x5, Pallas kernels, call(): pl.pallas_call(kernel, out_shape=jax.ShapeDtypeStruct(shape, jnp.float32)...  19 us
    ppermute x1, starting transfers between devices, on_device(): other = lax.ppermute(pack, 'col', [(i, i ^ 1) for i in range(cols)])  3.33 us
  transfers between devices with their start and end apart: 7, of which 6 were waited for; matrix products, arithmetic and copies ran while one was open for 4% of the time, Pallas kernels for 0%

commit v1 on v0

v1 whole, which is shorter than its diff:
```python
import functools

import jax
import jax.numpy as jnp
from jax import lax
from jax.experimental import pallas as pl
from jax.experimental.pallas import tpu as pltpu
from jax.sharding import PartitionSpec as P

LAT = 64
BLK = 128
ITERS = 2
NEG = -1e30
LN2 = 0.6931471805599453
KAPPA = 0.3125 / LN2
UNROLL = 32
PACK = 80
GROUP = 16


def chip_groups(cols):
    return [[c for c in range(cols) if c % 2 == core] for core in range(2)]


def swap_cores(x, cols):
    return lax.ppermute(x, "col", [(i, i ^ 1) for i in range(cols)])


def exchange(x, axis, groups=None):
    return lax.all_to_all(x, axis, 0, 0, axis_index_groups=groups)


def join(parts):
    top = jnp.max(parts, axis=0)
    return top + jnp.log2(jnp.sum(jnp.exp2(parts - top[None]), axis=0))


def join_pair(a, b):
    return jnp.maximum(a, b) + jnp.log2(1.0 + jnp.exp2(-jnp.abs(a - b)))


def bias_of(mass, level):
    return 3.2 * (mass - LN2 * level)


def pieces(a):
    hi = a.astype(jnp.bfloat16)
    rest = a - hi.astype(jnp.float32)
    mid = rest.astype(jnp.bfloat16)
    low = (rest - mid.astype(jnp.float32)).astype(jnp.bfloat16)
    return hi, mid, low


def fill_hot(hot_ref):
    row = lax.broadcasted_iota(jnp.int32, (BLK - LAT, BLK), 0)
    for q in range(GROUP):
        hit = ((row & (GROUP - 1)) == q) & (row < 3 * GROUP)
        hot_ref[q] = jnp.where(hit, 1.0, 0.0).astype(jnp.bfloat16)


def fill_biased(plain_ref, bias, full_ref):
    for first in range(0, plain_ref.shape[0], GROUP):
        hi, mid, low = pieces(bias[first : first + GROUP])
        blank = jnp.zeros((LAT, BLK), jnp.bfloat16)
        side = jnp.concatenate([blank, hi, mid, low, blank[:GROUP]], axis=0).T
        for block in range(first, first + GROUP):
            full_ref[block] = plain_ref[block] + side


def columns(jb):
    return pl.ds(pl.multiple_of(jb * BLK, BLK), BLK)


def dot(lhs, rhs):
    return jnp.dot(lhs, rhs, preferred_element_type=jnp.float32)


def sweep(list_ref, body):
    last_row = list_ref.shape[0] - 1
    turns = (list_ref[last_row, 0] + (UNROLL - 1)) // UNROLL
    per_row = BLK // UNROLL

    def turn(g, c):
        row, start = g // per_row, (g % per_row) * UNROLL
        body([list_ref[row, start + u] for u in range(UNROLL)])
        return c

    lax.fori_loop(0, turns, turn, 0)


def source_of(e):
    return e >> 6


def target_of(e):
    return e & 63


def fold_into(index, m, s, m_ref, s_ref):
    old = m_ref[index]
    new = jnp.maximum(old, m)
    s_ref[index] = s_ref[index] * jnp.exp2((old - new) * KAPPA) + s * jnp.exp2((m - new) * KAPPA)
    m_ref[index] = new


def finish(m, s):
    top = jnp.max(m, axis=1)
    total = jnp.sum(s * jnp.exp2((m - top[:, None, :]) * KAPPA), axis=1)
    return jnp.where(total > 0.0, top * KAPPA + jnp.log2(total), NEG)


def partial_stats(acc):
    split = acc.reshape(BLK // 8, 8, BLK)
    m = jnp.max(split, axis=0)
    return m, jnp.sum(jnp.exp2((split - m[None]) * KAPPA), axis=0)


def clear(m_ref, s_ref):
    m_ref[...] = jnp.full_like(m_ref, NEG)
    s_ref[...] = jnp.zeros_like(s_ref)


def source_block(x_ref, s):
    return x_ref[s >> 1, :, columns(s & 1)]


def target_by_source(entries, x_ref, yt_ref, hot_ref):
    last = 2 * x_ref.shape[0] - 1
    return [
        dot(
            yt_ref[target_of(e) & 31],
            jnp.concatenate(
                [source_block(x_ref, jnp.minimum(source_of(e), last)), hot_ref[e & (GROUP - 1)]],
                axis=0,
            ),
        )
        for e in entries
    ]


def transposed(block):
    return jnp.concatenate([block, jnp.zeros_like(block)], axis=0).T


def target_side_kernel(pack_ref, yt0_ref, minus_half_ref):
    for q in range(yt0_ref.shape[0]):
        block = pack_ref[:LAT, q * BLK : (q + 1) * BLK]
        yt0_ref[q] = transposed(block)
        minus_half_ref[q : q + 1, :] = -0.5 * jnp.sum(
            jnp.square(block.astype(jnp.float32)), axis=0, keepdims=True
        )


def spread_kernel(in_ref, out_ref):
    out_ref[...] = jnp.broadcast_to(in_ref[...][None], out_ref.shape)


def source_side_kernel(x_ref, xt0_ref):
    for q in range(xt0_ref.shape[0]):
        xt0_ref[q] = transposed(x_ref[q // 2, :, (q % 2) * BLK : (q % 2 + 1) * BLK])


def start_copy(from_ref, to_ref, sem):
    copy = pltpu.make_async_copy(from_ref, to_ref, sem)
    copy.start()
    return copy


def first_row_kernel(tiles_ref, b_ref, x_ref, yt0_ref, out_ref, list_ref, mass_ref, sems, *scratch):
    copy = start_copy(tiles_ref, list_ref, sems.at[0])
    row_pass(copy, list_ref, x_ref, yt0_ref, lambda: b_ref[...], out_ref, *scratch)


def row_kernel(
    tiles_ref, log_ref, x_ref, yt0_ref, c_ref, d_ref, out_ref, list_ref, mass_ref, sems, *scratch
):
    copy = start_copy(tiles_ref, list_ref, sems.at[0])
    mass = start_copy(log_ref, mass_ref, sems.at[1])

    def bias():
        level = join_pair(c_ref[...], d_ref[...])
        mass.wait()
        return bias_of(mass_ref[...], level)

    row_pass(copy, list_ref, x_ref, yt0_ref, bias, out_ref, *scratch)


def row_pass(copy, list_ref, x_ref, yt0_ref, bias, out_ref, yt_ref, hot_ref, m_ref, s_ref):
    fill_hot(hot_ref)
    clear(m_ref, s_ref)
    fill_biased(yt0_ref, bias(), yt_ref)
    copy.wait()

    def body(entries):
        stats = [partial_stats(a) for a in target_by_source(entries, x_ref, yt_ref, hot_ref)]
        for e, (m, s) in zip(entries, stats):
            fold_into(source_of(e), m, s, m_ref, s_ref)

    sweep(list_ref, body)
    n = m_ref.shape[0] - 1
    out_ref[...] = jnp.broadcast_to(finish(m_ref[:n], s_ref[:n])[None], out_ref.shape)


def col_kernel(
    tiles_ref, log_ref, xt0_ref, pack_ref, r_ref, out_ref, list_ref, mass_ref, sems, xt_ref, hot_ref, m_ref, s_ref
):
    copy = start_copy(tiles_ref, list_ref, sems.at[0])
    mass = start_copy(log_ref, mass_ref, sems.at[1])
    n = xt0_ref.shape[0]
    fill_hot(hot_ref)
    clear(m_ref, s_ref)
    level = join(r_ref[...])
    mass.wait()
    fill_biased(xt0_ref, bias_of(mass_ref[...], level), xt_ref)
    copy.wait()

    def body(entries):
        accs = []
        for e in entries:
            block = pack_ref[:LAT, columns(target_of(e) & 31)]
            rhs = jnp.concatenate([block, hot_ref[source_of(e) & (GROUP - 1)]], axis=0)
            accs.append(dot(xt_ref[jnp.minimum(source_of(e), n - 1)], rhs))
        stats = [partial_stats(acc) for acc in accs]
        for e, (m, s) in zip(entries, stats):
            fold_into(target_of(e), m, s, m_ref, s_ref)

    sweep(list_ref, body)
    k = m_ref.shape[0] - 1
    out_ref[...] = jnp.broadcast_to(finish(m_ref[:k], s_ref[:k])[None], out_ref.shape)


def project_kernel(
    tiles_ref, log_ref, x_ref, yt0_ref, pack_ref, c_ref, d_ref, out_ref, list_ref, mass_ref, sems, yt_ref, hot_ref, m_ref, w_ref
):
    copy = start_copy(tiles_ref, list_ref, sems.at[0])
    mass = start_copy(log_ref, mass_ref, sems.at[1])
    fill_hot(hot_ref)
    clear(m_ref, w_ref)
    level = join_pair(c_ref[...], d_ref[...])
    mass.wait()
    fill_biased(yt0_ref, bias_of(mass_ref[...], level), yt_ref)
    copy.wait()

    def body(entries):
        stats = []
        for e, acc in zip(entries, target_by_source(entries, x_ref, yt_ref, hot_ref)):
            m = jnp.max(acc, axis=0, keepdims=True)
            p = jnp.exp2((acc - m) * KAPPA)
            hi = p.astype(jnp.bfloat16)
            low = (p - hi.astype(jnp.float32)).astype(jnp.bfloat16)
            side = pack_ref[LAT:, columns(target_of(e) & 31)]
            both = jnp.concatenate([hi, low], axis=0)
            stats.append((m, dot(jnp.concatenate([side, side], axis=1), both)[:8]))
        for e, (m, w) in zip(entries, stats):
            fold_into(source_of(e), m, w, m_ref, w_ref)

    sweep(list_ref, body)
    out_ref[...] = jnp.zeros_like(out_ref)
    for ib in range(2 * x_ref.shape[0]):
        w = w_ref[ib]
        total = w[2:3]
        live = total > 0.0
        safe = jnp.where(live, total, 1.0)
        half = ib % 2
        out_ref[ib // 2, half : half + 1, :] = jnp.where(
            live, m_ref[ib] * KAPPA + jnp.log2(safe), NEG
        )
        out_ref[ib // 2, 2 + half : 3 + half, :] = w[0:1] / safe
        out_ref[ib // 2, 4 + half : 5 + half, :] = w[1:2] / safe


VMEM = pl.BlockSpec(memory_space=pltpu.VMEM)
HBM = pl.BlockSpec(memory_space=pltpu.HBM)


def call(kernel, outs, scratch, far, near):
    put = pltpu.with_memory_space_constraint
    return pl.pallas_call(
        kernel,
        out_shape=outs,
        in_specs=[HBM] * len(far) + [VMEM] * len(near),
        out_specs=jax.tree.map(lambda _: VMEM, outs),
        scratch_shapes=scratch,
        compiler_params=pltpu.CompilerParams(vmem_limit_bytes=16 << 20),
    )(*(put(a, pltpu.HBM) for a in far), *(put(a, pltpu.VMEM) for a in near))


def tile_list(support, chip, per_chip, slots):
    rows, per_list = support.shape
    owned = support // per_chip == chip
    flags = owned.astype(jnp.float32)
    upto = (jnp.arange(per_list)[:, None] <= jnp.arange(per_list)[None, :]).astype(jnp.float32)
    before = (jnp.arange(rows)[None, :] < jnp.arange(rows)[:, None]).astype(jnp.float32)
    within = flags @ upto
    start = before @ within[:, -1:]
    place = jnp.where(owned, (within + start).astype(jnp.int32) - 1, -1)
    count = jnp.sum(owned.astype(jnp.int32))
    code = jnp.arange(rows, dtype=jnp.int32)[:, None] * 64 + support % per_chip
    slot = jnp.arange(slots, dtype=jnp.int32)
    listed = jnp.sum(
        jnp.where(place[:, :, None] == slot, code[:, :, None], 0), axis=(0, 1), dtype=jnp.int32
    )
    listed = jnp.where(slot < count, listed, rows * 64 + per_chip)
    return jnp.concatenate([listed, jnp.broadcast_to(count, (BLK,))]).reshape(-1, BLK)


def on_device(
    source_latent, target_latent, log_source_mass, log_target_mass, target_coords, support
):
    rows, cols = lax.axis_size("row"), lax.axis_size("col")
    here = lax.axis_index("col")
    chip, core = here // 2, here % 2
    chips = cols // 2
    mine = support.shape[0] // cols
    own_k = target_latent.shape[1] // BLK
    n, k = chips * mine, 2 * own_k
    bf16, f32 = jnp.bfloat16, jnp.float32
    by_chip = chip_groups(cols)

    def of_core(a):
        split = a.reshape((chips, 2, mine) + a.shape[1:])
        split = jnp.where(core == 0, split[:, 0], split[:, 1])
        return split.reshape((n,) + a.shape[1:])

    spread = pl.pallas_call(
        spread_kernel,
        out_shape=jax.ShapeDtypeStruct((chips,) + source_latent.shape, bf16),
        in_specs=[VMEM],
        out_specs=VMEM,
    )(source_latent)
    x = exchange(spread, "col", by_chip)

    def pair(a):
        other = swap_cores(a, cols)
        return jnp.concatenate(
            [jnp.where(core == 0, a, other), jnp.where(core == 0, other, a)], axis=1
        )

    width = 2 * target_latent.shape[1]
    targets = pair(target_latent)
    coords, target_log = pair(target_coords), pair(log_target_mass[None])
    pack = jnp.concatenate(
        [targets, coords, jnp.ones((1, width), bf16), jnp.zeros((PACK - LAT - 3, width), bf16)],
        axis=0,
    )
    target_log = target_log.astype(f32).reshape(k, BLK)
    source_log = of_core(log_source_mass.reshape(-1, BLK))
    tiles = tile_list(of_core(support), chip, k, 12 * mine * chips)

    common = [
        pltpu.SMEM(tiles.shape, jnp.int32),
        pltpu.VMEM((n, BLK), f32),
        pltpu.SemaphoreType.DMA((2,)),
        pltpu.VMEM((n, BLK, BLK), bf16),
        pltpu.VMEM((GROUP, BLK - LAT, BLK), bf16),
    ]
    row_scratch = common + [pltpu.VMEM((n + 1, 8, BLK), f32)] * 2
    col_scratch = common + [pltpu.VMEM((k + 1, 8, BLK), f32)] * 2
    project_scratch = common + [pltpu.VMEM((n + 1, 1, BLK), f32), pltpu.VMEM((n + 1, 8, BLK), f32)]

    tiles, source_log, target_log = lax.optimization_barrier((tiles, source_log, target_log))
    yt0, minus_half = call(
        target_side_kernel,
        [pltpu.VMEM((k, BLK, BLK), bf16), pltpu.VMEM((k, BLK), f32)],
        [],
        [],
        [pack],
    )
    to_chips = jax.ShapeDtypeStruct((chips, n, BLK), f32)
    to_rows = jax.ShapeDtypeStruct((rows, k, BLK), f32)
    for sweep_index in range(ITERS):
        if sweep_index == 0:
            r = call(first_row_kernel, to_chips, row_scratch, [tiles], [minus_half, x, yt0])
            xt0 = call(source_side_kernel, pltpu.VMEM((n, BLK, BLK), bf16), [], [], [x])
        else:
            r = call(row_kernel, to_chips, row_scratch, [tiles, target_log], [x, yt0, c, d])
        r = exchange(r, "col", by_chip)
        c = call(col_kernel, to_rows, col_scratch, [tiles, source_log], [xt0, pack, r])
        c = join(exchange(c, "row"))
        d = swap_cores(c, cols)
    to_owners = jax.ShapeDtypeStruct((chips, 8, BLK), f32)
    part = call(
        project_kernel,
        to_owners,
        project_scratch,
        [tiles, target_log],
        [x, yt0, pack, c, d],
    )
    part, r, source_latent = lax.optimization_barrier((part, r, source_latent))
    part = exchange(part, "col", by_chip)
    level = part[:, :mine]
    weight = jnp.exp2(level - jnp.max(level, axis=0))
    bottom = jnp.sum(weight, axis=0)
    mapped = jnp.stack(
        [
            jnp.sum(weight * part[:, (q + 1) * mine : (q + 2) * mine], axis=0) / bottom
            for q in range(2)
        ]
    ).reshape(2, mine * BLK)

    own_r = join(lax.dynamic_slice_in_dim(r, chip * mine, mine, 1))
    own_log = lax.dynamic_slice_in_dim(source_log, chip * mine, mine)
    x_half = 0.5 * jnp.sum(jnp.square(source_latent.astype(f32)), axis=0)
    out_source = (bias_of(own_log, own_r).reshape(-1) + x_half) / 32.0
    b = bias_of(target_log, join_pair(c, d))
    out_target = lax.dynamic_slice_in_dim((b - minus_half) / 32.0, core * own_k, own_k).reshape(-1)
    return out_source, out_target, mapped


def solution(mesh):
    in_specs = (
        P(None, ("row", "col")),
        P(None, "col"),
        P("row"),
        P("col"),
        P(None, "col"),
        P("row", None),
    )
    out_specs = (P(("row", "col")), P("col"), P(None, ("row", "col")))
    return jax.shard_map(
        on_device, mesh=mesh, in_specs=in_specs, out_specs=out_specs, check_vma=False
    )
```

time: 120 us -> 110 us (0.917)
  blocking collectives: 0 us -> 38 us
  waiting for transfers between devices: 54 us -> 18.9 us
  starting transfers between devices: 36.6 us -> 26.5 us
  Pallas kernels: 19 us -> 16.2 us
  other arithmetic: 4.07 us -> 6.03 us
  local copies, waits for them, and re-layouts: 3.88 us -> 2.41 us
    all_to_all x0 -> x3, blocking collectives: none -> 38 us  [exchange(): return lax.all_to_all(x, axis, 0, 0, axis_index_groups=groups)]
    all_to_all x6 -> x3, waiting for transfers between devices: 54 us -> 17.2 us  [exchange(): return lax.all_to_all(x, axis, 0, 0, axis_index_groups=groups)]
    all_to_all x6 -> x3, starting transfers between devices: 33.2 us -> 15.8 us  [exchange(): return lax.all_to_all(x, axis, 0, 0, axis_index_groups=groups)]
    ppermute x1 -> x5, starting transfers between devices: 3.33 us -> 10.7 us  [swap_cores(): return lax.ppermute(x, 'col', [(i, i ^ 1) for i in range(cols)])]
    pallas_call x5 -> x8, Pallas kernels: 19 us -> 16.2 us  [the longest x7 14.6 us: call(): pl.pallas_call(kernel, out_shape=outs, in_specs=[HBM] * len(far) + [VMEM]...]
    concatenate x1 -> x2, local copies, waits for them, and re-layouts: 1.93 us -> 0.15 us  [on_device(): jnp.concatenate([targets, coords, jnp.ones((1, width), bf16), jnp.zeros((...]
    ppermute x1 -> x5, waiting for transfers between devices: 0.01 us -> 1.68 us  [swap_cores(): return lax.ppermute(x, 'col', [(i, i ^ 1) for i in range(cols)])]
    reshape x1, local copies, waits for them, and re-layouts: 0.01 us -> 1.23 us  [tile_list(): jnp.concatenate([listed, jnp.broadcast_to(count, (BLK,))]).reshape(-1, BLK)]
  transfers between devices with their start and end apart: 7 -> 8, of which waited for: 6 -> 5; matrix products, arithmetic and copies ran while one was open for 4% -> 7% of each run, Pallas kernels for 0% -> 2%
where the time goes in v1:
time: 110 us; the launch traced here: 109 us
  blocking collectives  38 us (35%)
  starting transfers between devices  26.5 us (24%)
  waiting for transfers between devices  18.9 us (17%)
  Pallas kernels  16.2 us (15%)
  other arithmetic  6.03 us (5%)
  local copies, waits for them, and re-layouts  2.41 us (2%)
    all_to_all x3, blocking collectives, exchange(): return lax.all_to_all(x, axis, 0, 0, axis_index_groups=groups)  38 us
    all_to_all x3, waiting for transfers between devices, exchange(): return lax.all_to_all(x, axis, 0, 0, axis_index_groups=groups)  17.2 us
    all_to_all x3, starting transfers between devices, exchange(): return lax.all_to_all(x, axis, 0, 0, axis_index_groups=groups)  15.8 us
    pallas_call x7, Pallas kernels, call(): pl.pallas_call(kernel, out_shape=outs, in_specs=[HBM] * len(far) + [VMEM]...  14.6 us
    ppermute x5, starting transfers between devices, swap_cores(): return lax.ppermute(x, 'col', [(i, i ^ 1) for i in range(cols)])  10.7 us
  transfers between devices with their start and end apart: 8, of which 5 were waited for; matrix products, arithmetic and copies ran while one was open for 7% of the time, Pallas kernels for 2%

profile of v1, /device:TPU:1, one launch (start us, length us, event | category | flops | bytes accessed | tf_op | source)
XLA Modules:
  0.0 109.3 jit_solution(12215990575570508898)
XLA Ops:
  0.6 0.0 copy-start.4
  0.6 0.0 copy-start.3
  0.7 0.7 broadcast_in_dim.27
  1.4 0.0 copy-start.5
  1.4 0.0 copy-start.6
  1.4 0.0 copy-start
  1.4 3.3 %collective-permute-start = (bf16[1,2048]{1,0:T(2,128)(2,1)S(1)}, bf16[1,2048]{1,0:T(2,128)(2,1)S(1)}, u32[]{:S(2)}, u32[]{:S(2)}) collective-permute-start(bf16[1,2048]{1,0:T(2,128)(2,1)S(1)} %broadcast_in_dim.27), channel_id=1, source_target_pairs={{0,1},{1,0},{2,3},{3,2},{4,5},{5,4},{6,7},{7,6},{8,9},{9,8},{10,11... | collective-permute-start | bytes 12296 | tf_op jit(solution)/shard_map/ppermute | solution.py:26
  4.7 0.1 collective-permute-start.2
  4.8 0.4 collective-permute-start.1
  5.2 1.6 %shard_map.85 = bf16[16,64,256]{2,1,0:T(8,128)(2,1)} custom-call(bf16[64,256]{1,0:T(8,128)(2,1)} %in_ref.1), custom_call_target="tpu_custom_call" | custom-call | tf_op jit(solution)/shard_map/pallas_call | solution.py:325
  6.8 5.0 %all-to-all-start = ((bf16[16,64,256]{2,1,0:T(8,128)(2,1)}), bf16[16,64,256]{2,1,0:T(8,128)(2,1)S(1)}, u32[]{:S(2)}, u32[]{:S(2)}) async-start(bf16[16,64,256]{2,1,0:T(8,128)(2,1)} %shard_map.85), calls=%async_computation | async-start | bytes 1048576 | tf_op jit(solution)/shard_map/all_to_all | solution.py:30
  11.9 0.0 copy-done.4
  11.9 0.1 copy.20
  12.0 0.0 copy-done.3
  12.0 0.6 slice_select_fusion
  12.6 0.7 fusion.2
  13.3 0.1 copy.21
  13.4 0.2 fusion.6
  13.6 0.1 copy.26
  13.6 0.1 convolution_bitcast_fusion
  13.8 0.1 copy.25
  13.9 0.4 select_reduce_fusion
  14.2 0.7 fusion.12
  14.9 1.2 %pad_bitcast_fusion.tiles_ref = s32[4,128]{1,0:T(4,128)} fusion(s32[384]{0:T(512)S(1)} %fusion.12, s32[]{:T(128)} %get-tuple-element.22), kind=kLoop, calls=%fused_computation.55 | loop fusion | bytes 3588 | tf_op jit(solution)/shard_map/reshape | solution.py:304
  16.1 0.1 pad.7.clone
  16.2 0.1 pad.8.clone
  16.3 0.0 collective-permute-done
  16.3 0.0 copy-done.5
  16.3 0.6 maximum_convert_fusion
  16.9 0.0 collective-permute-done.2
  16.9 0.0 copy-done.6
  17.0 0.0 collective-permute-done.1
  17.0 0.0 copy-done
  17.0 0.2 maximum_maximum_fusion.pack_ref
  17.2 0.3 shard_map.86
  17.6 5.3 %all-to-all-done.x_ref = bf16[16,64,256]{2,1,0:T(8,128)(2,1)S(1)} async-done(((bf16[16,64,256]{2,1,0:T(8,128)(2,1)}), bf16[16,64,256]{2,1,0:T(8,128)(2,1)S(1)}, u32[]{:S(2)}, u32[]{:S(2)}) %all-to-all-start) | async-done | bytes 524320 | tf_op jit(solution)/shard_map/all_to_all | solution.py:30
  22.9 2.9 %shard_map.88 = f32[16,32,128]{2,1,0:T(8,128)} custom-call(s32[4,128]{1,0:T(4,128)} %pad_bitcast_fusion.tiles_ref, f32[32,128]{1,0:T(8,128)S(1)} %get-tuple-element.15.b_ref, bf16[16,64,256]{2,1,0:T(8,128)(2,1)S(1)} %all-to-all-done.x_ref, bf16[32,128,128]{2,1,0:T(8,128)(2,1)S(1)} %get-tuple-element.14.yt0_ref), custom_call_target="tpu_custom_call" | custom-call | tf_op jit(solution)/shard_map/pallas_call | solution.py:278
  25.8 4.6 %all-to-all-start.1 = ((f32[16,32,128]{2,1,0:T(8,128)}), f32[16,32,128]{2,1,0:T(8,128)S(1)}, u32[]{:S(2)}, u32[]{:S(2)}) async-start(f32[16,32,128]{2,1,0:T(8,128)} %shard_map.88), calls=%async_computation.1 | async-start | bytes 524288 | tf_op jit(solution)/shard_map/all_to_all | solution.py:30
  30.4 0.3 shard_map.87.xt0_ref
  30.8 7.3 %all-to-all-done.1.r_ref = f32[16,32,128]{2,1,0:T(8,128)S(1)} async-done(((f32[16,32,128]{2,1,0:T(8,128)}), f32[16,32,128]{2,1,0:T(8,128)S(1)}, u32[]{:S(2)}, u32[]{:S(2)}) %all-to-all-start.1) | async-done | bytes 262176 | tf_op jit(solution)/shard_map/all_to_all | solution.py:30
  38.1 2.5 %shard_map.89 = f32[8,32,128]{2,1,0:T(8,128)S(1)} custom-call(s32[4,128]{1,0:T(4,128)} %pad_bitcast_fusion.tiles_ref, f32[32,128]{1,0:T(8,128)} %bitcast.25, bf16[32,128,128]{2,1,0:T(8,128)(2,1)S(1)} %shard_map.87.xt0_ref, bf16[80,4096]{1,0:T(8,128)(2,1)S(1)} %maximum_maximum_fusion.pack_ref, f32[16,32,128]{2,1,0:T(8,128)S(1)} %all-to-all-done.1.r_ref), custom_call_target="tpu_custom_call" | custom-call | tf_op jit(solution)/shard_map/pallas_call | solution.py:278
  40.6 14.9 %all_to_all.30 = f32[8,32,128]{2,1,0:T(8,128)S(1)} all-to-all(f32[8,32,128]{2,1,0:T(8,128)S(1)} %shard_map.89), channel_id=1, replica_groups=mesh['row'=8,'col'=32] {'row'}, dimensions={0} | all-to-all | bytes 262144 | tf_op jit(solution)/shard_map/all_to_all | solution.py:30
  55.5 4.2 %collective-permute-start.3 = (f32[32,128]{1,0:T(8,128)S(1)}, f32[32,128]{1,0:T(8,128)S(1)}, u32[]{:S(2)}, u32[]{:S(2)}) collective-permute-start(f32[32,128]{1,0:T(8,128)S(1)} %multiply_add_fusion.1.c_ref), channel_id=1, source_target_pairs={{0,1},{1,0},{2,3},{3,2},{4,5},{5,4},{6,7},{7,6},{8,9},{9,8},{10,11... | collective-permute-start | bytes 49160 | tf_op jit(solution)/shard_map/ppermute | solution.py:26
  59.7 0.8 collective-permute-done.3.d_ref
  60.5 2.5 %shard_map.90 = f32[16,32,128]{2,1,0:T(8,128)S(1)} custom-call(s32[4,128]{1,0:T(4,128)} %pad_bitcast_fusion.tiles_ref, f32[32,128]{1,0:T(8,128)} %bitcast.22, bf16[16,64,256]{2,1,0:T(8,128)(2,1)S(1)} %all-to-all-done.x_ref, bf16[32,128,128]{2,1,0:T(8,128)(2,1)S(1)} %get-tuple-element.14.yt0_ref, f32[32,128]{1,0:T(8,128)S(1)} %multiply_add_fusion.1.c_ref, ...), custom_call_target="tpu_custom_call" | custom-call | tf_op jit(solution)/shard_map/pallas_call | solution.py:278
  63.0 12.8 %all_to_all.31.r_ref = f32[16,32,128]{2,1,0:T(8,128)S(1)} all-to-all(f32[16,32,128]{2,1,0:T(8,128)S(1)} %shard_map.90), channel_id=1, replica_groups={{0,2,4,6,8,10,12,14,16,18,20,22,24,26,28,30},{1,3,5,7,9,11,13,15,17,19,..., dimensions={0} | all-to-all | bytes 524288 | tf_op jit(solution)/shard_map/all_to_all | solution.py:30
  75.8 2.5 %shard_map.91 = f32[8,32,128]{2,1,0:T(8,128)S(1)} custom-call(s32[4,128]{1,0:T(4,128)} %pad_bitcast_fusion.tiles_ref, f32[32,128]{1,0:T(8,128)} %bitcast.26, bf16[32,128,128]{2,1,0:T(8,128)(2,1)S(1)} %shard_map.87.xt0_ref, bf16[80,4096]{1,0:T(8,128)(2,1)S(1)} %maximum_maximum_fusion.pack_ref, f32[16,32,128]{2,1,0:T(8,128)S(1)} %all_to_all.31.r_ref), custom_call_target="tpu_custom_call" | custom-call | tf_op jit(solution)/shard_map/pallas_call | solution.py:278
  78.3 10.3 %all_to_all.32 = f32[8,32,128]{2,1,0:T(8,128)S(1)} all-to-all(f32[8,32,128]{2,1,0:T(8,128)S(1)} %shard_map.91), channel_id=1, replica_groups=mesh['row'=8,'col'=32] {'row'}, dimensions={0} | all-to-all | bytes 262144 | tf_op jit(solution)/shard_map/all_to_all | solution.py:30
  88.7 2.7 %collective-permute-start.4 = (f32[32,128]{1,0:T(8,128)S(1)}, f32[32,128]{1,0:T(8,128)S(1)}, u32[]{:S(2)}, u32[]{:S(2)}) collective-permute-start(f32[32,128]{1,0:T(8,128)S(1)} %multiply_add_fusion.c_ref), channel_id=1, source_target_pairs={{0,1},{1,0},{2,3},{3,2},{4,5},{5,4},{6,7},{7,6},{8,9},{9,8},{10,11... | collective-permute-start | bytes 49160 | tf_op jit(solution)/shard_map/ppermute | solution.py:26
  91.4 0.0 copy-start.2
  91.4 0.0 copy-start.1
  91.4 0.8 collective-permute-done.4.d_ref
  92.3 3.6 %shard_map.92 = f32[16,8,128]{2,1,0:T(8,128)} custom-call(s32[4,128]{1,0:T(4,128)} %pad_bitcast_fusion.tiles_ref, f32[32,128]{1,0:T(8,128)} %bitcast.23, bf16[16,64,256]{2,1,0:T(8,128)(2,1)S(1)} %all-to-all-done.x_ref, bf16[32,128,128]{2,1,0:T(8,128)(2,1)S(1)} %get-tuple-element.14.yt0_ref, bf16[80,4096]{1,0:T(8,128)(2,1)S(1)} %maximum_maximum_fusion.pack_ref, ...), custom_call_target="tpu_custom_call" | custom-call | tf_op jit(solution)/shard_map/pallas_call | solution.py:278
  96.0 0.0 copy-done.2
  96.0 6.1 %all-to-all-start.5 = ((f32[16,8,128]{2,1,0:T(8,128)}), f32[16,8,128]{2,1,0:T(8,128)S(1)}, u32[]{:S(2)}, u32[]{:S(2)}) async-start(f32[16,8,128]{2,1,0:T(8,128)} %shard_map.92), calls=%async_computation.5 | async-start | bytes 131072 | tf_op jit(solution)/shard_map/all_to_all | solution.py:30
  102.2 1.3 %fusion.17 = f32[256]{0:T(256)} fusion(f32[32,128]{1,0:T(8,128)} %bitcast.27, s32[]{:T(128)S(6)} %select_n.130, f32[256]{0:T(256)S(1)} %multiply_reduce_fusion, f32[2,128]{1,0:T(2,128)S(1)} %dynamic-slice_reduce_fusion, f32[2,128]{1,0:T(2,128)S(1)} %exponential_reduce_fusion.2), kind=kLoop, calls=%fused_computation.63 | loop fusion | flops 2048 | bytes 5124 | tf_op jit(solution)/shard_map/div | solution.py:404
  103.4 0.0 copy-done.1
  103.5 0.6 fusion.9
  104.1 4.6 %all-to-all-done.5 = f32[16,8,128]{2,1,0:T(8,128)S(1)} async-done(((f32[16,8,128]{2,1,0:T(8,128)}), f32[16,8,128]{2,1,0:T(8,128)S(1)}, u32[]{:S(2)}, u32[]{:S(2)}) %all-to-all-start.5) | async-done | bytes 65568 | tf_op jit(solution)/shard_map/all_to_all | solution.py:30
  108.8 0.6 pad_maximum_fusion
  (20 shorter events, 0.4 us)
Async XLA Ops:
  0.6 11.3 %copy-start.4 = (s32[64,32]{0,1:T(8,128)S(1)}, s32[64,32]{0,1:T(8,128)}, u32[]{:S(2)}) copy-start(s32[64,32]{0,1:T(8,128)} %param.11) | copy-start | bytes 24580
  0.6 11.4 %copy-start.3 = (f32[8192]{0:T(1024)S(1)}, f32[8192]{0:T(1024)}, u32[]{:S(2)}) copy-start(f32[8192]{0:T(1024)} %param.8) | copy-start | bytes 98308
  1.4 14.9 %copy-start.5 = (bf16[2048]{0:T(1024)(128)(2,1)S(1)}, bf16[2048]{0:T(1024)(128)(2,1)}, u32[]{:S(2)}) copy-start(bf16[2048]{0:T(1024)(128)(2,1)} %param.9) | copy-start | bytes 12292
  1.4 15.6 %copy-start.6 = (bf16[2,2048]{1,0:T(2,128)(2,1)S(1)}, bf16[2,2048]{1,0:T(2,128)(2,1)}, u32[]{:S(2)}) copy-start(bf16[2,2048]{1,0:T(2,128)(2,1)} %param.10) | copy-start | bytes 24580
  1.4 15.6 %copy-start = (bf16[64,2048]{1,0:T(8,128)(2,1)S(1)}, bf16[64,2048]{1,0:T(8,128)(2,1)}, u32[]{:S(2)}) copy-start(bf16[64,2048]{1,0:T(8,128)(2,1)} %param.7) | copy-start | bytes 786436
  1.4 14.9 %collective-permute-start = (bf16[1,2048]{1,0:T(2,128)(2,1)S(1)}, bf16[1,2048]{1,0:T(2,128)(2,1)S(1)}, u32[]{:S(2)}, u32[]{:S(2)}) collective-permute-start(bf16[1,2048]{1,0:T(2,128)(2,1)S(1)} %broadcast_in_dim.27), channel_id=1, source_target_pairs={{0,1},{1,0},{2,3},{3,2},{4,5},{5,4},{6,7},{7,6},{8,9},{9,8},{10,11... | collective-permute-start | bytes 12296 | tf_op jit(solution)/shard_map/ppermute | solution.py:26
  4.7 12.2 %collective-permute-start.2 = (bf16[2,2048]{1,0:T(2,128)(2,1)}, bf16[2,2048]{1,0:T(2,128)(2,1)S(1)}, u32[]{:S(2)}, u32[]{:S(2)}) collective-permute-start(bf16[2,2048]{1,0:T(2,128)(2,1)} %param.10), channel_id=1, source_target_pairs={{0,1},{1,0},{2,3},{3,2},{4,5},{5,4},{6,7},{7,6},{8,9},{9,8},{10,11... | collective-permute-start | bytes 24584 | tf_op jit(solution)/shard_map/ppermute | solution.py:26
  4.8 12.2 %collective-permute-start.1 = (bf16[64,2048]{1,0:T(8,128)(2,1)}, bf16[64,2048]{1,0:T(8,128)(2,1)S(1)}, u32[]{:S(2)}, u32[]{:S(2)}) collective-permute-start(bf16[64,2048]{1,0:T(8,128)(2,1)} %param.7), channel_id=1, source_target_pairs={{0,1},{1,0},{2,3},{3,2},{4,5},{5,4},{6,7},{7,6},{8,9},{9,8},{10,11... | collective-permute-start | bytes 786440 | tf_op jit(solution)/shard_map/ppermute | solution.py:26
  6.8 16.1 %all-to-all-start = ((bf16[16,64,256]{2,1,0:T(8,128)(2,1)}), bf16[16,64,256]{2,1,0:T(8,128)(2,1)S(1)}, u32[]{:S(2)}, u32[]{:S(2)}) async-start(bf16[16,64,256]{2,1,0:T(8,128)(2,1)} %shard_map.85), calls=%async_computation | async-start | bytes 1048576 | tf_op jit(solution)/shard_map/all_to_all | solution.py:30
  25.8 12.3 %all-to-all-start.1 = ((f32[16,32,128]{2,1,0:T(8,128)}), f32[16,32,128]{2,1,0:T(8,128)S(1)}, u32[]{:S(2)}, u32[]{:S(2)}) async-start(f32[16,32,128]{2,1,0:T(8,128)} %shard_map.88), calls=%async_computation.1 | async-start | bytes 524288 | tf_op jit(solution)/shard_map/all_to_all | solution.py:30
  55.5 5.0 %collective-permute-start.3 = (f32[32,128]{1,0:T(8,128)S(1)}, f32[32,128]{1,0:T(8,128)S(1)}, u32[]{:S(2)}, u32[]{:S(2)}) collective-permute-start(f32[32,128]{1,0:T(8,128)S(1)} %multiply_add_fusion.1.c_ref), channel_id=1, source_target_pairs={{0,1},{1,0},{2,3},{3,2},{4,5},{5,4},{6,7},{7,6},{8,9},{9,8},{10,11... | collective-permute-start | bytes 49160 | tf_op jit(solution)/shard_map/ppermute | solution.py:26
  88.7 3.5 %collective-permute-start.4 = (f32[32,128]{1,0:T(8,128)S(1)}, f32[32,128]{1,0:T(8,128)S(1)}, u32[]{:S(2)}, u32[]{:S(2)}) collective-permute-start(f32[32,128]{1,0:T(8,128)S(1)} %multiply_add_fusion.c_ref), channel_id=1, source_target_pairs={{0,1},{1,0},{2,3},{3,2},{4,5},{5,4},{6,7},{7,6},{8,9},{9,8},{10,11... | collective-permute-start | bytes 49160 | tf_op jit(solution)/shard_map/ppermute | solution.py:26
  91.4 4.6 %copy-start.2 = (bf16[64,256]{1,0:T(8,128)(2,1)S(1)}, bf16[64,256]{1,0:T(8,128)(2,1)}, u32[]{:S(2)}) copy-start(bf16[64,256]{1,0:T(8,128)(2,1)} %in_ref.1) | copy-start | bytes 98308
  91.4 12.0 %copy-start.1 = (f32[1,4096]{1,0:T(1,128)S(1)}, f32[1,4096]{1,0:T(1,128)}, u32[]{:S(2)}) copy-start(f32[1,4096]{1,0:T(1,128)} %maximum_convert_fusion) | copy-start | bytes 49156
  96.0 12.6 %all-to-all-start.5 = ((f32[16,8,128]{2,1,0:T(8,128)}), f32[16,8,128]{2,1,0:T(8,128)S(1)}, u32[]{:S(2)}, u32[]{:S(2)}) async-start(f32[16,8,128]{2,1,0:T(8,128)} %shard_map.92), calls=%async_computation.5 | async-start | bytes 131072 | tf_op jit(solution)/shard_map/all_to_all | solution.py:30

commit v2 on v1

v2 whole, which is shorter than its diff:
```python
import functools

import jax
import jax.numpy as jnp
from jax import lax
from jax.experimental import pallas as pl
from jax.experimental.pallas import tpu as pltpu
from jax.sharding import PartitionSpec as P

LAT = 64
BLK = 128
NEG = -1e30
LN2 = 0.6931471805599453
KAPPA = 0.3125 / LN2
LONG_TURN = 64
SHORT_TURN = 32
PACK = 80
GROUP = 16


def chip_groups(cols):
    return [[c for c in range(cols) if c % 2 == core] for core in range(2)]


def swap_cores(x, cols):
    return lax.ppermute(x, "col", [(i, i ^ 1) for i in range(cols)])


def exchange(x, axis, groups=None):
    return lax.all_to_all(x, axis, 0, 0, axis_index_groups=groups)


def join(parts):
    top = jnp.max(parts, axis=0)
    return top + jnp.log2(jnp.sum(jnp.exp2(parts - top[None]), axis=0))


def join_pair(a, b):
    return jnp.maximum(a, b) + jnp.log2(1.0 + jnp.exp2(-jnp.abs(a - b)))


def bias_of(mass, level):
    return 3.2 * (mass - LN2 * level)


def pieces(a):
    hi = a.astype(jnp.bfloat16)
    rest = a - hi.astype(jnp.float32)
    mid = rest.astype(jnp.bfloat16)
    low = (rest - mid.astype(jnp.float32)).astype(jnp.bfloat16)
    return hi, mid, low


def fill_hot(hot_ref):
    row = lax.broadcasted_iota(jnp.int32, hot_ref.shape[1:], 0)
    for q in range(GROUP):
        hot_ref[q] = jnp.where((row & (GROUP - 1)) == q, 1.0, 0.0).astype(jnp.bfloat16)


def fill_biased(plain_ref, bias, full_ref):
    for first in range(0, plain_ref.shape[0], GROUP):
        hi, mid, low = pieces(bias[first : first + GROUP])
        blank = jnp.zeros((LAT, BLK), jnp.bfloat16)
        side = jnp.concatenate([blank, hi, mid, low, jnp.ones_like(hi)], axis=0).T
        for block in range(first, first + GROUP):
            full_ref[block] = plain_ref[block] + side


def fill_tails(bias, tail_ref):
    row = lax.broadcasted_iota(jnp.int32, (GROUP, BLK), 0)
    hi, mid, low = (p.astype(jnp.float32) for p in pieces(bias))
    for block in range(bias.shape[0]):
        one = slice(block, block + 1)
        rows = jnp.where(row == 1, mid[one], jnp.where(row == 2, low[one], 0.0))
        tail_ref[block] = jnp.where(row == 0, hi[one], rows).astype(jnp.bfloat16)


def columns(jb):
    return pl.ds(pl.multiple_of(jb * BLK, BLK), BLK)


def dot(lhs, rhs):
    return jnp.dot(lhs, rhs, preferred_element_type=jnp.float32)


def sweep(list_ref, body):
    count = list_ref[list_ref.shape[0] - 1, 0]
    long_turns = count // LONG_TURN
    left = count - long_turns * LONG_TURN

    def turn(first, size):
        row, start = first // BLK, first % BLK
        body([list_ref[row, start + u] for u in range(size)])

    def long_turn(g, c):
        turn(g * LONG_TURN, LONG_TURN)
        return c

    def short_turn(g, c):
        turn(long_turns * LONG_TURN + g * SHORT_TURN, SHORT_TURN)
        return c

    lax.fori_loop(0, long_turns, long_turn, 0)
    lax.fori_loop(0, (left + (SHORT_TURN - 1)) // SHORT_TURN, short_turn, 0)


def source_of(e):
    return e >> 6


def target_of(e):
    return e & 63


def fold_into(index, m, s, m_ref, s_ref):
    old = m_ref[index]
    new = jnp.maximum(old, m)
    s_ref[index] = s_ref[index] * jnp.exp2((old - new) * KAPPA) + s * jnp.exp2((m - new) * KAPPA)
    m_ref[index] = new


def finish(m, s):
    top = jnp.max(m, axis=1)
    total = jnp.sum(s * jnp.exp2((m - top[:, None, :]) * KAPPA), axis=1)
    return jnp.where(total > 0.0, top * KAPPA + jnp.log2(total), NEG)


def partial_stats(acc):
    split = acc.reshape(BLK // 8, 8, BLK)
    m = jnp.max(split, axis=0)
    return m, jnp.sum(jnp.exp2((split - m[None]) * KAPPA), axis=0)


def clear(m_ref, s_ref):
    m_ref[...] = jnp.full_like(m_ref, NEG)
    s_ref[...] = jnp.zeros_like(s_ref)


def source_block(x_ref, s):
    return x_ref[s >> 1, :, columns(s & 1)]


def no_tail(index):
    return jnp.zeros((GROUP, BLK), jnp.bfloat16)


def target_by_source(entries, x_ref, yt_ref, hot_ref, tail=no_tail):
    accs = []
    for e in entries:
        source = jnp.minimum(source_of(e), 2 * x_ref.shape[0] - 1)
        parts = [source_block(x_ref, source), hot_ref[e & (GROUP - 1)], tail(source)]
        accs.append(dot(yt_ref[target_of(e) & 31], jnp.concatenate(parts, axis=0)))
    return accs


def source_by_target(entries, pack_ref, xt_ref, hot_ref, tail=no_tail):
    accs = []
    for e in entries:
        source, target = jnp.minimum(source_of(e), xt_ref.shape[0] - 1), target_of(e) & 31
        block = pack_ref[:LAT, columns(target)]
        parts = [block, hot_ref[source & (GROUP - 1)], tail(target)]
        accs.append(dot(xt_ref[source], jnp.concatenate(parts, axis=0)))
    return accs


def plain_sum(acc):
    return jnp.sum(jnp.exp2(acc * KAPPA).reshape(BLK // 8, 8, BLK), axis=0)


def total(s_ref):
    return jnp.sum(s_ref[: s_ref.shape[0] - 1], axis=1)


def transposed(block):
    return jnp.concatenate([block, jnp.zeros_like(block)], axis=0).T


def target_side_kernel(pack_ref, yt0_ref, minus_half_ref):
    for q in range(yt0_ref.shape[0]):
        block = pack_ref[:LAT, q * BLK : (q + 1) * BLK]
        yt0_ref[q] = transposed(block)
        minus_half_ref[q : q + 1, :] = -0.5 * jnp.sum(
            jnp.square(block.astype(jnp.float32)), axis=0, keepdims=True
        )


def spread_kernel(in_ref, out_ref):
    out_ref[...] = jnp.broadcast_to(in_ref[...][None], out_ref.shape)


def source_side_kernel(x_ref, xt0_ref):
    for q in range(xt0_ref.shape[0]):
        xt0_ref[q] = transposed(x_ref[q // 2, :, (q % 2) * BLK : (q % 2 + 1) * BLK])


def start_copy(from_ref, to_ref, sem):
    copy = pltpu.make_async_copy(from_ref, to_ref, sem)
    copy.start()
    return copy


def first_row_kernel(
    tiles_ref, b_ref, x_ref, yt0_ref, out_ref, list_ref, side_ref, sems, yt_ref, hot_ref, m_ref, s_ref
):
    copy = start_copy(tiles_ref, list_ref, sems.at[0])
    fill_hot(hot_ref)
    clear(m_ref, s_ref)
    fill_biased(yt0_ref, b_ref[...], yt_ref)
    copy.wait()

    def body(entries):
        stats = [partial_stats(a) for a in target_by_source(entries, x_ref, yt_ref, hot_ref)]
        for e, (m, s) in zip(entries, stats):
            fold_into(source_of(e), m, s, m_ref, s_ref)

    sweep(list_ref, body)
    n = m_ref.shape[0] - 1
    out_ref[...] = jnp.broadcast_to(finish(m_ref[:n], s_ref[:n])[None], out_ref.shape)


def first_col_kernel(
    tiles_ref, log_ref, xt0_ref, pack_ref, r_ref, out_ref, a_ref, next_ref, list_ref, side_ref, sems, xt_ref, hot_ref, m_ref, s_ref
):
    mass = start_copy(log_ref, side_ref.at[0], sems.at[1])
    copy = start_copy(tiles_ref, list_ref, sems.at[0])
    fill_hot(hot_ref)
    clear(m_ref, s_ref)
    level = join(r_ref[...])
    mass.wait()
    a = bias_of(side_ref[0], level)
    side_ref[1] = a
    side_ref[2] = a + 3.2 * side_ref[0]
    out_a = start_copy(side_ref.at[1], a_ref, sems.at[2])
    out_next = start_copy(side_ref.at[2], next_ref, sems.at[3])
    fill_biased(xt0_ref, a, xt_ref)
    copy.wait()

    def body(entries):
        stats = [partial_stats(a) for a in source_by_target(entries, pack_ref, xt_ref, hot_ref)]
        for e, (m, s) in zip(entries, stats):
            fold_into(target_of(e), m, s, m_ref, s_ref)

    sweep(list_ref, body)
    k = m_ref.shape[0] - 1
    out_ref[...] = jnp.broadcast_to(finish(m_ref[:k], s_ref[:k])[None], out_ref.shape)
    out_a.wait()
    out_next.wait()


def row_kernel(
    tiles_ref, log_ref, a_ref, x_ref, yt0_ref, c_ref, d_ref, out_ref, b_ref, next_ref, list_ref, side_ref, sems, yt_ref, hot_ref, tail_ref, s_ref
):
    mass = start_copy(log_ref, side_ref.at[0], sems.at[1])
    in_a = start_copy(a_ref, side_ref.at[3], sems.at[4])
    copy = start_copy(tiles_ref, list_ref, sems.at[0])
    fill_hot(hot_ref)
    s_ref[...] = jnp.zeros_like(s_ref)
    level = join_pair(c_ref[...], d_ref[...])
    mass.wait()
    b = bias_of(side_ref[0], level)
    side_ref[1] = b
    side_ref[2] = b + 3.2 * side_ref[0]
    out_b = start_copy(side_ref.at[1], b_ref, sems.at[2])
    out_next = start_copy(side_ref.at[2], next_ref, sems.at[3])
    fill_biased(yt0_ref, b, yt_ref)
    in_a.wait()
    fill_tails(side_ref[3], tail_ref)
    copy.wait()

    def body(entries):
        accs = target_by_source(entries, x_ref, yt_ref, hot_ref, lambda q: tail_ref[q])
        for e, s in zip(entries, [plain_sum(acc) for acc in accs]):
            s_ref[source_of(e)] += s

    sweep(list_ref, body)
    out_ref[...] = jnp.broadcast_to(total(s_ref)[None], out_ref.shape)
    out_b.wait()
    out_next.wait()


def col_kernel(
    tiles_ref, lifted_ref, b_ref, xt0_ref, pack_ref, r_ref, out_ref, a_ref, list_ref, side_ref, sems, xt_ref, hot_ref, tail_ref, s_ref
):
    lifted = start_copy(lifted_ref, side_ref.at[0], sems.at[1])
    in_b = start_copy(b_ref, side_ref.at[3], sems.at[4])
    copy = start_copy(tiles_ref, list_ref, sems.at[0])
    fill_hot(hot_ref)
    s_ref[...] = jnp.zeros_like(s_ref)
    drop = 3.2 * jnp.log(jnp.sum(r_ref[...], axis=0))
    lifted.wait()
    a = side_ref[0] - drop
    side_ref[1] = a
    out_a = start_copy(side_ref.at[1], a_ref, sems.at[2])
    fill_biased(xt0_ref, a, xt_ref)
    in_b.wait()
    fill_tails(side_ref[3], tail_ref)
    copy.wait()

    def body(entries):
        accs = source_by_target(entries, pack_ref, xt_ref, hot_ref, lambda q: tail_ref[q])
        for e, s in zip(entries, [plain_sum(acc) for acc in accs]):
            s_ref[target_of(e)] += s

    sweep(list_ref, body)
    out_ref[...] = jnp.broadcast_to(total(s_ref)[None], out_ref.shape)
    out_a.wait()


def project_kernel(
    tiles_ref, lifted_ref, a_ref, x_ref, yt0_ref, pack_ref, c_ref, d_ref, out_ref, b_ref, list_ref, side_ref, sems, yt_ref, hot_ref, tail_ref, w_ref
):
    lifted = start_copy(lifted_ref, side_ref.at[0], sems.at[1])
    in_a = start_copy(a_ref, side_ref.at[3], sems.at[4])
    copy = start_copy(tiles_ref, list_ref, sems.at[0])
    fill_hot(hot_ref)
    w_ref[...] = jnp.zeros_like(w_ref)
    drop = 3.2 * jnp.log(c_ref[...] + d_ref[...])
    lifted.wait()
    b = side_ref[0] - drop
    side_ref[1] = b
    out_b = start_copy(side_ref.at[1], b_ref, sems.at[2])
    fill_biased(yt0_ref, b, yt_ref)
    in_a.wait()
    fill_tails(side_ref[3], tail_ref)
    copy.wait()

    def body(entries):
        weighted = []
        accs = target_by_source(entries, x_ref, yt_ref, hot_ref, lambda q: tail_ref[q])
        for e, acc in zip(entries, accs):
            p = jnp.exp2(acc * KAPPA)
            hi = p.astype(jnp.bfloat16)
            low = (p - hi.astype(jnp.float32)).astype(jnp.bfloat16)
            side = pack_ref[LAT:, columns(target_of(e) & 31)]
            both = jnp.concatenate([hi, low], axis=0)
            weighted.append(dot(jnp.concatenate([side, side], axis=1), both)[:8])
        for e, w in zip(entries, weighted):
            w_ref[source_of(e)] += w

    sweep(list_ref, body)
    out_ref[...] = jnp.zeros_like(out_ref)
    for ib in range(2 * x_ref.shape[0]):
        w = w_ref[ib]
        for place, row in enumerate((2, 0, 1)):
            first = 2 * place + ib % 2
            out_ref[ib // 2, first : first + 1, :] = w[row : row + 1]
    out_b.wait()


VMEM = pl.BlockSpec(memory_space=pltpu.VMEM)
HBM = pl.BlockSpec(memory_space=pltpu.HBM)


def call(kernel, outs, scratch, far, near, far_outs=0):
    put = pltpu.with_memory_space_constraint
    return pl.pallas_call(
        kernel,
        out_shape=outs,
        in_specs=[HBM] * len(far) + [VMEM] * len(near),
        out_specs=[VMEM] * (len(outs) - far_outs) + [HBM] * far_outs,
        scratch_shapes=scratch,
        compiler_params=pltpu.CompilerParams(vmem_limit_bytes=16 << 20),
    )(*(put(a, pltpu.HBM) for a in far), *(put(a, pltpu.VMEM) for a in near))


def tile_list(support, chip, per_chip, slots):
    rows, per_list = support.shape
    owned = support // per_chip == chip
    flags = owned.astype(jnp.float32)
    upto = (jnp.arange(per_list)[:, None] <= jnp.arange(per_list)[None, :]).astype(jnp.float32)
    before = (jnp.arange(rows)[None, :] < jnp.arange(rows)[:, None]).astype(jnp.float32)
    within = flags @ upto
    start = before @ within[:, -1:]
    place = jnp.where(owned, (within + start).astype(jnp.int32) - 1, -1)
    count = jnp.sum(owned.astype(jnp.int32))
    code = jnp.arange(rows, dtype=jnp.int32)[:, None] * 64 + support % per_chip
    slot = jnp.arange(slots, dtype=jnp.int32)
    listed = jnp.sum(
        jnp.where(place[:, :, None] == slot, code[:, :, None], 0), axis=(0, 1), dtype=jnp.int32
    )
    listed = jnp.where(slot < count, listed, rows * 64 + per_chip)
    return jnp.concatenate([listed, jnp.broadcast_to(count, (BLK,))]).reshape(-1, BLK)


def on_device(
    source_latent, target_latent, log_source_mass, log_target_mass, target_coords, support
):
    rows, cols = lax.axis_size("row"), lax.axis_size("col")
    here = lax.axis_index("col")
    chip, core = here // 2, here % 2
    chips = cols // 2
    mine = support.shape[0] // cols
    own_k = target_latent.shape[1] // BLK
    n, k = chips * mine, 2 * own_k
    bf16, f32 = jnp.bfloat16, jnp.float32
    by_chip = chip_groups(cols)

    def of_core(a):
        split = a.reshape((chips, 2, mine) + a.shape[1:])
        split = jnp.where(core == 0, split[:, 0], split[:, 1])
        return split.reshape((n,) + a.shape[1:])

    spread = pl.pallas_call(
        spread_kernel,
        out_shape=jax.ShapeDtypeStruct((chips,) + source_latent.shape, bf16),
        in_specs=[VMEM],
        out_specs=VMEM,
    )(source_latent)
    spread, support = lax.optimization_barrier((spread, support))
    x = exchange(spread, "col", by_chip)
    tiles = tile_list(of_core(support), chip, k, 12 * mine * chips)
    tiles, target_latent, target_coords, log_target_mass = lax.optimization_barrier(
        (tiles, target_latent, target_coords, log_target_mass)
    )

    def pair(a):
        other = swap_cores(a, cols)
        return jnp.concatenate(
            [jnp.where(core == 0, a, other), jnp.where(core == 0, other, a)], axis=1
        )

    width = 2 * target_latent.shape[1]
    targets = pair(target_latent)
    coords, target_log = pair(target_coords), pair(log_target_mass[None])
    pack = jnp.concatenate(
        [targets, coords, jnp.ones((1, width), bf16), jnp.zeros((PACK - LAT - 3, width), bf16)],
        axis=0,
    )
    target_log = target_log.astype(f32).reshape(k, BLK)
    source_log = of_core(log_source_mass.reshape(-1, BLK))

    common = [
        pltpu.SMEM(tiles.shape, jnp.int32),
        pltpu.VMEM((4, n, BLK), f32),
        pltpu.SemaphoreType.DMA((5,)),
        pltpu.VMEM((n, BLK, BLK), bf16),
        pltpu.VMEM((GROUP, 3 * GROUP, BLK), bf16),
    ]
    sums = pltpu.VMEM((n + 1, 8, BLK), f32)
    first_scratch = common + [sums, sums]
    scratch = common + [pltpu.VMEM((n, GROUP, BLK), bf16), sums]

    tiles, source_log, target_log = lax.optimization_barrier((tiles, source_log, target_log))
    turned = pltpu.VMEM((n, BLK, BLK), bf16)
    yt0, minus_half = call(
        target_side_kernel, [turned, pltpu.VMEM((k, BLK), f32)], [], [], [pack]
    )
    small = pltpu.HBM((n, BLK), f32)
    to_chips = jax.ShapeDtypeStruct((chips, n, BLK), f32)
    to_rows = jax.ShapeDtypeStruct((rows, k, BLK), f32)
    to_owners = jax.ShapeDtypeStruct((chips, 8, BLK), f32)

    (r,) = call(first_row_kernel, [to_chips], first_scratch, [tiles], [minus_half, x, yt0])
    (xt0,) = call(source_side_kernel, [turned], [], [], [x])
    r = exchange(r, "col", by_chip)
    c, a, lifted = call(
        first_col_kernel,
        [to_rows, small, small],
        first_scratch,
        [tiles, source_log],
        [xt0, pack, r],
        2,
    )
    c = join(exchange(c, "row"))
    d = swap_cores(c, cols)
    r, b, target_lifted = call(
        row_kernel, [to_chips, small, small], scratch, [tiles, target_log, a], [x, yt0, c, d], 2
    )
    r = exchange(r, "col", by_chip)
    c, a = call(
        col_kernel, [to_rows, small], scratch, [tiles, lifted, b], [xt0, pack, r], 1
    )
    c = jnp.sum(exchange(c, "row"), axis=0)
    d = swap_cores(c, cols)
    part, b = call(
        project_kernel,
        [to_owners, small],
        scratch,
        [tiles, target_lifted, a],
        [x, yt0, pack, c, d],
        1,
    )
    part, a, b, source_latent = lax.optimization_barrier((part, a, b, source_latent))
    part = jnp.sum(exchange(part, "col", by_chip), axis=0)
    mapped = part[mine : 3 * mine].reshape(2, mine, BLK) / part[:mine]
    mapped = mapped.reshape(2, mine * BLK)

    own_a = lax.dynamic_slice_in_dim(a, chip * mine, mine).reshape(-1)
    x_half = 0.5 * jnp.sum(jnp.square(source_latent.astype(f32)), axis=0)
    out_source = (own_a + x_half) / 32.0
    out_target = lax.dynamic_slice_in_dim((b - minus_half) / 32.0, core * own_k, own_k).reshape(-1)
    return out_source, out_target, mapped


def solution(mesh):
    in_specs = (
        P(None, ("row", "col")),
        P(None, "col"),
        P("row"),
        P("col"),
        P(None, "col"),
        P("row", None),
    )
    out_specs = (P(("row", "col")), P("col"), P(None, ("row", "col")))
    return jax.shard_map(
        on_device, mesh=mesh, in_specs=in_specs, out_specs=out_specs, check_vma=False
    )
```

time: 110 us -> 106 us (0.964); the launches traced: 109 us -> 107 us
  waiting for transfers between devices: 18.9 us -> 16.1 us
  blocking collectives: 38 us -> 39.4 us
    all_to_all x3, waiting for transfers between devices: 17.2 us -> 14.4 us  [exchange(): return lax.all_to_all(x, axis, 0, 0, axis_index_groups=groups)]
    ppermute x5, starting transfers between devices: 10.7 us -> 8.69 us  [swap_cores(): return lax.ppermute(x, 'col', [(i, i ^ 1) for i in range(cols)])]
    all_to_all x3, starting transfers between devices: 15.8 us -> 17.6 us  [exchange(): return lax.all_to_all(x, axis, 0, 0, axis_index_groups=groups)]
    all_to_all x3, blocking collectives: 38 us -> 39.4 us  [exchange(): return lax.all_to_all(x, axis, 0, 0, axis_index_groups=groups)]
  transfers between devices with their start and end apart: 8 -> 8, of which waited for: 5 -> 5; matrix products, arithmetic and copies ran while one was open for 7% -> 7% of each run, Pallas kernels for 2% -> 1%
where the time goes in v2:
time: 106 us; the launch traced here: 107 us
  blocking collectives  39.4 us (37%)
  starting transfers between devices  26.3 us (25%)
  waiting for transfers between devices  16.1 us (15%)
  Pallas kernels  15.9 us (15%)
  other arithmetic  6.53 us (6%)
  local copies, waits for them, and re-layouts  1.73 us (2%)
    all_to_all x3, blocking collectives, exchange(): return lax.all_to_all(x, axis, 0, 0, axis_index_groups=groups)  39.4 us
    all_to_all x3, starting transfers between devices, exchange(): return lax.all_to_all(x, axis, 0, 0, axis_index_groups=groups)  17.6 us
    all_to_all x3, waiting for transfers between devices, exchange(): return lax.all_to_all(x, axis, 0, 0, axis_index_groups=groups)  14.4 us
    pallas_call x7, Pallas kernels, call(): pl.pallas_call(kernel, out_shape=outs, in_specs=[HBM] * len(far) + [VMEM]...  14.2 us
    ppermute x5, starting transfers between devices, swap_cores(): return lax.ppermute(x, 'col', [(i, i ^ 1) for i in range(cols)])  8.69 us
  transfers between devices with their start and end apart: 8, of which 5 were waited for; matrix products, arithmetic and copies ran while one was open for 7% of the time, Pallas kernels for 1%

profile of v2, /device:TPU:1, one launch (start us, length us, event | category | flops | bytes accessed | tf_op | source)
XLA Modules:
  0.0 107.2 jit_solution(7248539977662025222)
XLA Ops:
  0.6 0.0 copy-start.3
  0.6 0.0 copy-start.5
  0.7 0.0 copy-start.4
  0.7 0.0 copy-start
  0.7 0.0 copy-start.2
  0.7 1.6 %shard_map.85 = bf16[16,64,256]{2,1,0:T(8,128)(2,1)} custom-call(bf16[64,256]{1,0:T(8,128)(2,1)} %in_ref.1), custom_call_target="tpu_custom_call" | custom-call | tf_op jit(solution)/shard_map/pallas_call | solution.py:403
  2.3 7.6 %all-to-all-start = ((bf16[16,64,256]{2,1,0:T(8,128)(2,1)}), bf16[16,64,256]{2,1,0:T(8,128)(2,1)S(1)}, u32[]{:S(2)}, u32[]{:S(2)}) async-start(bf16[16,64,256]{2,1,0:T(8,128)(2,1)} %shard_map.85), calls=%async_computation | async-start | bytes 1048576 | tf_op jit(solution)/shard_map/all_to_all | solution.py:30
  10.0 0.0 copy-done.3
  10.0 0.1 copy.20
  10.0 0.7 fusion.2
  10.7 0.1 copy.21
  10.8 0.2 fusion.4
  11.0 0.1 copy.26
  11.1 0.1 convolution_bitcast_fusion
  11.3 0.1 copy.25
  11.3 0.4 select_reduce_fusion
  11.7 0.7 fusion.8
  12.3 1.2 %pad_bitcast_fusion.tiles_ref = s32[4,128]{1,0:T(4,128)} fusion(s32[384]{0:T(512)S(1)} %fusion.8, s32[]{:T(128)} %get-tuple-element.53), kind=kLoop, calls=%fused_computation.39 | loop fusion | bytes 3588 | tf_op jit(solution)/shard_map/reshape | solution.py:382
  13.6 0.0 copy-done.4
  13.6 1.0 collective-permute-start
  14.6 0.0 copy-done.5
  14.6 0.1 collective-permute-start.2
  14.7 0.0 copy-done
  14.7 0.4 collective-permute-start.1
  15.1 0.0 copy-done.2
  15.1 0.6 slice_select_fusion
  15.8 0.1 pad.5.clone
  15.8 0.1 pad.6.clone
  15.9 0.0 collective-permute-done
  15.9 0.6 maximum_convert_fusion
  16.6 0.0 collective-permute-done.2
  16.6 0.0 collective-permute-done.1
  16.6 0.1 broadcast_select_fusion.1
  16.7 0.2 maximum_maximum_fusion.pack_ref
  16.9 0.3 shard_map.87
  17.2 3.2 %all-to-all-done.x_ref = bf16[16,64,256]{2,1,0:T(8,128)(2,1)S(1)} async-done(((bf16[16,64,256]{2,1,0:T(8,128)(2,1)}), bf16[16,64,256]{2,1,0:T(8,128)(2,1)S(1)}, u32[]{:S(2)}, u32[]{:S(2)}) %all-to-all-start) | async-done | bytes 524320 | tf_op jit(solution)/shard_map/all_to_all | solution.py:30
  20.4 3.1 %shard_map.88 = f32[16,32,128]{2,1,0:T(8,128)} custom-call(s32[4,128]{1,0:T(4,128)} %pad_bitcast_fusion.tiles_ref, f32[32,128]{1,0:T(8,128)S(1)} %get-tuple-element.37.b_ref, bf16[16,64,256]{2,1,0:T(8,128)(2,1)S(1)} %all-to-all-done.x_ref, bf16[32,128,128]{2,1,0:T(8,128)(2,1)S(1)} %get-tuple-element.38.yt0_ref), custom_call_target="tpu_custom_call" | custom-call | tf_op jit(solution)/shard_map/pallas_call | solution.py:356
  23.5 4.7 %all-to-all-start.1 = ((f32[16,32,128]{2,1,0:T(8,128)}), f32[16,32,128]{2,1,0:T(8,128)S(1)}, u32[]{:S(2)}, u32[]{:S(2)}) async-start(f32[16,32,128]{2,1,0:T(8,128)} %shard_map.88), calls=%async_computation.1 | async-start | bytes 524288 | tf_op jit(solution)/shard_map/all_to_all | solution.py:30
  28.2 0.3 shard_map.86.xt0_ref
  28.6 7.2 %all-to-all-done.1.r_ref = f32[16,32,128]{2,1,0:T(8,128)S(1)} async-done(((f32[16,32,128]{2,1,0:T(8,128)}), f32[16,32,128]{2,1,0:T(8,128)S(1)}, u32[]{:S(2)}, u32[]{:S(2)}) %all-to-all-start.1) | async-done | bytes 262176 | tf_op jit(solution)/shard_map/all_to_all | solution.py:30
  35.8 2.4 %shard_map.89 = (f32[8,32,128]{2,1,0:T(8,128)S(1)}, f32[32,128]{1,0:T(8,128)}, f32[32,128]{1,0:T(8,128)}) custom-call(s32[4,128]{1,0:T(4,128)} %pad_bitcast_fusion.tiles_ref, f32[32,128]{1,0:T(8,128)} %bitcast.21, bf16[32,128,128]{2,1,0:T(8,128)(2,1)S(1)} %shard_map.86.xt0_ref, bf16[80,4096]{1,0:T(8,128)(2,1)S(1)} %maximum_maximum_fusion.pack_ref, ...), custom_call_target="tpu_custom_call" | custom-call | tf_op jit(solution)/shard_map/pallas_call | solution.py:356
  38.2 16.0 %all_to_all.30 = f32[8,32,128]{2,1,0:T(8,128)S(1)} all-to-all(f32[8,32,128]{2,1,0:T(8,128)S(1)} %get-tuple-element.40), channel_id=1, replica_groups=mesh['row'=8,'col'=32] {'row'}, dimensions={0} | all-to-all | bytes 262144 | tf_op jit(solution)/shard_map/all_to_all | solution.py:30
  54.3 4.6 %collective-permute-start.3 = (f32[32,128]{1,0:T(8,128)S(1)}, f32[32,128]{1,0:T(8,128)S(1)}, u32[]{:S(2)}, u32[]{:S(2)}) collective-permute-start(f32[32,128]{1,0:T(8,128)S(1)} %multiply_add_fusion.c_ref), channel_id=1, source_target_pairs={{0,1},{1,0},{2,3},{3,2},{4,5},{5,4},{6,7},{7,6},{8,9},{9,8},{10,11... | collective-permute-start | bytes 49160 | tf_op jit(solution)/shard_map/ppermute | solution.py:26
  58.9 0.8 collective-permute-done.3.d_ref
  59.7 2.2 %shard_map.90 = (f32[16,32,128]{2,1,0:T(8,128)S(1)}, f32[32,128]{1,0:T(8,128)}, f32[32,128]{1,0:T(8,128)}) custom-call(s32[4,128]{1,0:T(4,128)} %pad_bitcast_fusion.tiles_ref, f32[32,128]{1,0:T(8,128)} %bitcast.22, f32[32,128]{1,0:T(8,128)} %get-tuple-element.39.a_ref, bf16[16,64,256]{2,1,0:T(8,128)(2,1)S(1)} %all-to-all-done.x_ref, ...), custom_call_target="tpu_custom_call" | custom-call | tf_op jit(solution)/shard_map/pallas_call | solution.py:356
  61.9 13.0 %all_to_all.31.r_ref = f32[16,32,128]{2,1,0:T(8,128)S(1)} all-to-all(f32[16,32,128]{2,1,0:T(8,128)S(1)} %get-tuple-element.44), channel_id=1, replica_groups={{0,2,4,6,8,10,12,14,16,18,20,22,24,26,28,30},{1,3,5,7,9,11,13,15,17,19,..., dimensions={0} | all-to-all | bytes 524288 | tf_op jit(solution)/shard_map/all_to_all | solution.py:30
  75.0 2.4 %shard_map.91 = (f32[8,32,128]{2,1,0:T(8,128)S(1)}, f32[32,128]{1,0:T(8,128)}) custom-call(s32[4,128]{1,0:T(4,128)} %pad_bitcast_fusion.tiles_ref, f32[32,128]{1,0:T(8,128)} %get-tuple-element.42.lifted_ref, f32[32,128]{1,0:T(8,128)} %get-tuple-element.43.b_ref, bf16[32,128,128]{2,1,0:T(8,128)(2,1)S(1)} %shard_map.86.xt0_ref, ...), custom_call_target="tpu_custom_call" | custom-call | tf_op jit(solution)/shard_map/pallas_call | solution.py:356
  77.3 10.4 %all_to_all.32 = f32[8,32,128]{2,1,0:T(8,128)S(1)} all-to-all(f32[8,32,128]{2,1,0:T(8,128)S(1)} %get-tuple-element.46), channel_id=1, replica_groups=mesh['row'=8,'col'=32] {'row'}, dimensions={0} | all-to-all | bytes 262144 | tf_op jit(solution)/shard_map/all_to_all | solution.py:30
  87.8 2.6 %collective-permute-start.4 = (f32[32,128]{1,0:T(8,128)S(1)}, f32[32,128]{1,0:T(8,128)S(1)}, u32[]{:S(2)}, u32[]{:S(2)}) collective-permute-start(f32[32,128]{1,0:T(8,128)S(1)} %reduce_sum.57.c_ref), channel_id=1, source_target_pairs={{0,1},{1,0},{2,3},{3,2},{4,5},{5,4},{6,7},{7,6},{8,9},{9,8},{10,11... | collective-permute-start | bytes 49160 | tf_op jit(solution)/shard_map/ppermute | solution.py:26
  90.3 0.8 collective-permute-done.4.d_ref
  91.2 0.0 copy-start.1
  91.2 3.4 %shard_map.92 = (f32[16,8,128]{2,1,0:T(8,128)}, f32[32,128]{1,0:T(8,128)}) custom-call(s32[4,128]{1,0:T(4,128)} %pad_bitcast_fusion.tiles_ref, f32[32,128]{1,0:T(8,128)} %get-tuple-element.41.lifted_ref, f32[32,128]{1,0:T(8,128)} %get-tuple-element.49.a_ref, bf16[16,64,256]{2,1,0:T(8,128)(2,1)S(1)} %all-to-all-done.x_ref, ...), custom_call_target="tpu_custom_call" | custom-call | tf_op jit(solution)/shard_map/pallas_call | solution.py:356
  94.6 0.0 copy-done.1
  94.7 5.3 %all-to-all-start.5 = ((f32[16,8,128]{2,1,0:T(8,128)}), f32[16,8,128]{2,1,0:T(8,128)S(1)}, u32[]{:S(2)}, u32[]{:S(2)}) async-start(f32[16,8,128]{2,1,0:T(8,128)} %get-tuple-element.52), calls=%async_computation.5 | async-start | bytes 131072 | tf_op jit(solution)/shard_map/all_to_all | solution.py:30
  100.0 1.3 %fusion.9 = f32[256]{0:T(256)} fusion(f32[256]{0:T(256)S(1)} %multiply_reduce_fusion, f32[32,128]{1,0:T(8,128)} %get-tuple-element.49.a_ref, s32[]{:T(128)S(6)} %select_n.135), kind=kLoop, calls=%fused_computation.43 | loop fusion | flops 768 | bytes 3076 | tf_op jit(solution)/shard_map/div | solution.py:490
  101.3 1.3 %fusion.7 = f32[2048]{0:T(1024)} fusion(f32[32,128]{1,0:T(8,128)S(1)} %get-tuple-element.37.b_ref, s32[]{:T(128)S(6)} %select_n.136, f32[32,128]{1,0:T(8,128)} %get-tuple-element.51), kind=kLoop, calls=%fused_computation.38 | loop fusion | flops 4096 | bytes 24580 | tf_op jit(solution)/shard_map/reshape | solution.py:491
  102.6 4.0 %all-to-all-done.5 = f32[16,8,128]{2,1,0:T(8,128)S(1)} async-done(((f32[16,8,128]{2,1,0:T(8,128)}), f32[16,8,128]{2,1,0:T(8,128)S(1)}, u32[]{:S(2)}, u32[]{:S(2)}) %all-to-all-start.5) | async-done | bytes 65568 | tf_op jit(solution)/shard_map/all_to_all | solution.py:30
  106.6 0.6 broadcast_divide_fusion
  (16 shorter events, 0.2 us)
Async XLA Ops:
  0.6 9.3 %copy-start.3 = (s32[64,32]{0,1:T(8,128)S(1)}, s32[64,32]{0,1:T(8,128)}, u32[]{:S(2)}) copy-start(s32[64,32]{0,1:T(8,128)} %param.11) | copy-start | bytes 24580
  0.6 14.0 %copy-start.5 = (bf16[2,2048]{1,0:T(2,128)(2,1)S(1)}, bf16[2,2048]{1,0:T(2,128)(2,1)}, u32[]{:S(2)}) copy-start(bf16[2,2048]{1,0:T(2,128)(2,1)} %param.10) | copy-start | bytes 24580
  0.7 12.9 %copy-start.4 = (bf16[2048]{0:T(1024)(128)(2,1)S(1)}, bf16[2048]{0:T(1024)(128)(2,1)}, u32[]{:S(2)}) copy-start(bf16[2048]{0:T(1024)(128)(2,1)} %param.9) | copy-start | bytes 12292
  0.7 14.1 %copy-start = (bf16[64,2048]{1,0:T(8,128)(2,1)S(1)}, bf16[64,2048]{1,0:T(8,128)(2,1)}, u32[]{:S(2)}) copy-start(bf16[64,2048]{1,0:T(8,128)(2,1)} %param.7) | copy-start | bytes 786436
  0.7 14.5 %copy-start.2 = (f32[8192]{0:T(1024)S(1)}, f32[8192]{0:T(1024)}, u32[]{:S(2)}) copy-start(f32[8192]{0:T(1024)} %param.8) | copy-start | bytes 98308
  2.3 18.1 %all-to-all-start = ((bf16[16,64,256]{2,1,0:T(8,128)(2,1)}), bf16[16,64,256]{2,1,0:T(8,128)(2,1)S(1)}, u32[]{:S(2)}, u32[]{:S(2)}) async-start(bf16[16,64,256]{2,1,0:T(8,128)(2,1)} %shard_map.85), calls=%async_computation | async-start | bytes 1048576 | tf_op jit(solution)/shard_map/all_to_all | solution.py:30
  13.6 2.3 %collective-permute-start = (bf16[1,2048]{1,0:T(2,128)(2,1)S(1)}, bf16[1,2048]{1,0:T(2,128)(2,1)S(1)}, u32[]{:S(2)}, u32[]{:S(2)}) collective-permute-start(bf16[1,2048]{1,0:T(2,128)(2,1)S(1)} %broadcast_in_dim.41), channel_id=1, source_target_pairs={{0,1},{1,0},{2,3},{3,2},{4,5},{5,4},{6,7},{7,6},{8,9},{9,8},{10,11... | collective-permute-start | bytes 12296 | tf_op jit(solution)/shard_map/ppermute | solution.py:26
  14.6 1.9 %collective-permute-start.2 = (bf16[2,2048]{1,0:T(2,128)(2,1)S(1)}, bf16[2,2048]{1,0:T(2,128)(2,1)S(1)}, u32[]{:S(2)}, u32[]{:S(2)}) collective-permute-start(bf16[2,2048]{1,0:T(2,128)(2,1)S(1)} %copy-done.5), channel_id=1, source_target_pairs={{0,1},{1,0},{2,3},{3,2},{4,5},{5,4},{6,7},{7,6},{8,9},{9,8},{10,11... | collective-permute-start | bytes 24584 | tf_op jit(solution)/shard_map/ppermute | solution.py:26
  14.7 1.8 %collective-permute-start.1 = (bf16[64,2048]{1,0:T(8,128)(2,1)S(1)}, bf16[64,2048]{1,0:T(8,128)(2,1)S(1)}, u32[]{:S(2)}, u32[]{:S(2)}) collective-permute-start(bf16[64,2048]{1,0:T(8,128)(2,1)S(1)} %copy-done), channel_id=1, source_target_pairs={{0,1},{1,0},{2,3},{3,2},{4,5},{5,4},{6,7},{7,6},{8,9},{9,8},{10,11... | collective-permute-start | bytes 786440 | tf_op jit(solution)/shard_map/ppermute | solution.py:26
  23.5 12.3 %all-to-all-start.1 = ((f32[16,32,128]{2,1,0:T(8,128)}), f32[16,32,128]{2,1,0:T(8,128)S(1)}, u32[]{:S(2)}, u32[]{:S(2)}) async-start(f32[16,32,128]{2,1,0:T(8,128)} %shard_map.88), calls=%async_computation.1 | async-start | bytes 524288 | tf_op jit(solution)/shard_map/all_to_all | solution.py:30
  54.3 5.4 %collective-permute-start.3 = (f32[32,128]{1,0:T(8,128)S(1)}, f32[32,128]{1,0:T(8,128)S(1)}, u32[]{:S(2)}, u32[]{:S(2)}) collective-permute-start(f32[32,128]{1,0:T(8,128)S(1)} %multiply_add_fusion.c_ref), channel_id=1, source_target_pairs={{0,1},{1,0},{2,3},{3,2},{4,5},{5,4},{6,7},{7,6},{8,9},{9,8},{10,11... | collective-permute-start | bytes 49160 | tf_op jit(solution)/shard_map/ppermute | solution.py:26
  87.8 3.4 %collective-permute-start.4 = (f32[32,128]{1,0:T(8,128)S(1)}, f32[32,128]{1,0:T(8,128)S(1)}, u32[]{:S(2)}, u32[]{:S(2)}) collective-permute-start(f32[32,128]{1,0:T(8,128)S(1)} %reduce_sum.57.c_ref), channel_id=1, source_target_pairs={{0,1},{1,0},{2,3},{3,2},{4,5},{5,4},{6,7},{7,6},{8,9},{9,8},{10,11... | collective-permute-start | bytes 49160 | tf_op jit(solution)/shard_map/ppermute | solution.py:26
  91.2 3.5 %copy-start.1 = (bf16[64,256]{1,0:T(8,128)(2,1)S(1)}, bf16[64,256]{1,0:T(8,128)(2,1)}, u32[]{:S(2)}) copy-start(bf16[64,256]{1,0:T(8,128)(2,1)} %in_ref.1) | copy-start | bytes 98308
  94.7 11.9 %all-to-all-start.5 = ((f32[16,8,128]{2,1,0:T(8,128)}), f32[16,8,128]{2,1,0:T(8,128)S(1)}, u32[]{:S(2)}, u32[]{:S(2)}) async-start(f32[16,8,128]{2,1,0:T(8,128)} %get-tuple-element.52), calls=%async_computation.5 | async-start | bytes 131072 | tf_op jit(solution)/shard_map/all_to_all | solution.py:30

commit v3 on v2

--- a/solution.py
+++ b/solution.py
@@ -12,10 +12,10 @@
 NEG = -1e30
 LN2 = 0.6931471805599453
 KAPPA = 0.3125 / LN2
-LONG_TURN = 64
-SHORT_TURN = 32
+TURNS = (64, 32, 16)
 PACK = 80
 GROUP = 16
+PAD = 32 * 64 + 32
 
 
 def chip_groups(cols):
@@ -36,11 +36,13 @@
 
 
 def join_pair(a, b):
-    return jnp.maximum(a, b) + jnp.log2(1.0 + jnp.exp2(-jnp.abs(a - b)))
-
-
-def bias_of(mass, level):
-    return 3.2 * (mass - LN2 * level)
+    top = jnp.maximum(jnp.max(a, axis=0), jnp.max(b, axis=0))
+    total = jnp.sum(jnp.exp2(a - top[None]), axis=0) + jnp.sum(jnp.exp2(b - top[None]), axis=0)
+    return top + jnp.log2(total)
+
+
+def bias_of(level):
+    return -3.2 * LN2 * level
 
 
 def pieces(a):
@@ -85,23 +87,19 @@
 
 def sweep(list_ref, body):
     count = list_ref[list_ref.shape[0] - 1, 0]
-    long_turns = count // LONG_TURN
-    left = count - long_turns * LONG_TURN
-
-    def turn(first, size):
-        row, start = first // BLK, first % BLK
-        body([list_ref[row, start + u] for u in range(size)])
-
-    def long_turn(g, c):
-        turn(g * LONG_TURN, LONG_TURN)
-        return c
-
-    def short_turn(g, c):
-        turn(long_turns * LONG_TURN + g * SHORT_TURN, SHORT_TURN)
-        return c
-
-    lax.fori_loop(0, long_turns, long_turn, 0)
-    lax.fori_loop(0, (left + (SHORT_TURN - 1)) // SHORT_TURN, short_turn, 0)
+    done = 0
+    for size in TURNS:
+        left = jnp.maximum(count - done, 0)
+        turns = (left + (size // 2 if size > TURNS[-1] else size - 1)) // size
+
+        def turn(g, c, size=size, done=done):
+            first = done + g * size
+            row, start = first // BLK, first % BLK
+            body([list_ref[row, start + u] + PAD for u in range(size)])
+            return c
+
+        lax.fori_loop(0, turns, turn, 0)
+        done = done + turns * size
 
 
 def source_of(e):
@@ -167,15 +165,22 @@
     return jnp.sum(jnp.exp2(acc * KAPPA).reshape(BLK // 8, 8, BLK), axis=0)
 
 
-def total(s_ref):
-    return jnp.sum(s_ref[: s_ref.shape[0] - 1], axis=1)
+def finish_plain(s_ref, bias):
+    total = jnp.sum(s_ref[: s_ref.shape[0] - 1], axis=1)
+    live = total > 0.0
+    return jnp.where(live, jnp.log2(jnp.where(live, total, 1.0)), NEG) - KAPPA * bias
+
+
+def put_level(level, mass, out_ref):
+    out_ref[...] = jnp.broadcast_to((level - mass * (1.0 / LN2))[None], out_ref.shape)
 
 
 def transposed(block):
     return jnp.concatenate([block, jnp.zeros_like(block)], axis=0).T
 
 
-def target_side_kernel(pack_ref, yt0_ref, minus_half_ref):
+def target_side_kernel(pack_ref, yt0_ref, minus_half_ref, hot_ref):
+    fill_hot(hot_ref)
     for q in range(yt0_ref.shape[0]):
         block = pack_ref[:LAT, q * BLK : (q + 1) * BLK]
         yt0_ref[q] = transposed(block)
@@ -188,11 +193,6 @@
     out_ref[...] = jnp.broadcast_to(in_ref[...][None], out_ref.shape)
 
 
-def source_side_kernel(x_ref, xt0_ref):
-    for q in range(xt0_ref.shape[0]):
-        xt0_ref[q] = transposed(x_ref[q // 2, :, (q % 2) * BLK : (q % 2 + 1) * BLK])
-
-
 def start_copy(from_ref, to_ref, sem):
     copy = pltpu.make_async_copy(from_ref, to_ref, sem)
     copy.start()
@@ -200,12 +200,14 @@
 
 
 def first_row_kernel(
-    tiles_ref, b_ref, x_ref, yt0_ref, out_ref, list_ref, side_ref, sems, yt_ref, hot_ref, m_ref, s_ref
+    tiles_ref, log_ref, b_ref, hot_ref, x_ref, yt0_ref, out_ref, xt0_ref, list_ref, side_ref, sems, yt_ref, m_ref, s_ref
 ):
     copy = start_copy(tiles_ref, list_ref, sems.at[0])
-    fill_hot(hot_ref)
+    mass = start_copy(log_ref, side_ref.at[0], sems.at[1])
     clear(m_ref, s_ref)
     fill_biased(yt0_ref, b_ref[...], yt_ref)
+    for q in range(xt0_ref.shape[0]):
+        xt0_ref[q] = transposed(x_ref[q // 2, :, (q % 2) * BLK : (q % 2 + 1) * BLK])
     copy.wait()
 
     def body(entries):
@@ -215,24 +217,21 @@
 
     sweep(list_ref, body)
     n = m_ref.shape[0] - 1
-    out_ref[...] = jnp.broadcast_to(finish(m_ref[:n], s_ref[:n])[None], out_ref.shape)
+    mass.wait()
+    put_level(finish(m_ref[:n], s_ref[:n]), side_ref[0], out_ref)
 
 
 def first_col_kernel(
-    tiles_ref, log_ref, xt0_ref, pack_ref, r_ref, out_ref, a_ref, next_ref, list_ref, side_ref, sems, xt_ref, hot_ref, m_ref, s_ref
+    tiles_ref, log_ref, hot_ref, xt0_ref, pack_ref, r_ref, out_ref, tail_out_ref, a_ref, list_ref, side_ref, sems, xt_ref, m_ref, s_ref
 ):
+    copy = start_copy(tiles_ref, list_ref, sems.at[0])
     mass = start_copy(log_ref, side_ref.at[0], sems.at[1])
-    copy = start_copy(tiles_ref, list_ref, sems.at[0])
-    fill_hot(hot_ref)
+    a = bias_of(join(r_ref[...]))
+    side_ref[1] = a
+    out_a = start_copy(side_ref.at[1], a_ref, sems.at[2])
     clear(m_ref, s_ref)
-    level = join(r_ref[...])
-    mass.wait()
-    a = bias_of(side_ref[0], level)
-    side_ref[1] = a
-    side_ref[2] = a + 3.2 * side_ref[0]
-    out_a = start_copy(side_ref.at[1], a_ref, sems.at[2])
-    out_next = start_copy(side_ref.at[2], next_ref, sems.at[3])
     fill_biased(xt0_ref, a, xt_ref)
+    fill_tails(a, tail_out_ref)
     copy.wait()
 
     def body(entries):
@@ -242,29 +241,23 @@
 
     sweep(list_ref, body)
     k = m_ref.shape[0] - 1
-    out_ref[...] = jnp.broadcast_to(finish(m_ref[:k], s_ref[:k])[None], out_ref.shape)
+    mass.wait()
+    put_level(finish(m_ref[:k], s_ref[:k]), side_ref[0], out_ref)
     out_a.wait()
-    out_next.wait()
 
 
 def row_kernel(
-    tiles_ref, log_ref, a_ref, x_ref, yt0_ref, c_ref, d_ref, out_ref, b_ref, next_ref, list_ref, side_ref, sems, yt_ref, hot_ref, tail_ref, s_ref
+    tiles_ref, log_ref, a_ref, hot_ref, tail_ref, x_ref, yt0_ref, c_ref, d_ref, out_ref, tail_out_ref, b_ref, list_ref, side_ref, sems, yt_ref, s_ref
 ):
+    copy = start_copy(tiles_ref, list_ref, sems.at[0])
     mass = start_copy(log_ref, side_ref.at[0], sems.at[1])
-    in_a = start_copy(a_ref, side_ref.at[3], sems.at[4])
-    copy = start_copy(tiles_ref, list_ref, sems.at[0])
-    fill_hot(hot_ref)
+    in_a = start_copy(a_ref, side_ref.at[2], sems.at[3])
+    b = bias_of(join_pair(c_ref[...], d_ref[...]))
+    side_ref[1] = b
+    out_b = start_copy(side_ref.at[1], b_ref, sems.at[2])
     s_ref[...] = jnp.zeros_like(s_ref)
-    level = join_pair(c_ref[...], d_ref[...])
-    mass.wait()
-    b = bias_of(side_ref[0], level)
-    side_ref[1] = b
-    side_ref[2] = b + 3.2 * side_ref[0]
-    out_b = start_copy(side_ref.at[1], b_ref, sems.at[2])
-    out_next = start_copy(side_ref.at[2], next_ref, sems.at[3])
     fill_biased(yt0_ref, b, yt_ref)
-    in_a.wait()
-    fill_tails(side_ref[3], tail_ref)
+    fill_tails(b, tail_out_ref)
     copy.wait()
 
     def body(entries):
@@ -273,27 +266,24 @@
             s_ref[source_of(e)] += s
 
     sweep(list_ref, body)
-    out_ref[...] = jnp.broadcast_to(total(s_ref)[None], out_ref.shape)
+    mass.wait()
+    in_a.wait()
+    put_level(finish_plain(s_ref, side_ref[2]), side_ref[0], out_ref)
     out_b.wait()
-    out_next.wait()
 
 
 def col_kernel(
-    tiles_ref, lifted_ref, b_ref, xt0_ref, pack_ref, r_ref, out_ref, a_ref, list_ref, side_ref, sems, xt_ref, hot_ref, tail_ref, s_ref
+    tiles_ref, log_ref, b_ref, hot_ref, tail_ref, xt0_ref, pack_ref, r_ref, out_ref, tail_out_ref, a_ref, list_ref, side_ref, sems, xt_ref, s_ref
 ):
-    lifted = start_copy(lifted_ref, side_ref.at[0], sems.at[1])
-    in_b = start_copy(b_ref, side_ref.at[3], sems.at[4])
     copy = start_copy(tiles_ref, list_ref, sems.at[0])
-    fill_hot(hot_ref)
-    s_ref[...] = jnp.zeros_like(s_ref)
-    drop = 3.2 * jnp.log(jnp.sum(r_ref[...], axis=0))
-    lifted.wait()
-    a = side_ref[0] - drop
+    mass = start_copy(log_ref, side_ref.at[0], sems.at[1])
+    in_b = start_copy(b_ref, side_ref.at[2], sems.at[3])
+    a = bias_of(join(r_ref[...]))
     side_ref[1] = a
     out_a = start_copy(side_ref.at[1], a_ref, sems.at[2])
+    s_ref[...] = jnp.zeros_like(s_ref)
     fill_biased(xt0_ref, a, xt_ref)
-    in_b.wait()
-    fill_tails(side_ref[3], tail_ref)
+    fill_tails(a, tail_out_ref)
     copy.wait()
 
     def body(entries):
@@ -302,26 +292,21 @@
             s_ref[target_of(e)] += s
 
     sweep(list_ref, body)
-    out_ref[...] = jnp.broadcast_to(total(s_ref)[None], out_ref.shape)
+    mass.wait()
+    in_b.wait()
+    put_level(finish_plain(s_ref, side_ref[2]), side_ref[0], out_ref)
     out_a.wait()
 
 
 def project_kernel(
-    tiles_ref, lifted_ref, a_ref, x_ref, yt0_ref, pack_ref, c_ref, d_ref, out_ref, b_ref, list_ref, side_ref, sems, yt_ref, hot_ref, tail_ref, w_ref
+    tiles_ref, hot_ref, tail_ref, x_ref, yt0_ref, pack_ref, c_ref, d_ref, out_ref, b_ref, list_ref, side_ref, sems, yt_ref, w_ref
 ):
-    lifted = start_copy(lifted_ref, side_ref.at[0], sems.at[1])
-    in_a = start_copy(a_ref, side_ref.at[3], sems.at[4])
     copy = start_copy(tiles_ref, list_ref, sems.at[0])
-    fill_hot(hot_ref)
-    w_ref[...] = jnp.zeros_like(w_ref)
-    drop = 3.2 * jnp.log(c_ref[...] + d_ref[...])
-    lifted.wait()
-    b = side_ref[0] - drop
+    b = bias_of(join_pair(c_ref[...], d_ref[...]))
     side_ref[1] = b
     out_b = start_copy(side_ref.at[1], b_ref, sems.at[2])
+    w_ref[...] = jnp.zeros_like(w_ref)
     fill_biased(yt0_ref, b, yt_ref)
-    in_a.wait()
-    fill_tails(side_ref[3], tail_ref)
     copy.wait()
 
     def body(entries):
@@ -363,23 +348,22 @@
     )(*(put(a, pltpu.HBM) for a in far), *(put(a, pltpu.VMEM) for a in near))
 
 
-def tile_list(support, chip, per_chip, slots):
+def tile_list(support, chip, core, per_chip, slots):
     rows, per_list = support.shape
-    owned = support // per_chip == chip
+    row = jnp.arange(rows, dtype=jnp.int32)[:, None]
+    owned = (support // per_chip == chip) & (row // 2 % 2 == core)
     flags = owned.astype(jnp.float32)
     upto = (jnp.arange(per_list)[:, None] <= jnp.arange(per_list)[None, :]).astype(jnp.float32)
     before = (jnp.arange(rows)[None, :] < jnp.arange(rows)[:, None]).astype(jnp.float32)
     within = flags @ upto
     start = before @ within[:, -1:]
     place = jnp.where(owned, (within + start).astype(jnp.int32) - 1, -1)
-    count = jnp.sum(owned.astype(jnp.int32))
-    code = jnp.arange(rows, dtype=jnp.int32)[:, None] * 64 + support % per_chip
-    slot = jnp.arange(slots, dtype=jnp.int32)
-    listed = jnp.sum(
-        jnp.where(place[:, :, None] == slot, code[:, :, None], 0), axis=(0, 1), dtype=jnp.int32
-    )
-    listed = jnp.where(slot < count, listed, rows * 64 + per_chip)
-    return jnp.concatenate([listed, jnp.broadcast_to(count, (BLK,))]).reshape(-1, BLK)
+    code = (row // 4 * 2 + row % 2) * 64 + support % per_chip - PAD
+    slot = jnp.arange(slots + BLK, dtype=jnp.int32).reshape(-1, BLK)
+    place, code = place[:, :, None, None], code[:, :, None, None]
+    last = jnp.where((slot >= slots) & (place >= 0), 1, 0)
+    listed = jnp.where(place == slot, code, last)
+    return jnp.sum(listed, axis=(0, 1), dtype=jnp.int32), within
 
 
 def on_device(
@@ -408,9 +392,9 @@
     )(source_latent)
     spread, support = lax.optimization_barrier((spread, support))
     x = exchange(spread, "col", by_chip)
-    tiles = tile_list(of_core(support), chip, k, 12 * mine * chips)
-    tiles, target_latent, target_coords, log_target_mass = lax.optimization_barrier(
-        (tiles, target_latent, target_coords, log_target_mass)
+    tiles, early = tile_list(support, chip, core, k, 12 * mine * chips)
+    early, target_latent, target_coords, log_target_mass = lax.optimization_barrier(
+        (early, target_latent, target_coords, log_target_mass)
     )
 
     def pair(a):
@@ -426,58 +410,75 @@
         [targets, coords, jnp.ones((1, width), bf16), jnp.zeros((PACK - LAT - 3, width), bf16)],
         axis=0,
     )
-    target_log = target_log.astype(f32).reshape(k, BLK)
-    source_log = of_core(log_source_mass.reshape(-1, BLK))
-
     common = [
         pltpu.SMEM(tiles.shape, jnp.int32),
-        pltpu.VMEM((4, n, BLK), f32),
-        pltpu.SemaphoreType.DMA((5,)),
+        pltpu.VMEM((3, n, BLK), f32),
+        pltpu.SemaphoreType.DMA((4,)),
         pltpu.VMEM((n, BLK, BLK), bf16),
-        pltpu.VMEM((GROUP, 3 * GROUP, BLK), bf16),
     ]
     sums = pltpu.VMEM((n + 1, 8, BLK), f32)
     first_scratch = common + [sums, sums]
-    scratch = common + [pltpu.VMEM((n, GROUP, BLK), bf16), sums]
-
+    scratch = common + [sums]
+
+    target_log = target_log.astype(f32).reshape(k, BLK)
+    source_log = of_core(log_source_mass.reshape(-1, BLK))
     tiles, source_log, target_log = lax.optimization_barrier((tiles, source_log, target_log))
+
     turned = pltpu.VMEM((n, BLK, BLK), bf16)
-    yt0, minus_half = call(
-        target_side_kernel, [turned, pltpu.VMEM((k, BLK), f32)], [], [], [pack]
-    )
+    hot_shape = pltpu.VMEM((GROUP, 3 * GROUP, BLK), bf16)
+    yt0, minus_half, hot = call(
+        target_side_kernel, [turned, pltpu.VMEM((k, BLK), f32), hot_shape], [], [], [pack]
+    )
+    tail_shape = pltpu.VMEM((n, GROUP, BLK), bf16)
     small = pltpu.HBM((n, BLK), f32)
     to_chips = jax.ShapeDtypeStruct((chips, n, BLK), f32)
     to_rows = jax.ShapeDtypeStruct((rows, k, BLK), f32)
     to_owners = jax.ShapeDtypeStruct((chips, 8, BLK), f32)
-
-    (r,) = call(first_row_kernel, [to_chips], first_scratch, [tiles], [minus_half, x, yt0])
-    (xt0,) = call(source_side_kernel, [turned], [], [], [x])
+    by_sources, by_targets = [tiles, source_log], [tiles, target_log]
+
+    r, xt0 = call(
+        first_row_kernel,
+        [to_chips, turned],
+        first_scratch,
+        by_sources,
+        [minus_half, hot, x, yt0],
+    )
     r = exchange(r, "col", by_chip)
-    c, a, lifted = call(
+    c, tail, a = call(
         first_col_kernel,
-        [to_rows, small, small],
+        [to_rows, tail_shape, small],
         first_scratch,
-        [tiles, source_log],
-        [xt0, pack, r],
-        2,
-    )
-    c = join(exchange(c, "row"))
+        by_targets,
+        [hot, xt0, pack, r],
+        1,
+    )
+    c = exchange(c, "row")
     d = swap_cores(c, cols)
-    r, b, target_lifted = call(
-        row_kernel, [to_chips, small, small], scratch, [tiles, target_log, a], [x, yt0, c, d], 2
+    r, tail, b = call(
+        row_kernel,
+        [to_chips, tail_shape, small],
+        scratch,
+        by_sources + [a],
+        [hot, tail, x, yt0, c, d],
+        1,
     )
     r = exchange(r, "col", by_chip)
-    c, a = call(
-        col_kernel, [to_rows, small], scratch, [tiles, lifted, b], [xt0, pack, r], 1
-    )
-    c = jnp.sum(exchange(c, "row"), axis=0)
+    c, tail, a = call(
+        col_kernel,
+        [to_rows, tail_shape, small],
+        scratch,
+        by_targets + [b],
+        [hot, tail, xt0, pack, r],
+        1,
+    )
+    c = exchange(c, "row")
     d = swap_cores(c, cols)
     part, b = call(
         project_kernel,
         [to_owners, small],
         scratch,
-        [tiles, target_lifted, a],
-        [x, yt0, pack, c, d],
+        [tiles],
+        [hot, tail, x, yt0, pack, c, d],
         1,
     )
     part, a, b, source_latent = lax.optimization_barrier((part, a, b, source_latent))

time: 106 us -> 102 us (0.962); the launches traced: 107 us -> 101 us
  blocking collectives: 39.4 us -> 49.2 us
  starting transfers between devices: 26.3 us -> 20.4 us
  waiting for transfers between devices: 16.1 us -> 10.4 us
  Pallas kernels: 15.9 us -> 13 us
  local copies, waits for them, and re-layouts: 1.73 us -> 0.47 us
    all_to_all x3 -> x4, blocking collectives: 39.4 us -> 49.2 us  [exchange(): return lax.all_to_all(x, axis, 0, 0, axis_index_groups=groups)]
    all_to_all x3 -> x2, starting transfers between devices: 17.6 us -> 11.3 us  [exchange(): return lax.all_to_all(x, axis, 0, 0, axis_index_groups=groups)]
    all_to_all x3 -> x2, waiting for transfers between devices: 14.4 us -> 8.37 us  [exchange(): return lax.all_to_all(x, axis, 0, 0, axis_index_groups=groups)]
    pallas_call x7 -> x6, Pallas kernels: 14.2 us -> 11.3 us  [call(): pl.pallas_call(kernel, out_shape=outs, in_specs=[HBM] * len(far) + [VMEM]...]
    reshape x1 -> x0, local copies, waits for them, and re-layouts: 1.23 us -> none  [tile_list(): jnp.concatenate([listed, jnp.broadcast_to(count, (BLK,))]).reshape(-1, BLK)]
  transfers between devices with their start and end apart: 8 -> 7, of which waited for: 5 -> 4; matrix products, arithmetic and copies ran while one was open for 7% -> 7% of each run, Pallas kernels for 1% -> 0%
where the time goes in v3:
time: 102 us; the launch traced here: 101 us
  blocking collectives  49.2 us (48%)
  starting transfers between devices  20.4 us (20%)
  Pallas kernels  13 us (13%)
  waiting for transfers between devices  10.4 us (10%)
  other arithmetic  6.52 us (6%)
    all_to_all x4, blocking collectives, exchange(): return lax.all_to_all(x, axis, 0, 0, axis_index_groups=groups)  49.2 us
    pallas_call x6, Pallas kernels, call(): pl.pallas_call(kernel, out_shape=outs, in_specs=[HBM] * len(far) + [VMEM]...  11.3 us
    all_to_all x2, starting transfers between devices, exchange(): return lax.all_to_all(x, axis, 0, 0, axis_index_groups=groups)  11.3 us
    ppermute x5, starting transfers between devices, swap_cores(): return lax.ppermute(x, 'col', [(i, i ^ 1) for i in range(cols)])  9.12 us
    all_to_all x2, waiting for transfers between devices, exchange(): return lax.all_to_all(x, axis, 0, 0, axis_index_groups=groups)  8.37 us
  transfers between devices with their start and end apart: 7, of which 4 were waited for; matrix products, arithmetic and copies ran while one was open for 7% of the time, Pallas kernels for 0%

profile of v3, /device:TPU:1, one launch (start us, length us, event | category | flops | bytes accessed | tf_op | source)
XLA Modules:
  0.0 101.0 jit_solution(9270064890284262291)
XLA Ops:
  0.6 0.0 copy-start.2
  0.6 0.0 copy-start.5
  0.7 0.0 copy-start.4
  0.7 0.0 copy-start
  0.7 0.0 copy-start.3
  0.7 1.6 %shard_map.85 = bf16[16,64,256]{2,1,0:T(8,128)(2,1)} custom-call(bf16[64,256]{1,0:T(8,128)(2,1)} %in_ref.1), custom_call_target="tpu_custom_call" | custom-call | tf_op jit(solution)/shard_map/pallas_call | solution.py:387
  2.3 7.6 %all-to-all-start = ((bf16[16,64,256]{2,1,0:T(8,128)(2,1)}), bf16[16,64,256]{2,1,0:T(8,128)(2,1)S(1)}, u32[]{:S(2)}, u32[]{:S(2)}) async-start(bf16[16,64,256]{2,1,0:T(8,128)(2,1)} %shard_map.85), calls=%async_computation | async-start | bytes 1048576 | tf_op jit(solution)/shard_map/all_to_all | solution.py:30
  10.0 0.0 copy-done.2
  10.0 0.2 fusion.4
  10.2 0.0 copy-done.4
  10.2 1.0 %collective-permute-start = (bf16[1,2048]{1,0:T(2,128)(2,1)S(1)}, bf16[1,2048]{1,0:T(2,128)(2,1)S(1)}, u32[]{:S(2)}, u32[]{:S(2)}) collective-permute-start(bf16[1,2048]{1,0:T(2,128)(2,1)S(1)} %broadcast_in_dim.39), channel_id=1, source_target_pairs={{0,1},{1,0},{2,3},{3,2},{4,5},{5,4},{6,7},{7,6},{8,9},{9,8},{10,11... | collective-permute-start | bytes 12296 | tf_op jit(solution)/shard_map/ppermute | solution.py:26
  11.2 0.0 copy-done.5
  11.2 0.1 collective-permute-start.2
  11.3 0.0 copy-done
  11.3 0.4 collective-permute-start.1
  11.8 0.1 convolution_bitcast_fusion
  12.0 0.1 copy.17
  12.1 0.1 copy.16
  12.1 0.1 copy.15
  12.2 1.8 %select_reduce_fusion.tiles_ref = s32[4,128]{1,0:T(4,128)} fusion(s32[64,32]{1,0:T(8,128)S(1)} %copy.16, s32[4,128]{1,0:T(4,128)S(1)} %multiply_add_fusion, s32[64,32]{1,0:T(8,128)S(1)} %copy.15, pred[64,32]{1,0:T(8,128)(4,1)S(1)} %copy.17, pred[4,128]{1,0:T(4,128)(4,1)S(1)} %broadcast_compare_fusion.1), kind=kLoop, calls=%fused_computation | loop fusion | flops 5242368 | bytes 23040 | tf_op jit(solution)/shard_map/reduce_sum | solution.py:366
  14.0 0.0 copy-done.3
  14.0 0.6 slice_select_fusion
  14.6 0.1 pad.4.clone
  14.7 0.1 pad.5.clone
  14.7 0.0 collective-permute-done
  14.8 0.6 maximum_convert_fusion
  15.4 0.0 collective-permute-done.2
  15.4 0.0 collective-permute-done.1
  15.5 0.2 maximum_maximum_fusion.pack_ref
  15.7 0.3 shard_map.86
  16.0 4.4 %all-to-all-done.x_ref = bf16[16,64,256]{2,1,0:T(8,128)(2,1)S(1)} async-done(((bf16[16,64,256]{2,1,0:T(8,128)(2,1)}), bf16[16,64,256]{2,1,0:T(8,128)(2,1)S(1)}, u32[]{:S(2)}, u32[]{:S(2)}) %all-to-all-start) | async-done | bytes 524320 | tf_op jit(solution)/shard_map/all_to_all | solution.py:30
  20.4 2.1 %shard_map.87 = (f32[16,32,128]{2,1,0:T(8,128)S(1)}, bf16[32,128,128]{2,1,0:T(8,128)(2,1)S(1)}) custom-call(s32[4,128]{1,0:T(4,128)} %select_reduce_fusion.tiles_ref, f32[32,128]{1,0:T(8,128)} %bitcast.16, f32[32,128]{1,0:T(8,128)S(1)} %get-tuple-element.39.b_ref, bf16[16,48,128]{2,1,0:T(8,128)(2,1)S(1)} %get-tuple-element.36.hot_ref, ...), custom_call_target="tpu_custom_call" | custom-call | tf_op jit(solution)/shard_map/pallas_call | solution.py:341
  22.6 10.7 %all_to_all.30.r_ref = f32[16,32,128]{2,1,0:T(8,128)S(1)} all-to-all(f32[16,32,128]{2,1,0:T(8,128)S(1)} %get-tuple-element.43), channel_id=1, replica_groups={{0,2,4,6,8,10,12,14,16,18,20,22,24,26,28,30},{1,3,5,7,9,11,13,15,17,19,..., dimensions={0} | all-to-all | bytes 524288 | tf_op jit(solution)/shard_map/all_to_all | solution.py:30
  33.3 2.1 %shard_map.88 = (f32[8,32,128]{2,1,0:T(8,128)S(1)}, bf16[32,16,128]{2,1,0:T(8,128)(2,1)S(1)}, f32[32,128]{1,0:T(8,128)}) custom-call(s32[4,128]{1,0:T(4,128)} %select_reduce_fusion.tiles_ref, f32[32,128]{1,0:T(8,128)} %bitcast.18, bf16[16,48,128]{2,1,0:T(8,128)(2,1)S(1)} %get-tuple-element.36.hot_ref, bf16[32,128,128]{2,1,0:T(8,128)(2,1)S(1)} %get-tuple-element.42.xt0_ref, ...), custom_call_target="tpu_custom_call" | custom-call | tf_op jit(solution)/shard_map/pallas_call | solution.py:341
  35.5 16.4 %all_to_all.31.c_ref = f32[8,32,128]{2,1,0:T(8,128)S(1)} all-to-all(f32[8,32,128]{2,1,0:T(8,128)S(1)} %get-tuple-element.46), channel_id=1, replica_groups=mesh['row'=8,'col'=32] {'row'}, dimensions={0} | all-to-all | bytes 262144 | tf_op jit(solution)/shard_map/all_to_all | solution.py:30
  51.8 4.6 %collective-permute-start.3 = (f32[8,32,128]{2,1,0:T(8,128)S(1)}, f32[8,32,128]{2,1,0:T(8,128)S(1)}, u32[]{:S(2)}, u32[]{:S(2)}) collective-permute-start(f32[8,32,128]{2,1,0:T(8,128)S(1)} %all_to_all.31.c_ref), channel_id=1, source_target_pairs={{0,1},{1,0},{2,3},{3,2},{4,5},{5,4},{6,7},{7,6},{8,9},{9,8},{10,11... | collective-permute-start | bytes 393224 | tf_op jit(solution)/shard_map/ppermute | solution.py:26
  56.5 1.0 collective-permute-done.3.d_ref
  57.4 1.7 %shard_map.89 = (f32[16,32,128]{2,1,0:T(8,128)S(1)}, bf16[32,16,128]{2,1,0:T(8,128)(2,1)S(1)}, f32[32,128]{1,0:T(8,128)}) custom-call(s32[4,128]{1,0:T(4,128)} %select_reduce_fusion.tiles_ref, f32[32,128]{1,0:T(8,128)} %bitcast.17, f32[32,128]{1,0:T(8,128)} %get-tuple-element.44.a_ref, bf16[16,48,128]{2,1,0:T(8,128)(2,1)S(1)} %get-tuple-element.36.hot_ref, ...), custom_call_target="tpu_custom_call" | custom-call | tf_op jit(solution)/shard_map/pallas_call | solution.py:341
  59.2 11.5 %all_to_all.32.r_ref = f32[16,32,128]{2,1,0:T(8,128)S(1)} all-to-all(f32[16,32,128]{2,1,0:T(8,128)S(1)} %get-tuple-element.49), channel_id=1, replica_groups={{0,2,4,6,8,10,12,14,16,18,20,22,24,26,28,30},{1,3,5,7,9,11,13,15,17,19,..., dimensions={0} | all-to-all | bytes 524288 | tf_op jit(solution)/shard_map/all_to_all | solution.py:30
  70.7 1.9 %shard_map.90 = (f32[8,32,128]{2,1,0:T(8,128)S(1)}, bf16[32,16,128]{2,1,0:T(8,128)(2,1)S(1)}, f32[32,128]{1,0:T(8,128)}) custom-call(s32[4,128]{1,0:T(4,128)} %select_reduce_fusion.tiles_ref, f32[32,128]{1,0:T(8,128)} %bitcast.19, f32[32,128]{1,0:T(8,128)} %get-tuple-element.47.b_ref, bf16[16,48,128]{2,1,0:T(8,128)(2,1)S(1)} %get-tuple-element.36.hot_ref, ...), custom_call_target="tpu_custom_call" | custom-call | tf_op jit(solution)/shard_map/pallas_call | solution.py:341
  72.6 10.6 %all_to_all.33.c_ref = f32[8,32,128]{2,1,0:T(8,128)S(1)} all-to-all(f32[8,32,128]{2,1,0:T(8,128)S(1)} %get-tuple-element.51), channel_id=1, replica_groups=mesh['row'=8,'col'=32] {'row'}, dimensions={0} | all-to-all | bytes 262144 | tf_op jit(solution)/shard_map/all_to_all | solution.py:30
  83.1 2.9 %collective-permute-start.4 = (f32[8,32,128]{2,1,0:T(8,128)S(1)}, f32[8,32,128]{2,1,0:T(8,128)S(1)}, u32[]{:S(2)}, u32[]{:S(2)}) collective-permute-start(f32[8,32,128]{2,1,0:T(8,128)S(1)} %all_to_all.33.c_ref), channel_id=1, source_target_pairs={{0,1},{1,0},{2,3},{3,2},{4,5},{5,4},{6,7},{7,6},{8,9},{9,8},{10,11... | collective-permute-start | bytes 393224 | tf_op jit(solution)/shard_map/ppermute | solution.py:26
  86.1 1.0 collective-permute-done.4.d_ref
  87.1 0.0 copy-start.1
  87.1 3.1 %shard_map.91 = (f32[16,8,128]{2,1,0:T(8,128)}, f32[32,128]{1,0:T(8,128)}) custom-call(s32[4,128]{1,0:T(4,128)} %select_reduce_fusion.tiles_ref, bf16[16,48,128]{2,1,0:T(8,128)(2,1)S(1)} %get-tuple-element.36.hot_ref, bf16[32,16,128]{2,1,0:T(8,128)(2,1)S(1)} %get-tuple-element.50.tail_ref, bf16[16,64,256]{2,1,0:T(8,128)(2,1)S(1)} %all-to-all-done.x_ref, ...), custom_call_target="tpu_custom_call" | custom-call | tf_op jit(solution)/shard_map/pallas_call | solution.py:341
  90.1 0.0 copy-done.1
  90.2 3.7 %all-to-all-start.5 = ((f32[16,8,128]{2,1,0:T(8,128)}), f32[16,8,128]{2,1,0:T(8,128)S(1)}, u32[]{:S(2)}, u32[]{:S(2)}) async-start(f32[16,8,128]{2,1,0:T(8,128)} %get-tuple-element.58), calls=%async_computation.5 | async-start | bytes 131072 | tf_op jit(solution)/shard_map/all_to_all | solution.py:30
  93.9 1.3 %fusion.9 = f32[256]{0:T(256)} fusion(f32[256]{0:T(256)S(1)} %multiply_reduce_fusion, f32[32,128]{1,0:T(8,128)} %get-tuple-element.55, s32[]{:T(128)S(6)} %select_n.149), kind=kLoop, calls=%fused_computation.40 | loop fusion | flops 768 | bytes 3076 | tf_op jit(solution)/shard_map/div | solution.py:491
  95.1 1.3 %fusion.8 = f32[2048]{0:T(1024)} fusion(f32[32,128]{1,0:T(8,128)S(1)} %get-tuple-element.39.b_ref, s32[]{:T(128)S(6)} %select_n.150, f32[32,128]{1,0:T(8,128)} %get-tuple-element.57), kind=kLoop, calls=%fused_computation.30 | loop fusion | flops 4096 | bytes 24580 | tf_op jit(solution)/shard_map/reshape | solution.py:492
  96.4 4.0 %all-to-all-done.5 = f32[16,8,128]{2,1,0:T(8,128)S(1)} async-done(((f32[16,8,128]{2,1,0:T(8,128)}), f32[16,8,128]{2,1,0:T(8,128)S(1)}, u32[]{:S(2)}, u32[]{:S(2)}) %all-to-all-start.5) | async-done | bytes 65568 | tf_op jit(solution)/shard_map/all_to_all | solution.py:30
  100.4 0.6 broadcast_divide_fusion
  (16 shorter events, 0.2 us)
Async XLA Ops:
  0.6 9.3 %copy-start.2 = (s32[64,32]{0,1:T(8,128)S(1)}, s32[64,32]{0,1:T(8,128)}, u32[]{:S(2)}) copy-start(s32[64,32]{0,1:T(8,128)} %param.11) | copy-start | bytes 24580
  0.6 10.6 %copy-start.5 = (bf16[2,2048]{1,0:T(2,128)(2,1)S(1)}, bf16[2,2048]{1,0:T(2,128)(2,1)}, u32[]{:S(2)}) copy-start(bf16[2,2048]{1,0:T(2,128)(2,1)} %param.10) | copy-start | bytes 24580
  0.7 9.5 %copy-start.4 = (bf16[2048]{0:T(1024)(128)(2,1)S(1)}, bf16[2048]{0:T(1024)(128)(2,1)}, u32[]{:S(2)}) copy-start(bf16[2048]{0:T(1024)(128)(2,1)} %param.9) | copy-start | bytes 12292
  0.7 10.7 %copy-start = (bf16[64,2048]{1,0:T(8,128)(2,1)S(1)}, bf16[64,2048]{1,0:T(8,128)(2,1)}, u32[]{:S(2)}) copy-start(bf16[64,2048]{1,0:T(8,128)(2,1)} %param.7) | copy-start | bytes 786436
  0.7 13.3 %copy-start.3 = (f32[8192]{0:T(1024)S(1)}, f32[8192]{0:T(1024)}, u32[]{:S(2)}) copy-start(f32[8192]{0:T(1024)} %param.8) | copy-start | bytes 98308
  2.3 18.1 %all-to-all-start = ((bf16[16,64,256]{2,1,0:T(8,128)(2,1)}), bf16[16,64,256]{2,1,0:T(8,128)(2,1)S(1)}, u32[]{:S(2)}, u32[]{:S(2)}) async-start(bf16[16,64,256]{2,1,0:T(8,128)(2,1)} %shard_map.85), calls=%async_computation | async-start | bytes 1048576 | tf_op jit(solution)/shard_map/all_to_all | solution.py:30
  10.2 4.6 %collective-permute-start = (bf16[1,2048]{1,0:T(2,128)(2,1)S(1)}, bf16[1,2048]{1,0:T(2,128)(2,1)S(1)}, u32[]{:S(2)}, u32[]{:S(2)}) collective-permute-start(bf16[1,2048]{1,0:T(2,128)(2,1)S(1)} %broadcast_in_dim.39), channel_id=1, source_target_pairs={{0,1},{1,0},{2,3},{3,2},{4,5},{5,4},{6,7},{7,6},{8,9},{9,8},{10,11... | collective-permute-start | bytes 12296 | tf_op jit(solution)/shard_map/ppermute | solution.py:26
  11.2 4.1 %collective-permute-start.2 = (bf16[2,2048]{1,0:T(2,128)(2,1)S(1)}, bf16[2,2048]{1,0:T(2,128)(2,1)S(1)}, u32[]{:S(2)}, u32[]{:S(2)}) collective-permute-start(bf16[2,2048]{1,0:T(2,128)(2,1)S(1)} %copy-done.5), channel_id=1, source_target_pairs={{0,1},{1,0},{2,3},{3,2},{4,5},{5,4},{6,7},{7,6},{8,9},{9,8},{10,11... | collective-permute-start | bytes 24584 | tf_op jit(solution)/shard_map/ppermute | solution.py:26
  11.3 4.1 %collective-permute-start.1 = (bf16[64,2048]{1,0:T(8,128)(2,1)S(1)}, bf16[64,2048]{1,0:T(8,128)(2,1)S(1)}, u32[]{:S(2)}, u32[]{:S(2)}) collective-permute-start(bf16[64,2048]{1,0:T(8,128)(2,1)S(1)} %copy-done), channel_id=1, source_target_pairs={{0,1},{1,0},{2,3},{3,2},{4,5},{5,4},{6,7},{7,6},{8,9},{9,8},{10,11... | collective-permute-start | bytes 786440 | tf_op jit(solution)/shard_map/ppermute | solution.py:26
  51.8 5.6 %collective-permute-start.3 = (f32[8,32,128]{2,1,0:T(8,128)S(1)}, f32[8,32,128]{2,1,0:T(8,128)S(1)}, u32[]{:S(2)}, u32[]{:S(2)}) collective-permute-start(f32[8,32,128]{2,1,0:T(8,128)S(1)} %all_to_all.31.c_ref), channel_id=1, source_target_pairs={{0,1},{1,0},{2,3},{3,2},{4,5},{5,4},{6,7},{7,6},{8,9},{9,8},{10,11... | collective-permute-start | bytes 393224 | tf_op jit(solution)/shard_map/ppermute | solution.py:26
  83.1 3.9 %collective-permute-start.4 = (f32[8,32,128]{2,1,0:T(8,128)S(1)}, f32[8,32,128]{2,1,0:T(8,128)S(1)}, u32[]{:S(2)}, u32[]{:S(2)}) collective-permute-start(f32[8,32,128]{2,1,0:T(8,128)S(1)} %all_to_all.33.c_ref), channel_id=1, source_target_pairs={{0,1},{1,0},{2,3},{3,2},{4,5},{5,4},{6,7},{7,6},{8,9},{9,8},{10,11... | collective-permute-start | bytes 393224 | tf_op jit(solution)/shard_map/ppermute | solution.py:26
  87.1 3.1 %copy-start.1 = (bf16[64,256]{1,0:T(8,128)(2,1)S(1)}, bf16[64,256]{1,0:T(8,128)(2,1)}, u32[]{:S(2)}) copy-start(bf16[64,256]{1,0:T(8,128)(2,1)} %in_ref.1) | copy-start | bytes 98308
  90.2 10.2 %all-to-all-start.5 = ((f32[16,8,128]{2,1,0:T(8,128)}), f32[16,8,128]{2,1,0:T(8,128)S(1)}, u32[]{:S(2)}, u32[]{:S(2)}) async-start(f32[16,8,128]{2,1,0:T(8,128)} %get-tuple-element.58), calls=%async_computation.5 | async-start | bytes 131072 | tf_op jit(solution)/shard_map/all_to_all | solution.py:30

commit v4 on v3

--- a/solution.py
+++ b/solution.py
@@ -12,7 +12,8 @@
 NEG = -1e30
 LN2 = 0.6931471805599453
 KAPPA = 0.3125 / LN2
-TURNS = (64, 32, 16)
+PLAIN_TURNS = (128, 64, 32, 16)
+TURNS = (64, 16)
 PACK = 80
 GROUP = 16
 PAD = 32 * 64 + 32
@@ -85,12 +86,12 @@
     return jnp.dot(lhs, rhs, preferred_element_type=jnp.float32)
 
 
-def sweep(list_ref, body):
+def sweep(list_ref, body, sizes=TURNS):
     count = list_ref[list_ref.shape[0] - 1, 0]
     done = 0
-    for size in TURNS:
+    for size in sizes:
         left = jnp.maximum(count - done, 0)
-        turns = (left + (size // 2 if size > TURNS[-1] else size - 1)) // size
+        turns = (left + (size // 4 if size > sizes[-1] else size) - 1) // size
 
         def turn(g, c, size=size, done=done):
             first = done + g * size
@@ -200,7 +201,7 @@
 
 
 def first_row_kernel(
-    tiles_ref, log_ref, b_ref, hot_ref, x_ref, yt0_ref, out_ref, xt0_ref, list_ref, side_ref, sems, yt_ref, m_ref, s_ref
+    log_ref, tiles_ref, b_ref, hot_ref, x_ref, yt0_ref, out_ref, xt0_ref, list_ref, side_ref, sems, yt_ref, m_ref, s_ref
 ):
     copy = start_copy(tiles_ref, list_ref, sems.at[0])
     mass = start_copy(log_ref, side_ref.at[0], sems.at[1])
@@ -222,7 +223,7 @@
 
 
 def first_col_kernel(
-    tiles_ref, log_ref, hot_ref, xt0_ref, pack_ref, r_ref, out_ref, tail_out_ref, a_ref, list_ref, side_ref, sems, xt_ref, m_ref, s_ref
+    log_ref, tiles_ref, hot_ref, xt0_ref, pack_ref, r_ref, out_ref, tail_out_ref, a_ref, list_ref, side_ref, sems, xt_ref, m_ref, s_ref
 ):
     copy = start_copy(tiles_ref, list_ref, sems.at[0])
     mass = start_copy(log_ref, side_ref.at[0], sems.at[1])
@@ -247,7 +248,7 @@
 
 
 def row_kernel(
-    tiles_ref, log_ref, a_ref, hot_ref, tail_ref, x_ref, yt0_ref, c_ref, d_ref, out_ref, tail_out_ref, b_ref, list_ref, side_ref, sems, yt_ref, s_ref
+    log_ref, a_ref, tiles_ref, hot_ref, tail_ref, x_ref, yt0_ref, c_ref, d_ref, out_ref, tail_out_ref, b_ref, list_ref, side_ref, sems, yt_ref, s_ref
 ):
     copy = start_copy(tiles_ref, list_ref, sems.at[0])
     mass = start_copy(log_ref, side_ref.at[0], sems.at[1])
@@ -265,7 +266,7 @@
         for e, s in zip(entries, [plain_sum(acc) for acc in accs]):
             s_ref[source_of(e)] += s
 
-    sweep(list_ref, body)
+    sweep(list_ref, body, PLAIN_TURNS)
     mass.wait()
     in_a.wait()
     put_level(finish_plain(s_ref, side_ref[2]), side_ref[0], out_ref)
@@ -273,7 +274,7 @@
 
 
 def col_kernel(
-    tiles_ref, log_ref, b_ref, hot_ref, tail_ref, xt0_ref, pack_ref, r_ref, out_ref, tail_out_ref, a_ref, list_ref, side_ref, sems, xt_ref, s_ref
+    log_ref, b_ref, tiles_ref, hot_ref, tail_ref, xt0_ref, pack_ref, r_ref, out_ref, tail_out_ref, a_ref, list_ref, side_ref, sems, xt_ref, s_ref
 ):
     copy = start_copy(tiles_ref, list_ref, sems.at[0])
     mass = start_copy(log_ref, side_ref.at[0], sems.at[1])
@@ -291,7 +292,7 @@
         for e, s in zip(entries, [plain_sum(acc) for acc in accs]):
             s_ref[target_of(e)] += s
 
-    sweep(list_ref, body)
+    sweep(list_ref, body, PLAIN_TURNS)
     mass.wait()
     in_b.wait()
     put_level(finish_plain(s_ref, side_ref[2]), side_ref[0], out_ref)
@@ -434,14 +435,14 @@
     to_chips = jax.ShapeDtypeStruct((chips, n, BLK), f32)
     to_rows = jax.ShapeDtypeStruct((rows, k, BLK), f32)
     to_owners = jax.ShapeDtypeStruct((chips, 8, BLK), f32)
-    by_sources, by_targets = [tiles, source_log], [tiles, target_log]
+    by_sources, by_targets = [source_log], [target_log]
 
     r, xt0 = call(
         first_row_kernel,
         [to_chips, turned],
         first_scratch,
         by_sources,
-        [minus_half, hot, x, yt0],
+        [tiles, minus_half, hot, x, yt0],
     )
     r = exchange(r, "col", by_chip)
     c, tail, a = call(
@@ -449,7 +450,7 @@
         [to_rows, tail_shape, small],
         first_scratch,
         by_targets,
-        [hot, xt0, pack, r],
+        [tiles, hot, xt0, pack, r],
         1,
     )
     c = exchange(c, "row")
@@ -459,7 +460,7 @@
         [to_chips, tail_shape, small],
         scratch,
         by_sources + [a],
-        [hot, tail, x, yt0, c, d],
+        [tiles, hot, tail, x, yt0, c, d],
         1,
     )
     r = exchange(r, "col", by_chip)
@@ -468,7 +469,7 @@
         [to_rows, tail_shape, small],
         scratch,
         by_targets + [b],
-        [hot, tail, xt0, pack, r],
+        [tiles, hot, tail, xt0, pack, r],
         1,
     )
     c = exchange(c, "row")
@@ -477,8 +478,8 @@
         project_kernel,
         [to_owners, small],
         scratch,
-        [tiles],
-        [hot, tail, x, yt0, pack, c, d],
+        [],
+        [tiles, hot, tail, x, yt0, pack, c, d],
         1,
     )
     part, a, b, source_latent = lax.optimization_barrier((part, a, b, source_latent))

time: 102 us -> 101 us (level); the launches traced: 101 us -> 98.9 us
  transfers between devices with their start and end apart: 7 -> 7, of which waited for: 4 -> 4; matrix products, arithmetic and copies ran while one was open for 7% -> 6% of each run, Pallas kernels for 0% -> 0%
where the time goes in v4:
time: 101 us; the launch traced here: 98.9 us
  blocking collectives  48.4 us (48%)
  starting transfers between devices  19.8 us (20%)
  Pallas kernels  12.1 us (12%)
  waiting for transfers between devices  10.9 us (11%)
  other arithmetic  5.94 us (6%)
    all_to_all x4, blocking collectives, exchange(): return lax.all_to_all(x, axis, 0, 0, axis_index_groups=groups)  48.4 us
    all_to_all x2, starting transfers between devices, exchange(): return lax.all_to_all(x, axis, 0, 0, axis_index_groups=groups)  11.6 us
    pallas_call x6, Pallas kernels, call(): pl.pallas_call(kernel, out_shape=outs, in_specs=[HBM] * len(far) + [VMEM]...  10.5 us
    all_to_all x2, waiting for transfers between devices, exchange(): return lax.all_to_all(x, axis, 0, 0, axis_index_groups=groups)  8.94 us
    ppermute x5, starting transfers between devices, swap_cores(): return lax.ppermute(x, 'col', [(i, i ^ 1) for i in range(cols)])  8.22 us
  transfers between devices with their start and end apart: 7, of which 4 were waited for; matrix products, arithmetic and copies ran while one was open for 6% of the time, Pallas kernels for 0%

profile of v4, /device:TPU:1, one launch (start us, length us, event | category | flops | bytes accessed | tf_op | source)
XLA Modules:
  0.0 98.9 jit_solution(15401688093460384279)
XLA Ops:
  0.6 0.0 copy-start.2
  0.6 0.0 copy-start.5
  0.7 0.0 copy-start.4
  0.7 0.0 copy-start
  0.7 0.0 copy-start.3
  0.7 1.6 %shard_map.85 = bf16[16,64,256]{2,1,0:T(8,128)(2,1)} custom-call(bf16[64,256]{1,0:T(8,128)(2,1)} %in_ref.1), custom_call_target="tpu_custom_call" | custom-call | tf_op jit(solution)/shard_map/pallas_call | solution.py:388
  2.3 7.6 %all-to-all-start = ((bf16[16,64,256]{2,1,0:T(8,128)(2,1)}), bf16[16,64,256]{2,1,0:T(8,128)(2,1)S(1)}, u32[]{:S(2)}, u32[]{:S(2)}) async-start(bf16[16,64,256]{2,1,0:T(8,128)(2,1)} %shard_map.85), calls=%async_computation | async-start | bytes 1048576 | tf_op jit(solution)/shard_map/all_to_all | solution.py:31
  10.0 0.0 copy-done.2
  10.0 0.2 fusion.4
  10.2 0.0 copy-done.4
  10.2 1.0 %collective-permute-start = (bf16[1,2048]{1,0:T(2,128)(2,1)S(1)}, bf16[1,2048]{1,0:T(2,128)(2,1)S(1)}, u32[]{:S(2)}, u32[]{:S(2)}) collective-permute-start(bf16[1,2048]{1,0:T(2,128)(2,1)S(1)} %broadcast_in_dim.39), channel_id=1, source_target_pairs={{0,1},{1,0},{2,3},{3,2},{4,5},{5,4},{6,7},{7,6},{8,9},{9,8},{10,11... | collective-permute-start | bytes 12296 | tf_op jit(solution)/shard_map/ppermute | solution.py:27
  11.2 0.0 copy-done.5
  11.2 0.1 collective-permute-start.2
  11.3 0.0 copy-done
  11.3 0.4 collective-permute-start.1
  11.8 0.1 convolution_bitcast_fusion
  12.0 0.1 copy.17
  12.1 0.1 copy.16
  12.1 0.1 copy.15
  12.2 1.2 %select_reduce_fusion.tiles_ref = s32[4,128]{1,0:T(4,128)S(1)} fusion(s32[64,32]{1,0:T(8,128)S(1)} %copy.16, s32[4,128]{1,0:T(4,128)S(1)} %multiply_add_fusion, s32[64,32]{1,0:T(8,128)S(1)} %copy.15, pred[64,32]{1,0:T(8,128)(4,1)S(1)} %copy.17, pred[4,128]{1,0:T(4,128)(4,1)S(1)} %broadcast_compare_fusion.1), kind=kLoop, calls=%fused_computation | loop fusion | flops 5242368 | bytes 23040 | tf_op jit(solution)/shard_map/reduce_sum | solution.py:367
  13.4 0.0 copy-done.3
  13.4 0.6 slice_select_fusion
  14.0 0.1 pad.4.clone
  14.1 0.1 pad.5.clone
  14.2 0.0 collective-permute-done
  14.2 0.6 maximum_convert_fusion
  14.8 0.0 collective-permute-done.2
  14.8 0.0 collective-permute-done.1
  14.9 0.2 maximum_maximum_fusion.pack_ref
  15.1 0.3 shard_map.86
  15.5 5.0 %all-to-all-done.x_ref = bf16[16,64,256]{2,1,0:T(8,128)(2,1)S(1)} async-done(((bf16[16,64,256]{2,1,0:T(8,128)(2,1)}), bf16[16,64,256]{2,1,0:T(8,128)(2,1)S(1)}, u32[]{:S(2)}, u32[]{:S(2)}) %all-to-all-start) | async-done | bytes 524320 | tf_op jit(solution)/shard_map/all_to_all | solution.py:31
  20.4 2.0 %shard_map.87 = (f32[16,32,128]{2,1,0:T(8,128)S(1)}, bf16[32,128,128]{2,1,0:T(8,128)(2,1)S(1)}) custom-call(f32[32,128]{1,0:T(8,128)} %bitcast.16, s32[4,128]{1,0:T(4,128)S(1)} %select_reduce_fusion.tiles_ref, f32[32,128]{1,0:T(8,128)S(1)} %get-tuple-element.39.b_ref, bf16[16,48,128]{2,1,0:T(8,128)(2,1)S(1)} %get-tuple-element.36.hot_ref, ...), custom_call_target="tpu_custom_call" | custom-call | tf_op jit(solution)/shard_map/pallas_call | solution.py:342
  22.4 10.7 %all_to_all.30.r_ref = f32[16,32,128]{2,1,0:T(8,128)S(1)} all-to-all(f32[16,32,128]{2,1,0:T(8,128)S(1)} %get-tuple-element.43), channel_id=1, replica_groups={{0,2,4,6,8,10,12,14,16,18,20,22,24,26,28,30},{1,3,5,7,9,11,13,15,17,19,..., dimensions={0} | all-to-all | bytes 524288 | tf_op jit(solution)/shard_map/all_to_all | solution.py:31
  33.2 2.0 %shard_map.88 = (f32[8,32,128]{2,1,0:T(8,128)S(1)}, bf16[32,16,128]{2,1,0:T(8,128)(2,1)S(1)}, f32[32,128]{1,0:T(8,128)}) custom-call(f32[32,128]{1,0:T(8,128)} %bitcast.18, s32[4,128]{1,0:T(4,128)S(1)} %select_reduce_fusion.tiles_ref, bf16[16,48,128]{2,1,0:T(8,128)(2,1)S(1)} %get-tuple-element.36.hot_ref, ...), custom_call_target="tpu_custom_call" | custom-call | tf_op jit(solution)/shard_map/pallas_call | solution.py:342
  35.1 16.1 %all_to_all.31.c_ref = f32[8,32,128]{2,1,0:T(8,128)S(1)} all-to-all(f32[8,32,128]{2,1,0:T(8,128)S(1)} %get-tuple-element.46), channel_id=1, replica_groups=mesh['row'=8,'col'=32] {'row'}, dimensions={0} | all-to-all | bytes 262144 | tf_op jit(solution)/shard_map/all_to_all | solution.py:31
  51.2 4.1 %collective-permute-start.3 = (f32[8,32,128]{2,1,0:T(8,128)S(1)}, f32[8,32,128]{2,1,0:T(8,128)S(1)}, u32[]{:S(2)}, u32[]{:S(2)}) collective-permute-start(f32[8,32,128]{2,1,0:T(8,128)S(1)} %all_to_all.31.c_ref), channel_id=1, source_target_pairs={{0,1},{1,0},{2,3},{3,2},{4,5},{5,4},{6,7},{7,6},{8,9},{9,8},{10,11... | collective-permute-start | bytes 393224 | tf_op jit(solution)/shard_map/ppermute | solution.py:27
  55.4 1.0 collective-permute-done.3.d_ref
  56.4 1.6 %shard_map.89 = (f32[16,32,128]{2,1,0:T(8,128)S(1)}, bf16[32,16,128]{2,1,0:T(8,128)(2,1)S(1)}, f32[32,128]{1,0:T(8,128)}) custom-call(f32[32,128]{1,0:T(8,128)} %bitcast.17, f32[32,128]{1,0:T(8,128)} %get-tuple-element.44.a_ref, s32[4,128]{1,0:T(4,128)S(1)} %select_reduce_fusion.tiles_ref, bf16[16,48,128]{2,1,0:T(8,128)(2,1)S(1)} %get-tuple-element.36.hot_ref, ...), custom_call_target="tpu_custom_call" | custom-call | tf_op jit(solution)/shard_map/pallas_call | solution.py:342
  58.0 10.5 %all_to_all.32.r_ref = f32[16,32,128]{2,1,0:T(8,128)S(1)} all-to-all(f32[16,32,128]{2,1,0:T(8,128)S(1)} %get-tuple-element.49), channel_id=1, replica_groups={{0,2,4,6,8,10,12,14,16,18,20,22,24,26,28,30},{1,3,5,7,9,11,13,15,17,19,..., dimensions={0} | all-to-all | bytes 524288 | tf_op jit(solution)/shard_map/all_to_all | solution.py:31
  68.5 1.6 %shard_map.90 = (f32[8,32,128]{2,1,0:T(8,128)S(1)}, bf16[32,16,128]{2,1,0:T(8,128)(2,1)S(1)}, f32[32,128]{1,0:T(8,128)}) custom-call(f32[32,128]{1,0:T(8,128)} %bitcast.19, f32[32,128]{1,0:T(8,128)} %get-tuple-element.47.b_ref, s32[4,128]{1,0:T(4,128)S(1)} %select_reduce_fusion.tiles_ref, bf16[16,48,128]{2,1,0:T(8,128)(2,1)S(1)} %get-tuple-element.36.hot_ref, ...), custom_call_target="tpu_custom_call" | custom-call | tf_op jit(solution)/shard_map/pallas_call | solution.py:342
  70.1 11.1 %all_to_all.33.c_ref = f32[8,32,128]{2,1,0:T(8,128)S(1)} all-to-all(f32[8,32,128]{2,1,0:T(8,128)S(1)} %get-tuple-element.51), channel_id=1, replica_groups=mesh['row'=8,'col'=32] {'row'}, dimensions={0} | all-to-all | bytes 262144 | tf_op jit(solution)/shard_map/all_to_all | solution.py:31
  81.2 2.5 %collective-permute-start.4 = (f32[8,32,128]{2,1,0:T(8,128)S(1)}, f32[8,32,128]{2,1,0:T(8,128)S(1)}, u32[]{:S(2)}, u32[]{:S(2)}) collective-permute-start(f32[8,32,128]{2,1,0:T(8,128)S(1)} %all_to_all.33.c_ref), channel_id=1, source_target_pairs={{0,1},{1,0},{2,3},{3,2},{4,5},{5,4},{6,7},{7,6},{8,9},{9,8},{10,11... | collective-permute-start | bytes 393224 | tf_op jit(solution)/shard_map/ppermute | solution.py:27
  83.8 1.0 collective-permute-done.4.d_ref
  84.7 0.0 copy-start.1
  84.7 2.9 %shard_map.91 = (f32[16,8,128]{2,1,0:T(8,128)}, f32[32,128]{1,0:T(8,128)}) custom-call(s32[4,128]{1,0:T(4,128)S(1)} %select_reduce_fusion.tiles_ref, bf16[16,48,128]{2,1,0:T(8,128)(2,1)S(1)} %get-tuple-element.36.hot_ref, bf16[32,16,128]{2,1,0:T(8,128)(2,1)S(1)} %get-tuple-element.50.tail_ref, bf16[16,64,256]{2,1,0:T(8,128)(2,1)S(1)} %all-to-all-done.x_ref, ...), custom_call_target="tpu_custom_call" | custom-call | tf_op jit(solution)/shard_map/pallas_call | solution.py:342
  87.7 0.0 copy-done.1
  87.7 4.0 %all-to-all-start.5 = ((f32[16,8,128]{2,1,0:T(8,128)}), f32[16,8,128]{2,1,0:T(8,128)S(1)}, u32[]{:S(2)}, u32[]{:S(2)}) async-start(f32[16,8,128]{2,1,0:T(8,128)} %get-tuple-element.58), calls=%async_computation.5 | async-start | bytes 131072 | tf_op jit(solution)/shard_map/all_to_all | solution.py:31
  91.7 1.3 %fusion.9 = f32[256]{0:T(256)} fusion(f32[256]{0:T(256)S(1)} %multiply_reduce_fusion, f32[32,128]{1,0:T(8,128)} %get-tuple-element.55, s32[]{:T(128)S(6)} %select_n.149), kind=kLoop, calls=%fused_computation.40 | loop fusion | flops 768 | bytes 3076 | tf_op jit(solution)/shard_map/div | solution.py:492
  93.0 1.3 %fusion.8 = f32[2048]{0:T(1024)} fusion(f32[32,128]{1,0:T(8,128)S(1)} %get-tuple-element.39.b_ref, s32[]{:T(128)S(6)} %select_n.150, f32[32,128]{1,0:T(8,128)} %get-tuple-element.57), kind=kLoop, calls=%fused_computation.30 | loop fusion | flops 4096 | bytes 24580 | tf_op jit(solution)/shard_map/reshape | solution.py:493
  94.3 4.0 %all-to-all-done.5 = f32[16,8,128]{2,1,0:T(8,128)S(1)} async-done(((f32[16,8,128]{2,1,0:T(8,128)}), f32[16,8,128]{2,1,0:T(8,128)S(1)}, u32[]{:S(2)}, u32[]{:S(2)}) %all-to-all-start.5) | async-done | bytes 65568 | tf_op jit(solution)/shard_map/all_to_all | solution.py:31
  98.3 0.6 broadcast_divide_fusion
  (16 shorter events, 0.2 us)
Async XLA Ops:
  0.6 9.3 %copy-start.2 = (s32[64,32]{0,1:T(8,128)S(1)}, s32[64,32]{0,1:T(8,128)}, u32[]{:S(2)}) copy-start(s32[64,32]{0,1:T(8,128)} %param.11) | copy-start | bytes 24580
  0.6 10.6 %copy-start.5 = (bf16[2,2048]{1,0:T(2,128)(2,1)S(1)}, bf16[2,2048]{1,0:T(2,128)(2,1)}, u32[]{:S(2)}) copy-start(bf16[2,2048]{1,0:T(2,128)(2,1)} %param.10) | copy-start | bytes 24580
  0.7 9.5 %copy-start.4 = (bf16[2048]{0:T(1024)(128)(2,1)S(1)}, bf16[2048]{0:T(1024)(128)(2,1)}, u32[]{:S(2)}) copy-start(bf16[2048]{0:T(1024)(128)(2,1)} %param.9) | copy-start | bytes 12292
  0.7 10.7 %copy-start = (bf16[64,2048]{1,0:T(8,128)(2,1)S(1)}, bf16[64,2048]{1,0:T(8,128)(2,1)}, u32[]{:S(2)}) copy-start(bf16[64,2048]{1,0:T(8,128)(2,1)} %param.7) | copy-start | bytes 786436
  0.7 12.7 %copy-start.3 = (f32[8192]{0:T(1024)S(1)}, f32[8192]{0:T(1024)}, u32[]{:S(2)}) copy-start(f32[8192]{0:T(1024)} %param.8) | copy-start | bytes 98308
  2.3 18.1 %all-to-all-start = ((bf16[16,64,256]{2,1,0:T(8,128)(2,1)}), bf16[16,64,256]{2,1,0:T(8,128)(2,1)S(1)}, u32[]{:S(2)}, u32[]{:S(2)}) async-start(bf16[16,64,256]{2,1,0:T(8,128)(2,1)} %shard_map.85), calls=%async_computation | async-start | bytes 1048576 | tf_op jit(solution)/shard_map/all_to_all | solution.py:31
  10.2 4.0 %collective-permute-start = (bf16[1,2048]{1,0:T(2,128)(2,1)S(1)}, bf16[1,2048]{1,0:T(2,128)(2,1)S(1)}, u32[]{:S(2)}, u32[]{:S(2)}) collective-permute-start(bf16[1,2048]{1,0:T(2,128)(2,1)S(1)} %broadcast_in_dim.39), channel_id=1, source_target_pairs={{0,1},{1,0},{2,3},{3,2},{4,5},{5,4},{6,7},{7,6},{8,9},{9,8},{10,11... | collective-permute-start | bytes 12296 | tf_op jit(solution)/shard_map/ppermute | solution.py:27
  11.2 3.6 %collective-permute-start.2 = (bf16[2,2048]{1,0:T(2,128)(2,1)S(1)}, bf16[2,2048]{1,0:T(2,128)(2,1)S(1)}, u32[]{:S(2)}, u32[]{:S(2)}) collective-permute-start(bf16[2,2048]{1,0:T(2,128)(2,1)S(1)} %copy-done.5), channel_id=1, source_target_pairs={{0,1},{1,0},{2,3},{3,2},{4,5},{5,4},{6,7},{7,6},{8,9},{9,8},{10,11... | collective-permute-start | bytes 24584 | tf_op jit(solution)/shard_map/ppermute | solution.py:27
  11.3 3.5 %collective-permute-start.1 = (bf16[64,2048]{1,0:T(8,128)(2,1)S(1)}, bf16[64,2048]{1,0:T(8,128)(2,1)S(1)}, u32[]{:S(2)}, u32[]{:S(2)}) collective-permute-start(bf16[64,2048]{1,0:T(8,128)(2,1)S(1)} %copy-done), channel_id=1, source_target_pairs={{0,1},{1,0},{2,3},{3,2},{4,5},{5,4},{6,7},{7,6},{8,9},{9,8},{10,11... | collective-permute-start | bytes 786440 | tf_op jit(solution)/shard_map/ppermute | solution.py:27
  51.2 5.1 %collective-permute-start.3 = (f32[8,32,128]{2,1,0:T(8,128)S(1)}, f32[8,32,128]{2,1,0:T(8,128)S(1)}, u32[]{:S(2)}, u32[]{:S(2)}) collective-permute-start(f32[8,32,128]{2,1,0:T(8,128)S(1)} %all_to_all.31.c_ref), channel_id=1, source_target_pairs={{0,1},{1,0},{2,3},{3,2},{4,5},{5,4},{6,7},{7,6},{8,9},{9,8},{10,11... | collective-permute-start | bytes 393224 | tf_op jit(solution)/shard_map/ppermute | solution.py:27
  81.2 3.5 %collective-permute-start.4 = (f32[8,32,128]{2,1,0:T(8,128)S(1)}, f32[8,32,128]{2,1,0:T(8,128)S(1)}, u32[]{:S(2)}, u32[]{:S(2)}) collective-permute-start(f32[8,32,128]{2,1,0:T(8,128)S(1)} %all_to_all.33.c_ref), channel_id=1, source_target_pairs={{0,1},{1,0},{2,3},{3,2},{4,5},{5,4},{6,7},{7,6},{8,9},{9,8},{10,11... | collective-permute-start | bytes 393224 | tf_op jit(solution)/shard_map/ppermute | solution.py:27
  84.7 2.9 %copy-start.1 = (bf16[64,256]{1,0:T(8,128)(2,1)S(1)}, bf16[64,256]{1,0:T(8,128)(2,1)}, u32[]{:S(2)}) copy-start(bf16[64,256]{1,0:T(8,128)(2,1)} %in_ref.1) | copy-start | bytes 98308
  87.7 10.5 %all-to-all-start.5 = ((f32[16,8,128]{2,1,0:T(8,128)}), f32[16,8,128]{2,1,0:T(8,128)S(1)}, u32[]{:S(2)}, u32[]{:S(2)}) async-start(f32[16,8,128]{2,1,0:T(8,128)} %get-tuple-element.58), calls=%async_computation.5 | async-start | bytes 131072 | tf_op jit(solution)/shard_map/all_to_all | solution.py:31

commit v5 on v4

--- a/solution.py
+++ b/solution.py
@@ -180,7 +180,7 @@
     return jnp.concatenate([block, jnp.zeros_like(block)], axis=0).T
 
 
-def target_side_kernel(pack_ref, yt0_ref, minus_half_ref, hot_ref):
+def target_side_kernel(pack_ref, yt0_ref, first_ref, hot_ref, minus_half_ref):
     fill_hot(hot_ref)
     for q in range(yt0_ref.shape[0]):
         block = pack_ref[:LAT, q * BLK : (q + 1) * BLK]
@@ -188,6 +188,7 @@
         minus_half_ref[q : q + 1, :] = -0.5 * jnp.sum(
             jnp.square(block.astype(jnp.float32)), axis=0, keepdims=True
         )
+    fill_biased(yt0_ref, minus_half_ref[...], first_ref)
 
 
 def spread_kernel(in_ref, out_ref):
@@ -201,12 +202,11 @@
 
 
 def first_row_kernel(
-    log_ref, tiles_ref, b_ref, hot_ref, x_ref, yt0_ref, out_ref, xt0_ref, list_ref, side_ref, sems, yt_ref, m_ref, s_ref
+    log_ref, tiles_ref, hot_ref, x_ref, yt_ref, out_ref, xt0_ref, list_ref, side_ref, sems, full_ref, m_ref, s_ref
 ):
     copy = start_copy(tiles_ref, list_ref, sems.at[0])
     mass = start_copy(log_ref, side_ref.at[0], sems.at[1])
     clear(m_ref, s_ref)
-    fill_biased(yt0_ref, b_ref[...], yt_ref)
     for q in range(xt0_ref.shape[0]):
         xt0_ref[q] = transposed(x_ref[q // 2, :, (q % 2) * BLK : (q % 2 + 1) * BLK])
     copy.wait()
@@ -274,18 +274,23 @@
 
 
 def col_kernel(
-    log_ref, b_ref, tiles_ref, hot_ref, tail_ref, xt0_ref, pack_ref, r_ref, out_ref, tail_out_ref, a_ref, list_ref, side_ref, sems, xt_ref, s_ref
+    log_ref, b_ref, half_ref, tiles_ref, hot_ref, tail_ref, xt0_ref, pack_ref, r_ref, out_ref, tail_out_ref, source_ref, list_ref, side_ref, sems, xt_ref, s_ref
 ):
     copy = start_copy(tiles_ref, list_ref, sems.at[0])
     mass = start_copy(log_ref, side_ref.at[0], sems.at[1])
     in_b = start_copy(b_ref, side_ref.at[2], sems.at[3])
+    mine = half_ref.shape[0]
+    half = start_copy(half_ref, side_ref.at[3, pl.ds(0, mine)], sems.at[4])
     a = bias_of(join(r_ref[...]))
     side_ref[1] = a
-    out_a = start_copy(side_ref.at[1], a_ref, sems.at[2])
     s_ref[...] = jnp.zeros_like(s_ref)
     fill_biased(xt0_ref, a, xt_ref)
     fill_tails(a, tail_out_ref)
     copy.wait()
+    half.wait()
+    own = side_ref[1, pl.ds(lax.axis_index("col") // 2 * mine, mine), :]
+    side_ref[3, 8 : 8 + mine, :] = (own + side_ref[3, :mine, :]) * (1.0 / 32)
+    potential = start_copy(side_ref.at[3, pl.ds(8, mine)], source_ref, sems.at[2])
 
     def body(entries):
         accs = source_by_target(entries, pack_ref, xt_ref, hot_ref, lambda q: tail_ref[q])
@@ -296,19 +301,23 @@
     mass.wait()
     in_b.wait()
     put_level(finish_plain(s_ref, side_ref[2]), side_ref[0], out_ref)
-    out_a.wait()
+    potential.wait()
 
 
 def project_kernel(
-    tiles_ref, hot_ref, tail_ref, x_ref, yt0_ref, pack_ref, c_ref, d_ref, out_ref, b_ref, list_ref, side_ref, sems, yt_ref, w_ref
+    half_ref, tiles_ref, hot_ref, tail_ref, x_ref, yt0_ref, pack_ref, c_ref, d_ref, out_ref, target_ref, list_ref, side_ref, sems, yt_ref, w_ref
 ):
     copy = start_copy(tiles_ref, list_ref, sems.at[0])
+    half = start_copy(half_ref, side_ref.at[2], sems.at[1])
     b = bias_of(join_pair(c_ref[...], d_ref[...]))
-    side_ref[1] = b
-    out_b = start_copy(side_ref.at[1], b_ref, sems.at[2])
     w_ref[...] = jnp.zeros_like(w_ref)
     fill_biased(yt0_ref, b, yt_ref)
     copy.wait()
+    half.wait()
+    side_ref[1] = (b - side_ref[2]) * (1.0 / 32)
+    own_k = target_ref.shape[0]
+    first = pl.multiple_of(lax.axis_index("col") % 2 * own_k, own_k)
+    potential = start_copy(side_ref.at[1, pl.ds(first, own_k)], target_ref, sems.at[2])
 
     def body(entries):
         weighted = []
@@ -330,7 +339,7 @@
         for place, row in enumerate((2, 0, 1)):
             first = 2 * place + ib % 2
             out_ref[ib // 2, first : first + 1, :] = w[row : row + 1]
-    out_b.wait()
+    potential.wait()
 
 
 VMEM = pl.BlockSpec(memory_space=pltpu.VMEM)
@@ -394,8 +403,10 @@
     spread, support = lax.optimization_barrier((spread, support))
     x = exchange(spread, "col", by_chip)
     tiles, early = tile_list(support, chip, core, k, 12 * mine * chips)
-    early, target_latent, target_coords, log_target_mass = lax.optimization_barrier(
-        (early, target_latent, target_coords, log_target_mass)
+    early, target_latent, target_coords, log_target_mass, source_latent = (
+        lax.optimization_barrier(
+            (early, target_latent, target_coords, log_target_mass, source_latent)
+        )
     )
 
     def pair(a):
@@ -413,8 +424,8 @@
     )
     common = [
         pltpu.SMEM(tiles.shape, jnp.int32),
-        pltpu.VMEM((3, n, BLK), f32),
-        pltpu.SemaphoreType.DMA((4,)),
+        pltpu.VMEM((4, n, BLK), f32),
+        pltpu.SemaphoreType.DMA((5,)),
         pltpu.VMEM((n, BLK, BLK), bf16),
     ]
     sums = pltpu.VMEM((n + 1, 8, BLK), f32)
@@ -423,15 +434,22 @@
 
     target_log = target_log.astype(f32).reshape(k, BLK)
     source_log = of_core(log_source_mass.reshape(-1, BLK))
-    tiles, source_log, target_log = lax.optimization_barrier((tiles, source_log, target_log))
+    x_half = 0.5 * jnp.sum(jnp.square(source_latent.astype(f32)), axis=0).reshape(mine, BLK)
+    tiles, source_log, target_log, x_half = lax.optimization_barrier(
+        (tiles, source_log, target_log, x_half)
+    )
 
     turned = pltpu.VMEM((n, BLK, BLK), bf16)
     hot_shape = pltpu.VMEM((GROUP, 3 * GROUP, BLK), bf16)
-    yt0, minus_half, hot = call(
-        target_side_kernel, [turned, pltpu.VMEM((k, BLK), f32), hot_shape], [], [], [pack]
+    small = pltpu.HBM((n, BLK), f32)
+    yt0, yt_first, hot, minus_half = call(
+        target_side_kernel,
+        [turned, turned, hot_shape, pltpu.VMEM((k, BLK), f32)],
+        [],
+        [],
+        [pack],
     )
     tail_shape = pltpu.VMEM((n, GROUP, BLK), bf16)
-    small = pltpu.HBM((n, BLK), f32)
     to_chips = jax.ShapeDtypeStruct((chips, n, BLK), f32)
     to_rows = jax.ShapeDtypeStruct((rows, k, BLK), f32)
     to_owners = jax.ShapeDtypeStruct((chips, 8, BLK), f32)
@@ -442,7 +460,7 @@
         [to_chips, turned],
         first_scratch,
         by_sources,
-        [tiles, minus_half, hot, x, yt0],
+        [tiles, hot, x, yt_first],
     )
     r = exchange(r, "col", by_chip)
     c, tail, a = call(
@@ -464,34 +482,28 @@
         1,
     )
     r = exchange(r, "col", by_chip)
-    c, tail, a = call(
+    c, tail, out_source = call(
         col_kernel,
-        [to_rows, tail_shape, small],
+        [to_rows, tail_shape, pltpu.HBM((mine, BLK), f32)],
         scratch,
-        by_targets + [b],
+        by_targets + [b, x_half],
         [tiles, hot, tail, xt0, pack, r],
         1,
     )
     c = exchange(c, "row")
     d = swap_cores(c, cols)
-    part, b = call(
+    part, out_target = call(
         project_kernel,
-        [to_owners, small],
+        [to_owners, pltpu.HBM((own_k, BLK), f32)],
         scratch,
-        [],
+        [minus_half],
         [tiles, hot, tail, x, yt0, pack, c, d],
         1,
     )
-    part, a, b, source_latent = lax.optimization_barrier((part, a, b, source_latent))
     part = jnp.sum(exchange(part, "col", by_chip), axis=0)
     mapped = part[mine : 3 * mine].reshape(2, mine, BLK) / part[:mine]
     mapped = mapped.reshape(2, mine * BLK)
-
-    own_a = lax.dynamic_slice_in_dim(a, chip * mine, mine).reshape(-1)
-    x_half = 0.5 * jnp.sum(jnp.square(source_latent.astype(f32)), axis=0)
-    out_source = (own_a + x_half) / 32.0
-    out_target = lax.dynamic_slice_in_dim((b - minus_half) / 32.0, core * own_k, own_k).reshape(-1)
-    return out_source, out_target, mapped
+    return out_source.reshape(-1), out_target.reshape(-1), mapped
 
 
 def solution(mesh):

time: 101 us -> 100 us (0.990); the launches traced: 98.9 us -> 99.4 us
  blocking collectives: 48.4 us -> 60 us
  waiting for transfers between devices: 10.9 us -> 5.52 us
  starting transfers between devices: 19.8 us -> 15.7 us
  other arithmetic: 5.94 us -> 3.94 us
    all_to_all x4 -> x5, blocking collectives: 48.4 us -> 60 us  [exchange(): return lax.all_to_all(x, axis, 0, 0, axis_index_groups=groups)]
    all_to_all x2 -> x1, waiting for transfers between devices: 8.94 us -> 3.54 us  [exchange(): return lax.all_to_all(x, axis, 0, 0, axis_index_groups=groups)]
    all_to_all x2 -> x1, starting transfers between devices: 11.6 us -> 7.58 us  [exchange(): return lax.all_to_all(x, axis, 0, 0, axis_index_groups=groups)]
    reshape x1 -> x0, other arithmetic: 1.3 us -> none  [on_device(): lax.dynamic_slice_in_dim((b - minus_half) / 32.0, core * own_k, own_k)]
    div x1 -> x0, other arithmetic: 1.25 us -> none  [on_device(): out_source = (own_a + x_half) / 32.0]
  transfers between devices with their start and end apart: 7 -> 6, of which waited for: 4 -> 3; matrix products, arithmetic and copies ran while one was open for 6% -> 4% of each run, Pallas kernels for 0% -> 1%
where the time goes in v5:
time: 100 us; the launch traced here: 99.4 us
  blocking collectives  60 us (60%)
  starting transfers between devices  15.7 us (16%)
  Pallas kernels  12 us (12%)
  waiting for transfers between devices  5.52 us (6%)
  other arithmetic  3.94 us (4%)
  local copies, waits for them, and re-layouts  1.06 us (1%)
    all_to_all x5, blocking collectives, exchange(): return lax.all_to_all(x, axis, 0, 0, axis_index_groups=groups)  60 us
    pallas_call x6, Pallas kernels, call(): pl.pallas_call(kernel, out_shape=outs, in_specs=[HBM] * len(far) + [VMEM]...  10.4 us
    ppermute x5, starting transfers between devices, swap_cores(): return lax.ppermute(x, 'col', [(i, i ^ 1) for i in range(cols)])  8.09 us
    all_to_all x1, starting transfers between devices, exchange(): return lax.all_to_all(x, axis, 0, 0, axis_index_groups=groups)  7.58 us
    all_to_all x1, waiting for transfers between devices, exchange(): return lax.all_to_all(x, axis, 0, 0, axis_index_groups=groups)  3.54 us
  transfers between devices with their start and end apart: 6, of which 3 were waited for; matrix products, arithmetic and copies ran while one was open for 4% of the time, Pallas kernels for 1%

profile of v5, /device:TPU:1, one launch (start us, length us, event | category | flops | bytes accessed | tf_op | source)
XLA Modules:
  0.0 99.4 jit_solution(1130497384844652499)
XLA Ops:
  0.6 0.0 copy-start.2
  0.6 0.0 copy-start.3
  0.7 0.0 copy-start.6
  0.7 0.0 copy-start.5
  0.7 0.0 copy-start.1
  0.7 0.0 copy-start.4
  0.7 1.6 %shard_map.85 = bf16[16,64,256]{2,1,0:T(8,128)(2,1)} custom-call(bf16[64,256]{1,0:T(8,128)(2,1)} %in_ref.1), custom_call_target="tpu_custom_call" | custom-call | tf_op jit(solution)/shard_map/pallas_call | solution.py:397
  2.3 7.6 %all-to-all-start = ((bf16[16,64,256]{2,1,0:T(8,128)(2,1)}), bf16[16,64,256]{2,1,0:T(8,128)(2,1)S(1)}, u32[]{:S(2)}, u32[]{:S(2)}) async-start(bf16[16,64,256]{2,1,0:T(8,128)(2,1)} %shard_map.85), calls=%async_computation | async-start | bytes 1048576 | tf_op jit(solution)/shard_map/all_to_all | solution.py:31
  10.0 0.0 copy-done.3
  10.0 0.2 fusion.4
  10.2 0.0 copy-done.5
  10.2 1.0 %collective-permute-start = (bf16[1,2048]{1,0:T(2,128)(2,1)S(1)}, bf16[1,2048]{1,0:T(2,128)(2,1)S(1)}, u32[]{:S(2)}, u32[]{:S(2)}) collective-permute-start(bf16[1,2048]{1,0:T(2,128)(2,1)S(1)} %broadcast_in_dim.39), channel_id=1, source_target_pairs={{0,1},{1,0},{2,3},{3,2},{4,5},{5,4},{6,7},{7,6},{8,9},{9,8},{10,11... | collective-permute-start | bytes 12296 | tf_op jit(solution)/shard_map/ppermute | solution.py:27
  11.2 0.0 copy-done.6
  11.2 0.1 collective-permute-start.2
  11.3 0.0 copy-done.1
  11.3 0.4 collective-permute-start.1
  11.8 0.1 convolution_bitcast_fusion
  11.9 0.0 copy-done.2
  12.0 0.1 copy.17
  12.1 0.1 copy.16
  12.2 0.1 copy.15
  12.3 0.0 copy-done.4
  12.3 0.6 slice_select_fusion
  12.9 1.2 %select_reduce_fusion.tiles_ref = s32[4,128]{1,0:T(4,128)S(1)} fusion(s32[64,32]{1,0:T(8,128)S(1)} %copy.16, s32[4,128]{1,0:T(4,128)S(1)} %multiply_add_fusion, s32[64,32]{1,0:T(8,128)S(1)} %copy.15, pred[64,32]{1,0:T(8,128)(4,1)S(1)} %copy.17, pred[4,128]{1,0:T(4,128)(4,1)S(1)} %broadcast_compare_fusion.1), kind=kLoop, calls=%fused_computation | loop fusion | flops 5242368 | bytes 23040 | tf_op jit(solution)/shard_map/reduce_sum | solution.py:376
  14.0 0.6 multiply_bitcast_fusion.half_ref
  14.6 0.1 pad.4.clone
  14.7 0.1 pad.5.clone
  14.8 0.0 collective-permute-done
  14.8 0.6 maximum_convert_fusion
  15.4 0.0 collective-permute-done.2
  15.4 0.0 collective-permute-done.1
  15.5 0.2 maximum_maximum_fusion.pack_ref
  15.7 0.6 shard_map.86
  16.3 0.0 copy-start
  16.3 0.6 copy-done
  16.9 3.5 %all-to-all-done.x_ref = bf16[16,64,256]{2,1,0:T(8,128)(2,1)S(1)} async-done(((bf16[16,64,256]{2,1,0:T(8,128)(2,1)}), bf16[16,64,256]{2,1,0:T(8,128)(2,1)S(1)}, u32[]{:S(2)}, u32[]{:S(2)}) %all-to-all-start) | async-done | bytes 524320 | tf_op jit(solution)/shard_map/all_to_all | solution.py:31
  20.4 2.0 %shard_map.87 = (f32[16,32,128]{2,1,0:T(8,128)S(1)}, bf16[32,128,128]{2,1,0:T(8,128)(2,1)S(1)}) custom-call(f32[32,128]{1,0:T(8,128)} %bitcast.14, s32[4,128]{1,0:T(4,128)S(1)} %select_reduce_fusion.tiles_ref, bf16[16,48,128]{2,1,0:T(8,128)(2,1)S(1)} %get-tuple-element.38.hot_ref, bf16[16,64,256]{2,1,0:T(8,128)(2,1)S(1)} %all-to-all-done.x_ref, ...), custom_call_target="tpu_custom_call" | custom-call | tf_op jit(solution)/shard_map/pallas_call | solution.py:351
  22.5 11.2 %all_to_all.30.r_ref = f32[16,32,128]{2,1,0:T(8,128)S(1)} all-to-all(f32[16,32,128]{2,1,0:T(8,128)S(1)} %get-tuple-element.42), channel_id=1, replica_groups={{0,2,4,6,8,10,12,14,16,18,20,22,24,26,28,30},{1,3,5,7,9,11,13,15,17,19,..., dimensions={0} | all-to-all | bytes 524288 | tf_op jit(solution)/shard_map/all_to_all | solution.py:31
  33.7 2.0 %shard_map.88 = (f32[8,32,128]{2,1,0:T(8,128)S(1)}, bf16[32,16,128]{2,1,0:T(8,128)(2,1)S(1)}, f32[32,128]{1,0:T(8,128)}) custom-call(f32[32,128]{1,0:T(8,128)} %bitcast.16, s32[4,128]{1,0:T(4,128)S(1)} %select_reduce_fusion.tiles_ref, bf16[16,48,128]{2,1,0:T(8,128)(2,1)S(1)} %get-tuple-element.38.hot_ref, ...), custom_call_target="tpu_custom_call" | custom-call | tf_op jit(solution)/shard_map/pallas_call | solution.py:351
  35.7 16.0 %all_to_all.31.c_ref = f32[8,32,128]{2,1,0:T(8,128)S(1)} all-to-all(f32[8,32,128]{2,1,0:T(8,128)S(1)} %get-tuple-element.46), channel_id=1, replica_groups=mesh['row'=8,'col'=32] {'row'}, dimensions={0} | all-to-all | bytes 262144 | tf_op jit(solution)/shard_map/all_to_all | solution.py:31
  51.7 4.1 %collective-permute-start.3 = (f32[8,32,128]{2,1,0:T(8,128)S(1)}, f32[8,32,128]{2,1,0:T(8,128)S(1)}, u32[]{:S(2)}, u32[]{:S(2)}) collective-permute-start(f32[8,32,128]{2,1,0:T(8,128)S(1)} %all_to_all.31.c_ref), channel_id=1, source_target_pairs={{0,1},{1,0},{2,3},{3,2},{4,5},{5,4},{6,7},{7,6},{8,9},{9,8},{10,11... | collective-permute-start | bytes 393224 | tf_op jit(solution)/shard_map/ppermute | solution.py:27
  55.8 1.0 collective-permute-done.3.d_ref
  56.8 1.6 %shard_map.89 = (f32[16,32,128]{2,1,0:T(8,128)S(1)}, bf16[32,16,128]{2,1,0:T(8,128)(2,1)S(1)}, f32[32,128]{1,0:T(8,128)}) custom-call(f32[32,128]{1,0:T(8,128)} %bitcast.15, f32[32,128]{1,0:T(8,128)} %get-tuple-element.43.a_ref, s32[4,128]{1,0:T(4,128)S(1)} %select_reduce_fusion.tiles_ref, bf16[16,48,128]{2,1,0:T(8,128)(2,1)S(1)} %get-tuple-element.38.hot_ref, ...), custom_call_target="tpu_custom_call" | custom-call | tf_op jit(solution)/shard_map/pallas_call | solution.py:351
  58.5 12.2 %all_to_all.32.r_ref = f32[16,32,128]{2,1,0:T(8,128)S(1)} all-to-all(f32[16,32,128]{2,1,0:T(8,128)S(1)} %get-tuple-element.50), channel_id=1, replica_groups={{0,2,4,6,8,10,12,14,16,18,20,22,24,26,28,30},{1,3,5,7,9,11,13,15,17,19,..., dimensions={0} | all-to-all | bytes 524288 | tf_op jit(solution)/shard_map/all_to_all | solution.py:31
  70.7 1.7 %shard_map.90 = (f32[8,32,128]{2,1,0:T(8,128)S(1)}, bf16[32,16,128]{2,1,0:T(8,128)(2,1)S(1)}, f32[2,128]{1,0:T(2,128)}) custom-call(f32[32,128]{1,0:T(8,128)} %bitcast.17, f32[32,128]{1,0:T(8,128)} %get-tuple-element.47.b_ref, f32[2,128]{1,0:T(2,128)} %multiply_bitcast_fusion.half_ref, s32[4,128]{1,0:T(4,128)S(1)} %select_reduce_fusion.tiles_ref, ...), custom_call_target="tpu_custom_call" | custom-call | tf_op jit(solution)/shard_map/pallas_call | solution.py:351
  72.4 10.1 %all_to_all.33.c_ref = f32[8,32,128]{2,1,0:T(8,128)S(1)} all-to-all(f32[8,32,128]{2,1,0:T(8,128)S(1)} %get-tuple-element.54), channel_id=1, replica_groups=mesh['row'=8,'col'=32] {'row'}, dimensions={0} | all-to-all | bytes 262144 | tf_op jit(solution)/shard_map/all_to_all | solution.py:31
  82.5 2.4 %collective-permute-start.4 = (f32[8,32,128]{2,1,0:T(8,128)S(1)}, f32[8,32,128]{2,1,0:T(8,128)S(1)}, u32[]{:S(2)}, u32[]{:S(2)}) collective-permute-start(f32[8,32,128]{2,1,0:T(8,128)S(1)} %all_to_all.33.c_ref), channel_id=1, source_target_pairs={{0,1},{1,0},{2,3},{3,2},{4,5},{5,4},{6,7},{7,6},{8,9},{9,8},{10,11... | collective-permute-start | bytes 393224 | tf_op jit(solution)/shard_map/ppermute | solution.py:27
  85.0 1.0 collective-permute-done.4.d_ref
  85.9 2.4 %shard_map.91 = (f32[16,8,128]{2,1,0:T(8,128)S(1)}, f32[16,128]{1,0:T(8,128)}) custom-call(f32[32,128]{1,0:T(8,128)} %copy-done, s32[4,128]{1,0:T(4,128)S(1)} %select_reduce_fusion.tiles_ref, bf16[16,48,128]{2,1,0:T(8,128)(2,1)S(1)} %get-tuple-element.38.hot_ref, bf16[32,16,128]{2,1,0:T(8,128)(2,1)S(1)} %get-tuple-element.53.tail_ref, ...), custom_call_target="tpu_custom_call" | custom-call | tf_op jit(solution)/shard_map/pallas_call | solution.py:351
  88.4 10.4 %all_to_all.34 = f32[16,8,128]{2,1,0:T(8,128)S(1)} all-to-all(f32[16,8,128]{2,1,0:T(8,128)S(1)} %get-tuple-element.56), channel_id=1, replica_groups={{0,2,4,6,8,10,12,14,16,18,20,22,24,26,28,30},{1,3,5,7,9,11,13,15,17,19,..., dimensions={0} | all-to-all | bytes 131072 | tf_op jit(solution)/shard_map/all_to_all | solution.py:31
  98.8 0.6 broadcast_divide_fusion
  (16 shorter events, 0.2 us)
Async XLA Ops:
  0.6 11.3 %copy-start.2 = (bf16[64,256]{1,0:T(8,128)(2,1)S(1)}, bf16[64,256]{1,0:T(8,128)(2,1)}, u32[]{:S(2)}) copy-start(bf16[64,256]{1,0:T(8,128)(2,1)} %in_ref.1) | copy-start | bytes 98308
  0.6 9.3 %copy-start.3 = (s32[64,32]{0,1:T(8,128)S(1)}, s32[64,32]{0,1:T(8,128)}, u32[]{:S(2)}) copy-start(s32[64,32]{0,1:T(8,128)} %param.11) | copy-start | bytes 24580
  0.7 10.6 %copy-start.6 = (bf16[2,2048]{1,0:T(2,128)(2,1)S(1)}, bf16[2,2048]{1,0:T(2,128)(2,1)}, u32[]{:S(2)}) copy-start(bf16[2,2048]{1,0:T(2,128)(2,1)} %param.10) | copy-start | bytes 24580
  0.7 9.5 %copy-start.5 = (bf16[2048]{0:T(1024)(128)(2,1)S(1)}, bf16[2048]{0:T(1024)(128)(2,1)}, u32[]{:S(2)}) copy-start(bf16[2048]{0:T(1024)(128)(2,1)} %param.9) | copy-start | bytes 12292
  0.7 10.7 %copy-start.1 = (bf16[64,2048]{1,0:T(8,128)(2,1)S(1)}, bf16[64,2048]{1,0:T(8,128)(2,1)}, u32[]{:S(2)}) copy-start(bf16[64,2048]{1,0:T(8,128)(2,1)} %param.7) | copy-start | bytes 786436
  0.7 11.6 %copy-start.4 = (f32[8192]{0:T(1024)S(1)}, f32[8192]{0:T(1024)}, u32[]{:S(2)}) copy-start(f32[8192]{0:T(1024)} %param.8) | copy-start | bytes 98308
  2.3 18.1 %all-to-all-start = ((bf16[16,64,256]{2,1,0:T(8,128)(2,1)}), bf16[16,64,256]{2,1,0:T(8,128)(2,1)S(1)}, u32[]{:S(2)}, u32[]{:S(2)}) async-start(bf16[16,64,256]{2,1,0:T(8,128)(2,1)} %shard_map.85), calls=%async_computation | async-start | bytes 1048576 | tf_op jit(solution)/shard_map/all_to_all | solution.py:31
  10.2 4.6 %collective-permute-start = (bf16[1,2048]{1,0:T(2,128)(2,1)S(1)}, bf16[1,2048]{1,0:T(2,128)(2,1)S(1)}, u32[]{:S(2)}, u32[]{:S(2)}) collective-permute-start(bf16[1,2048]{1,0:T(2,128)(2,1)S(1)} %broadcast_in_dim.39), channel_id=1, source_target_pairs={{0,1},{1,0},{2,3},{3,2},{4,5},{5,4},{6,7},{7,6},{8,9},{9,8},{10,11... | collective-permute-start | bytes 12296 | tf_op jit(solution)/shard_map/ppermute | solution.py:27
  11.2 4.2 %collective-permute-start.2 = (bf16[2,2048]{1,0:T(2,128)(2,1)S(1)}, bf16[2,2048]{1,0:T(2,128)(2,1)S(1)}, u32[]{:S(2)}, u32[]{:S(2)}) collective-permute-start(bf16[2,2048]{1,0:T(2,128)(2,1)S(1)} %copy-done.6), channel_id=1, source_target_pairs={{0,1},{1,0},{2,3},{3,2},{4,5},{5,4},{6,7},{7,6},{8,9},{9,8},{10,11... | collective-permute-start | bytes 24584 | tf_op jit(solution)/shard_map/ppermute | solution.py:27
  11.3 4.1 %collective-permute-start.1 = (bf16[64,2048]{1,0:T(8,128)(2,1)S(1)}, bf16[64,2048]{1,0:T(8,128)(2,1)S(1)}, u32[]{:S(2)}, u32[]{:S(2)}) collective-permute-start(bf16[64,2048]{1,0:T(8,128)(2,1)S(1)} %copy-done.1), channel_id=1, source_target_pairs={{0,1},{1,0},{2,3},{3,2},{4,5},{5,4},{6,7},{7,6},{8,9},{9,8},{10,11... | collective-permute-start | bytes 786440 | tf_op jit(solution)/shard_map/ppermute | solution.py:27
  16.3 0.6 copy-start
  51.7 5.1 %collective-permute-start.3 = (f32[8,32,128]{2,1,0:T(8,128)S(1)}, f32[8,32,128]{2,1,0:T(8,128)S(1)}, u32[]{:S(2)}, u32[]{:S(2)}) collective-permute-start(f32[8,32,128]{2,1,0:T(8,128)S(1)} %all_to_all.31.c_ref), channel_id=1, source_target_pairs={{0,1},{1,0},{2,3},{3,2},{4,5},{5,4},{6,7},{7,6},{8,9},{9,8},{10,11... | collective-permute-start | bytes 393224 | tf_op jit(solution)/shard_map/ppermute | solution.py:27
  82.5 3.4 %collective-permute-start.4 = (f32[8,32,128]{2,1,0:T(8,128)S(1)}, f32[8,32,128]{2,1,0:T(8,128)S(1)}, u32[]{:S(2)}, u32[]{:S(2)}) collective-permute-start(f32[8,32,128]{2,1,0:T(8,128)S(1)} %all_to_all.33.c_ref), channel_id=1, source_target_pairs={{0,1},{1,0},{2,3},{3,2},{4,5},{5,4},{6,7},{7,6},{8,9},{9,8},{10,11... | collective-permute-start | bytes 393224 | tf_op jit(solution)/shard_map/ppermute | solution.py:27
